TPU v7x, 32 devices: a whole 2x2x4 slice. The times are simulated.
32 devices in a mesh: fsdp: 32 (over z, y, x, core).
Axes of the slice: x: 2, y: 2, z: 4, core: 2. Of those that a mesh axis runs over, the one named last changes fastest.
Arguments:
- layer_input: bfloat16 [4096, 1536], P('fsdp'), may hold values from -6 to 6
- cotangent: bfloat16 [4096, 1536], P('fsdp'), may hold values from -6 to 6
- sequence_ids: int32 [4096], P('fsdp'), may hold values from 0 to 3, as said below
- expert_ids: int32 [4096, 8], P('fsdp'), may hold values from 0 to 39, all different within a row; in each aligned block of 128 rows (0 to 127, 128 to 255, ...) at most 32 rows name the same one
- attention_gain: bfloat16 [1536], P('fsdp'), may hold values from 0.5 to 1.5
- qkv_weight: bfloat16 [1536, 2560], P('fsdp'), may hold values from -2 to 2
- output_weight: bfloat16 [1536, 1536], P('fsdp'), may hold values from -3.59375 to 3.59375
- moe_gain: bfloat16 [1536], P('fsdp'), may hold values from 0.5 to 1.5
- router: bfloat16 [1536, 40], P('fsdp'), may hold values from -1 to 1
- gate_up: bfloat16 [1536, 40, 1024], P('fsdp'), may hold values from -0.15625 to 0.15625
- down_proj: bfloat16 [1536, 40, 512], P('fsdp'), may hold values from -24 to 24
Outputs:
- layer_output: bfloat16 [4096, 1536], P('fsdp')
- input_grad: bfloat16 [4096, 1536], P('fsdp')
- attention_gain_grad: float32 [1536], P('fsdp')
- qkv_weight_grad: float32 [1536, 2560], P('fsdp')
- output_weight_grad: float32 [1536, 1536], P('fsdp')
- moe_gain_grad: float32 [1536], P('fsdp')
- router_grad: float32 [1536, 40], P('fsdp')
- gate_up_grad: float32 [1536, 40, 1024], P('fsdp')
- down_grad: float32 [1536, 40, 512], P('fsdp')
Inputs may be any that keep to these rules, and one draw needn't show every extreme that they name: `sequence_ids`: along one device's 128 tokens the numbers never fall; a run of equal numbers is one sequence; some device holds a single sequence of 128 tokens. `expert_ids`: among the 128 rows of one device no expert is named by more than 32 rows.
All inputs are finite; a program needn't handle non-finite values.
Results may differ from a plain program's by a relative error of at most 0.014.
Values may be sent and summed in bfloat16 or wider, within the bound.
A program may use at most 448 MiB of HBM per device.

v0:
```python
import math

import jax
import jax.numpy as jnp
import numpy as np
from jax import lax
from jax.sharding import PartitionSpec as P

MODEL_WIDTH = 1536
QUERY_HEADS = 24
KEY_VALUE_HEADS = 8
HEAD_WIDTH = 64
E = 40
F = 512
TOP = 8
CAP = 32


EPSILON = 1e-06
ATTN_SCALE = 0.015625
RESIDUAL_SCALE = 0.22
ROPE_BASE = 10000.0
PRECISE_ARITHMETIC = lax.Precision.HIGHEST


def positions(sequence_ids):
    sequence_length = sequence_ids.shape[0]
    places = jnp.arange(sequence_length, dtype=jnp.int32)
    starts_new = jnp.concatenate([jnp.ones((1,), jnp.bool_), sequence_ids[1:] != sequence_ids[:-1]])
    begins = lax.cummax(jnp.where(starts_new, places, 0), axis=0)
    return places - begins


def rope_tables(places, head_size):
    half_size = head_size // 2
    exponents = jnp.arange(half_size, dtype=jnp.float32) * (2.0 / head_size)
    inverse = jnp.exp(exponents * -math.log(ROPE_BASE))
    angles = places.astype(jnp.float32)[:, None] * inverse[None, :]
    return (jnp.cos(angles), jnp.sin(angles))


def apply_rotary(tensor, cosine_lookup, sine_lookup):
    half_size = tensor.shape[-1] // 2
    first_half = tensor[..., :half_size]
    second_half = tensor[..., half_size:]
    cosine_rows = cosine_lookup[:, None, :]
    sine_rows = sine_lookup[:, None, :]
    return jnp.concatenate(
        [
            first_half * cosine_rows - second_half * sine_rows,
            second_half * cosine_rows + first_half * sine_rows,
        ],
        axis=-1,
    )


def rotate_back(tensor, cosine_lookup, sine_lookup):
    half_size = tensor.shape[-1] // 2
    first_half = tensor[..., :half_size]
    second_half = tensor[..., half_size:]
    cosine_rows = cosine_lookup[:, None, :]
    sine_rows = sine_lookup[:, None, :]
    return jnp.concatenate(
        [
            first_half * cosine_rows + second_half * sine_rows,
            second_half * cosine_rows - first_half * sine_rows,
        ],
        axis=-1,
    )


def norm_scale(hidden_state):
    return lax.rsqrt(jnp.mean(hidden_state * hidden_state, axis=-1, keepdims=True) + EPSILON)


def norm_back(hidden_state, gain_vector, scale_rows, upstream):
    weighted = upstream * gain_vector.astype(jnp.float32)
    inner_mean = jnp.mean(weighted * hidden_state, axis=-1, keepdims=True)
    grad_hidden = scale_rows * weighted - hidden_state * scale_rows**3 * inner_mean
    grad_gain = jnp.sum(upstream * hidden_state * scale_rows, axis=0)
    return (grad_hidden, grad_gain)


def expert_slots(expert_ids, experts, capacity):
    flat_ids = expert_ids.reshape(-1)
    onehot = (flat_ids[:, None] == jnp.arange(experts, dtype=jnp.int32)[None, :]).astype(jnp.int32)
    running = jnp.cumsum(onehot, axis=0, dtype=jnp.int32)
    ranks = jnp.sum((running - 1) * onehot, axis=-1, dtype=jnp.int32)
    return flat_ids * capacity + ranks


def owner_tables(devices):
    width_owned = E * F // devices
    span_count = (F + width_owned - 2) // F + 1
    first_expert = np.arange(devices) * width_owned // F
    send_table = np.minimum(first_expert[:, None] + np.arange(span_count)[None, :], E).reshape(-1)
    combine_table = (send_table[None, :] == np.arange(E)[:, None]).astype(np.float32)
    return (width_owned, span_count, send_table, combine_table)


def dispatch_rows(buffer_rows, send_table, devices, span_count):
    padded = jnp.concatenate(
        [buffer_rows, jnp.zeros((1, CAP, MODEL_WIDTH), buffer_rows.dtype)], axis=0
    )
    picked_rows = jnp.take(padded, jnp.asarray(send_table, dtype=jnp.int32), axis=0)
    return picked_rows.reshape(devices, span_count, CAP, MODEL_WIDTH)


def merge_entries(returned, combine_table):
    flat_rows = returned.reshape(returned.shape[0] * returned.shape[1], CAP * MODEL_WIDTH)
    summed = jnp.dot(
        jnp.asarray(combine_table),
        flat_rows,
        precision=PRECISE_ARITHMETIC,
        preferred_element_type=jnp.float32,
    )
    return summed.reshape(E, CAP, MODEL_WIDTH)


def on_device(
    layer_input,
    cotangent,
    sequence_ids,
    expert_ids,
    attention_gain,
    qkv_weight,
    output_weight,
    moe_gain,
    router,
    gate_up,
    down_proj,
):
    sequence_length = layer_input.shape[0]
    shard_rows = gate_up.shape[0]
    query_group_count = QUERY_HEADS // KEY_VALUE_HEADS
    query_feature_width = QUERY_HEADS * HEAD_WIDTH
    key_feature_width = KEY_VALUE_HEADS * HEAD_WIDTH
    rows_per_block = min(512, sequence_length)
    devices = lax.axis_size("fsdp")
    dense_set = (
        lax.all_gather(attention_gain, "fsdp", axis=0, tiled=True),
        lax.all_gather(qkv_weight, "fsdp", axis=0, tiled=True),
        lax.all_gather(output_weight, "fsdp", axis=0, tiled=True),
        lax.all_gather(moe_gain, "fsdp", axis=0, tiled=True),
        lax.all_gather(router, "fsdp", axis=0, tiled=True),
    )
    gain_one, qkv_full, out_full, gain_two, router_full = dense_set
    width_owned, span_count, send_table, combine_table = owner_tables(devices)
    gate_cols = jnp.transpose(gate_up.reshape(shard_rows, E, 2, F), (0, 2, 1, 3)).reshape(
        shard_rows, 2, E * F
    )
    down_cols = down_proj.reshape(shard_rows, 1, E * F)
    owned_weights = lax.all_to_all(
        jnp.concatenate([gate_cols, down_cols], axis=1),
        "fsdp",
        split_axis=2,
        concat_axis=0,
        tiled=True,
    )
    owned_gate_up = owned_weights[:, :2, :]
    owned_down = owned_weights[:, 2, :]
    owner_index = lax.axis_index("fsdp")
    owned_start = owner_index * width_owned
    owned_columns = owned_start + jnp.arange(width_owned, dtype=jnp.int32)
    slot_of = owned_columns // F - owned_start // F
    column_mask = (slot_of[None, :] == jnp.arange(span_count, dtype=jnp.int32)[:, None]).astype(
        jnp.float32
    )
    inputs = layer_input.astype(jnp.float32)
    scale_one = norm_scale(inputs)
    normed_one = (inputs * scale_one * gain_one.astype(jnp.float32)).astype(jnp.bfloat16)
    joined_projection = jnp.dot(normed_one, qkv_full, preferred_element_type=jnp.float32)
    places = positions(sequence_ids)
    cosine_lookup, sine_lookup = rope_tables(places, HEAD_WIDTH)
    query_rows = apply_rotary(
        joined_projection[:, :query_feature_width].reshape(
            sequence_length, QUERY_HEADS, HEAD_WIDTH
        ),
        cosine_lookup,
        sine_lookup,
    ).astype(jnp.bfloat16)
    query_rows = query_rows.reshape(sequence_length, KEY_VALUE_HEADS, query_group_count, HEAD_WIDTH)
    rotated_keys = apply_rotary(
        joined_projection[:, query_feature_width : query_feature_width + key_feature_width].reshape(
            sequence_length, KEY_VALUE_HEADS, HEAD_WIDTH
        ),
        cosine_lookup,
        sine_lookup,
    ).astype(jnp.bfloat16)
    value_inputs = (
        joined_projection[:, query_feature_width + key_feature_width :]
        .reshape(sequence_length, KEY_VALUE_HEADS, HEAD_WIDTH)
        .astype(jnp.bfloat16)
    )
    token_index = jnp.arange(sequence_length, dtype=jnp.int32)

    def block_scores(offset):
        scores = (
            jnp.einsum(
                "qkgd,tkd->kgqt", query_rows, rotated_keys, preferred_element_type=jnp.float32
            )
            * ATTN_SCALE
        )
        allowed = (
            sequence_ids[offset : offset + rows_per_block, None] == sequence_ids[None, :]
        ) & (token_index[None, :] <= token_index[offset : offset + rows_per_block, None])
        return jnp.where(allowed, scores, -jnp.inf)

    offset = 0
    scores = block_scores(offset)
    row_peak = jnp.max(scores, axis=-1, keepdims=True)
    log_total = row_peak + jnp.log(jnp.sum(jnp.exp(scores - row_peak), axis=-1, keepdims=True))
    probs_half = jnp.exp(scores - log_total).astype(jnp.bfloat16)
    mixed_heads = jnp.einsum(
        "kgqt,tkd->qkgd", probs_half, value_inputs, preferred_element_type=jnp.float32
    )
    attention_output_list = mixed_heads.reshape(rows_per_block, query_feature_width).astype(
        jnp.bfloat16
    )
    total_list = [log_total]
    branch = jnp.dot(attention_output_list, out_full, preferred_element_type=jnp.float32)
    middle = inputs + RESIDUAL_SCALE * branch
    scale_two = norm_scale(middle)
    normed_two = (middle * scale_two * gain_two.astype(jnp.float32)).astype(jnp.bfloat16)
    logits = jnp.dot(normed_two, router_full, preferred_element_type=jnp.float32)
    gate_probs = jax.nn.softmax(logits, axis=-1)
    picked = (expert_ids[:, :, None] == jnp.arange(E, dtype=jnp.int32)[None, None, :]).astype(
        jnp.float32
    )
    route_weight = jnp.einsum("tke,te->tk", picked, gate_probs, precision=PRECISE_ARITHMETIC)
    slot_rows = expert_slots(expert_ids, E, CAP)
    received_storage = (
        jnp.zeros((E * CAP, MODEL_WIDTH), jnp.bfloat16)
        .at[slot_rows]
        .set(jnp.repeat(normed_two, TOP, axis=0))
        .reshape(E, CAP, MODEL_WIDTH)
    )
    send_in = dispatch_rows(received_storage, send_table, devices, span_count)
    pre_cols = jnp.einsum(
        "nrkd,dgw->nrkgw",
        lax.all_to_all(send_in, "fsdp", split_axis=0, concat_axis=0, tiled=True),
        owned_gate_up,
        preferred_element_type=jnp.float32,
    )
    pre_cols = pre_cols * column_mask[None, :, None, None, :]
    gate_cols_pre = pre_cols[..., 0, :]
    up_cols_pre = pre_cols[..., 1, :]
    acted = (gate_cols_pre * jax.nn.sigmoid(gate_cols_pre) * up_cols_pre).astype(jnp.bfloat16)
    partial_out = jnp.einsum("nrkw,dw->nrkd", acted, owned_down, preferred_element_type=jnp.float32)
    returned_out = lax.all_to_all(partial_out, "fsdp", split_axis=0, concat_axis=0, tiled=True)
    buffer_out = merge_entries(returned_out, combine_table)
    routed_out = buffer_out.reshape(E * CAP, MODEL_WIDTH)[slot_rows].reshape(
        sequence_length, TOP, MODEL_WIDTH
    )
    combined = jnp.einsum("tk,tkd->td", route_weight, routed_out, precision=PRECISE_ARITHMETIC)
    layer_output = (middle + RESIDUAL_SCALE * combined).astype(jnp.bfloat16)
    upstream = cotangent.astype(jnp.float32)
    grad_mix = RESIDUAL_SCALE * upstream
    grad_weight = jnp.einsum("td,tkd->tk", grad_mix, routed_out, precision=PRECISE_ARITHMETIC)
    grad_rows = (
        (route_weight[:, :, None] * grad_mix[:, None, :])
        .astype(jnp.bfloat16)
        .reshape(sequence_length * TOP, MODEL_WIDTH)
    )
    buffer_grad = (
        jnp.zeros((E * CAP, MODEL_WIDTH), jnp.bfloat16)
        .at[slot_rows]
        .set(grad_rows)
        .reshape(E, CAP, MODEL_WIDTH)
    )
    gain_one_back, qkv_back, out_back, gain_two_back, router_back = dense_set
    send_grad = dispatch_rows(buffer_grad, send_table, devices, span_count)
    rows_in = lax.all_to_all(send_in, "fsdp", split_axis=0, concat_axis=0, tiled=True)
    rows_grad = lax.all_to_all(send_grad, "fsdp", split_axis=0, concat_axis=0, tiled=True)
    pre_cols = jnp.einsum(
        "nrkd,dgw->nrkgw", rows_in, owned_gate_up, preferred_element_type=jnp.float32
    )
    pre_cols = pre_cols * column_mask[None, :, None, None, :]
    gate_cols_pre = pre_cols[..., 0, :]
    up_cols_pre = pre_cols[..., 1, :]
    sigmoid_cols = jax.nn.sigmoid(gate_cols_pre)
    silu_cols = gate_cols_pre * sigmoid_cols
    acted = (silu_cols * up_cols_pre).astype(jnp.bfloat16)
    grad_act_cols = jnp.einsum(
        "nrkd,dw->nrkw", rows_grad, owned_down, preferred_element_type=jnp.float32
    )
    grad_gate_cols = (
        grad_act_cols * up_cols_pre * sigmoid_cols * (1.0 + gate_cols_pre * (1.0 - sigmoid_cols))
    )
    grad_up_cols = grad_act_cols * silu_cols
    grad_pair = jnp.stack([grad_gate_cols, grad_up_cols], axis=3).astype(jnp.bfloat16)
    partial_back = jnp.einsum(
        "nrkgw,dgw->nrkd", grad_pair, owned_gate_up, preferred_element_type=jnp.float32
    )
    returned_back = lax.all_to_all(partial_back, "fsdp", split_axis=0, concat_axis=0, tiled=True)
    results = (returned_back, rows_in, rows_grad, grad_pair, acted)
    returned_back, rows_in_all, rows_grad_all, grad_pair_all, acted_all = results
    backward_buffer = merge_entries(returned_back, combine_table)
    owned_gate_up_grad = jnp.einsum(
        "nrkd,nrkgw->dgw", rows_in_all, grad_pair_all, preferred_element_type=jnp.float32
    )
    owned_down_grad = jnp.einsum(
        "nrkd,nrkw->dw", rows_grad_all, acted_all, preferred_element_type=jnp.float32
    )
    owned_grads = jnp.concatenate([owned_gate_up_grad, owned_down_grad[:, None, :]], axis=1)
    relaid = lax.all_to_all(owned_grads, "fsdp", split_axis=0, concat_axis=2, tiled=True)
    gate_up_grad = jnp.transpose(
        relaid[:, :2, :].reshape(shard_rows, 2, E, F), (0, 2, 1, 3)
    ).reshape(shard_rows, E, 2 * F)
    down_grad = relaid[:, 2, :].reshape(shard_rows, E, F)
    grad_normed = jnp.sum(
        backward_buffer.reshape(E * CAP, MODEL_WIDTH)[slot_rows].reshape(
            sequence_length, TOP, MODEL_WIDTH
        ),
        axis=1,
    )
    grad_gates = jnp.einsum("tk,tke->te", grad_weight, picked, precision=PRECISE_ARITHMETIC)
    grad_logits = gate_probs * (
        grad_gates - jnp.sum(gate_probs * grad_gates, axis=-1, keepdims=True)
    )
    grad_normed = grad_normed + jnp.einsum(
        "te,de->td", grad_logits, router_back.astype(jnp.float32), precision=PRECISE_ARITHMETIC
    )
    router_part = jnp.einsum(
        "td,te->de", normed_two.astype(jnp.float32), grad_logits, precision=PRECISE_ARITHMETIC
    )
    grad_middle, gain_two_part = norm_back(middle, gain_two_back, scale_two, grad_normed)
    grad_middle = grad_middle + upstream
    grad_branch = (RESIDUAL_SCALE * grad_middle).astype(jnp.bfloat16)
    out_part = jnp.einsum(
        "tq,td->qd", attention_output_list, grad_branch, preferred_element_type=jnp.float32
    )
    attention_output_gradient = jnp.einsum(
        "td,qd->tq", grad_branch, out_back, preferred_element_type=jnp.float32
    ).astype(jnp.bfloat16)
    value_gradient = jnp.zeros((sequence_length, KEY_VALUE_HEADS, HEAD_WIDTH), jnp.float32)
    key_gradient = jnp.zeros((sequence_length, KEY_VALUE_HEADS, HEAD_WIDTH), jnp.float32)
    query_grads = []
    for block_number, offset in enumerate(range(0, sequence_length, rows_per_block)):
        scores = block_scores(offset)
        attn_probs = jnp.exp(scores - total_list[block_number])
        block_gradient = attention_output_gradient.reshape(
            rows_per_block, KEY_VALUE_HEADS, query_group_count, HEAD_WIDTH
        )
        attention_output_block = attention_output_list.reshape(
            rows_per_block, KEY_VALUE_HEADS, query_group_count, HEAD_WIDTH
        )
        row_delta = jnp.sum(
            block_gradient.astype(jnp.float32) * attention_output_block.astype(jnp.float32), axis=-1
        )
        row_delta = jnp.transpose(row_delta, (1, 2, 0))[..., None]
        value_gradient = jnp.einsum(
            "kgqt,qkgd->tkd",
            attn_probs.astype(jnp.bfloat16),
            block_gradient,
            preferred_element_type=jnp.float32,
        )
        grad_probs = jnp.einsum(
            "qkgd,tkd->kgqt", block_gradient, value_inputs, preferred_element_type=jnp.float32
        )
        grad_scores = (attn_probs * (grad_probs - row_delta) * ATTN_SCALE).astype(jnp.bfloat16)
        query_grads.append(
            jnp.einsum(
                "kgqt,tkd->qkgd", grad_scores, rotated_keys, preferred_element_type=jnp.float32
            )
        )
        key_gradient = jnp.einsum(
            "kgqt,qkgd->tkd", grad_scores, query_rows, preferred_element_type=jnp.float32
        )
    grad_queries = query_grads[0].reshape(sequence_length, QUERY_HEADS, HEAD_WIDTH)
    grad_joined = jnp.concatenate(
        [
            rotate_back(grad_queries, cosine_lookup, sine_lookup).reshape(
                sequence_length, query_feature_width
            ),
            rotate_back(key_gradient, cosine_lookup, sine_lookup).reshape(
                sequence_length, key_feature_width
            ),
            value_gradient.reshape(sequence_length, key_feature_width),
        ],
        axis=-1,
    ).astype(jnp.bfloat16)
    qkv_part = jnp.einsum("td,tm->dm", normed_one, grad_joined, preferred_element_type=jnp.float32)
    grad_normed_one = jnp.einsum(
        "tm,dm->td", grad_joined, qkv_back, preferred_element_type=jnp.float32
    )
    grad_inputs, gain_one_part = norm_back(inputs, gain_one_back, scale_one, grad_normed_one)
    input_grad = (grad_inputs + grad_middle).astype(jnp.bfloat16)
    dense_grads = (
        lax.psum_scatter(gain_one_part, "fsdp", scatter_dimension=0, tiled=True),
        lax.psum_scatter(qkv_part, "fsdp", scatter_dimension=0, tiled=True),
        lax.psum_scatter(out_part, "fsdp", scatter_dimension=0, tiled=True),
        lax.psum_scatter(gain_two_part, "fsdp", scatter_dimension=0, tiled=True),
        lax.psum_scatter(router_part, "fsdp", scatter_dimension=0, tiled=True),
    )
    return (
        layer_output,
        input_grad,
        dense_grads[0],
        dense_grads[1],
        dense_grads[2],
        dense_grads[3],
        dense_grads[4],
        gate_up_grad,
        down_grad,
    )


def solution(mesh):
    placed = (
        P("fsdp", None),
        P("fsdp", None),
        P("fsdp"),
        P("fsdp", None),
        P("fsdp"),
        P("fsdp", None),
        P("fsdp", None),
        P("fsdp"),
        P("fsdp", None),
        P("fsdp", None, None),
        P("fsdp", None, None),
    )
    return jax.shard_map(
        on_device,
        mesh=mesh,
        in_specs=placed,
        out_specs=(
            P("fsdp", None),
            P("fsdp", None),
            P("fsdp"),
            P("fsdp", None),
            P("fsdp", None),
            P("fsdp"),
            P("fsdp", None),
            P("fsdp", None, None),
            P("fsdp", None, None),
        ),
        check_vma=False,
    )
```

profile of v0, /device:TPU:0, one launch (start us, length us, event | category | flops | bytes accessed | tf_op | source)
XLA Modules:
  0.0 2428.2 jit_solution(1918369729955381953)
XLA Ops:
  7.9 4.4 copy.233
  12.3 6.4 reshape.362
  18.6 2.8 reshape.363
  21.4 5.3 pad_maximum_fusion.2
  26.8 25.0 %copy.172 = bf16[48,3,20480]{0,1,2:T(4,128)(2,1)} copy(bf16[48,3,20480]{2,0,1:T(8,128)(2,1)} %pad_maximum_fusion.2) | data formatting | bytes 11796480 | tf_op jit(solution)/shard_map/concatenate | solution.py:154
  51.8 32.0 %reshape.460 = bf16[32,2,46080]{2,1,0:T(2,128)(2,1)} reshape(bf16[20480,3,48]{2,1,0:T(4,128)(2,1)} %bitcast.319) | data formatting | bytes 11796480
  83.8 7.2 all-to-all-start.1
  92.6 171.0 %all-reduce.7 = (bf16[1536]{0:T(1024)(128)(2,1)S(1)}, bf16[1536]{0:T(1024)(128)(2,1)S(1)}) all-reduce(bf16[1536]{0:T(1024)(128)(2,1)S(1)} %dynamic-update-slice, bf16[1536]{0:T(1024)(128)(2,1)S(1)} %dynamic-update-slice.1), channel_id=1, replica_groups=mesh['fsdp'=32] {'fsdp'}, use_global_device_ids=true, to_apply=%add.2 | all-reduce | flops 3072 | bytes 12288
  264.2 11.3 reduce-window.19
  277.2 4.5 fusion.86
  285.4 3.4 multiply_reduce_fusion.3
  289.9 8.0 scatter_custom_fusion
  297.8 4.5 concatenate.55
  302.4 9.7 gather_fusion.2
  312.0 4.5 all-to-all-start
  316.6 32.9 %reshape.461 = bf16[20480,3,48]{2,1,0:T(4,128)(2,1)} reshape(bf16[32,2,46080]{2,1,0:T(2,128)(2,1)} %all-to-all-done.1) | data formatting | bytes 11796480
  349.5 24.7 %copy.211 = bf16[48,3,32,640]{3,0,2,1:T(8,128)(2,1)} copy(bf16[48,3,32,640]{0,1,3,2:T(4,128)(2,1)} %bitcast.320) | data formatting | bytes 11796480 | tf_op jit(solution)/shard_map/all_to_all | solution.py:153
  374.2 151.6 %all-to-all-done = bf16[32,3,32,1536]{3,2,1,0:T(8,128)(2,1)} async-done(((bf16[32,3,32,1536]{3,2,1,0:T(8,128)(2,1)}), bf16[32,3,32,1536]{3,2,1,0:T(8,128)(2,1)}, u32[]{:S(2)}, u32[]{:S(2)}) %all-to-all-start) | async-done | bytes 9437216 | tf_op jit(solution)/shard_map/all_to_all | solution.py:241
  525.8 18.1 convolution_multiply_fusion
  543.9 15.3 fusion.31
  559.2 4.1 all-to-all-start.2
  563.3 385.3 %all-gather = bf16[32,48,40]{1,2,0:T(8,128)(2,1)S(1)} all-gather(bf16[1,48,40]{1,2,0:T(8,128)(2,1)S(1)} %bitcast.370), channel_id=1, replica_groups=mesh['fsdp'=32] {'fsdp'}, dimensions={0}, use_global_device_ids=true | all-gather | bytes 126720 | tf_op jit(solution)/shard_map/all_gather | solution.py:145
  949.6 34.3 %all-to-all-done.2 = f32[32,3,32,1536]{3,2,1,0:T(8,128)} async-done(((f32[32,3,32,1536]{3,2,1,0:T(8,128)}), f32[32,3,32,1536]{3,2,1,0:T(8,128)}, u32[]{:S(2)}, u32[]{:S(2)}) %all-to-all-start.2) | async-done | bytes 18874400 | tf_op jit(solution)/shard_map/all_to_all | solution.py:250
  983.9 17.0 copy.218
  1000.9 11.5 fusion.117
  1012.4 8.6 reshape_reshape.6
  1021.0 10.9 gather_fusion
  1031.9 13.2 fusion.56
  1046.7 8.4 scatter_custom_fusion.1
  1055.0 4.6 concatenate.57
  1059.6 10.0 gather_fusion.3
  1069.6 235.0 %all_to_all.57 = bf16[32,3,32,1536]{3,2,1,0:T(8,128)(2,1)S(1)} all-to-all(bf16[32,3,32,1536]{3,2,1,0:T(8,128)(2,1)} %bitcast.328), channel_id=1, replica_groups=mesh['fsdp'=32] {'fsdp'}, dimensions={0} | all-to-all | bytes 18874368 | tf_op jit(solution)/shard_map/all_to_all | solution.py:274
  1304.6 17.7 fusion.34
  1322.3 15.7 fusion.15
  1338.1 6.9 copy.231
  1344.9 4.0 all-to-all-start.4
  1349.0 1.5 fusion.96
  1350.5 7.7 fusion.21
  1358.3 16.3 fusion.35
  1374.6 396.7 %all-to-all-done.4 = f32[32,3,32,1536]{3,2,1,0:T(8,128)} async-done(((f32[32,3,32,1536]{3,2,1,0:T(8,128)}), f32[32,3,32,1536]{3,2,1,0:T(8,128)}, u32[]{:S(2)}, u32[]{:S(2)}) %all-to-all-start.4) | async-done | bytes 18874400 | tf_op jit(solution)/shard_map/all_to_all | solution.py:295
  1771.3 17.0 copy.219
  1788.3 11.7 fusion.118
  1799.9 8.6 reshape_reshape.7
  1808.5 10.9 gather_fusion.1
  1819.5 4.4 bitcast_reduce_fusion
  1826.3 5.0 fusion.83
  1831.3 16.9 fusion.23
  1848.2 7.6 pad_maximum_fusion
  1855.8 22.8 copy.182
  1878.5 3.9 all-to-all-start.5
  1882.9 4.7 convolution_convert_fusion
  1890.6 1.5 convolution_bitcast_fusion.1
  1895.4 7.8 fusion.74
  1903.3 1.4 copy.213
  1904.7 425.0 %all-to-all-done.5 = f32[1536,3,640]{2,1,0:T(4,128)} async-done(((f32[1536,3,640]{2,1,0:T(4,128)}), f32[1536,3,640]{2,1,0:T(4,128)}, u32[]{:S(2)}, u32[]{:S(2)}) %all-to-all-start.5) | async-done | bytes 11796512 | tf_op jit(solution)/shard_map/all_to_all | solution.py:306
  2329.7 17.1 copy.232
  2346.8 12.8 all_to_all.50
  2359.6 3.2 slice-done
  2362.9 5.4 copy.220
  2368.3 5.0 copy.216
  2373.3 4.2 copy.221
  2377.5 3.6 fusion.68
  2381.1 37.0 %all-reduce.6 = (f32[1536]{0:T(1024)S(1)}, f32[1536]{0:T(1024)S(1)}) all-reduce(f32[1536]{0:T(1024)S(1)} %get-tuple-element.12, f32[1536]{0:T(1024)S(1)} %copy-done.37), channel_id=2, replica_groups=mesh['fsdp'=32] {'fsdp'}, use_global_device_ids=true, to_apply=%region_18.20.clone | all-reduce | flops 3072 | bytes 24576
  2419.3 2.2 fusion.65
  (204 shorter events, 21.9 us)
Async XLA Ops:
  7.2 270.0 %all-gather.4.cloned.1.call-start = ((), (), s32[]{:S(2)}) async-start(), calls=%async_computation.9 | async-start | bytes 8110080 | tf_op jit(solution)/shard_map/all_gather | solution.py:142
  83.7 8.0 copy-start.38
  83.7 8.3 copy-start.50
  83.7 8.6 copy-start.51
  83.8 179.8 %copy-start.46 = (s32[128]{0:T(128)S(1)}, s32[128]{0:T(128)}, u32[]{:S(2)}) copy-start(s32[128]{0:T(128)} %param.18) | copy-start | bytes 1540
  83.8 192.2 %copy-start.49 = (s32[96]{0:T(128)S(1)}, s32[96]{0:T(128)}, u32[]{:S(2)}) copy-start(s32[96]{0:T(128)} %constant.128) | copy-start | bytes 1156
  83.8 192.4 %copy-start.2 = (bf16[128,1536]{1,0:T(8,128)(2,1)S(1)}, bf16[128,1536]{1,0:T(8,128)(2,1)}, u32[]{:S(2)}) copy-start(bf16[128,1536]{1,0:T(8,128)(2,1)} %param.16) | copy-start | bytes 1179652
  83.8 228.3 %all-to-all-start.1 = ((bf16[32,2,46080]{2,1,0:T(2,128)(2,1)}), bf16[32,2,46080]{2,1,0:T(2,128)(2,1)}, u32[]{:S(2)}, u32[]{:S(2)}) async-start(bf16[32,2,46080]{2,1,0:T(2,128)(2,1)} %reshape.460), calls=%async_computation.1 | async-start | bytes 11796480 | tf_op jit(solution)/shard_map/all_to_all | solution.py:153
  91.0 194.4 %all-gather.6.cloned.1.call-start = ((), (), s32[]{:S(2)}) async-start(), calls=%async_computation.10 | async-start | bytes 4866048 | tf_op jit(solution)/shard_map/all_gather | solution.py:143
  91.9 172.3 %copy-start.16 = (s32[128,8]{1,0:T(8,128)}, s32[128,8]{1,0:T(8,128)S(1)}, u32[]{:S(2)}) copy-start(s32[128,8]{1,0:T(8,128)S(1)} %copy.164) | copy-start | bytes 12292
  263.6 18.2 copy-start.26
  263.8 25.5 %copy-start.33 = (f32[1536]{0:T(1024)}, f32[1536]{0:T(1024)S(1)}, u32[]{:S(2)}) copy-start(f32[1536]{0:T(1024)S(1)} %convert_element_type.110) | copy-start | bytes 18436
  276.0 26.3 %copy-start.43 = (s32[1024]{0:T(1024)}, s32[1024]{0:T(1024)S(1)}, u32[]{:S(2)}) copy-start(s32[1024]{0:T(1024)S(1)} %pad_clamp_fusion) | copy-start | bytes 12292
  276.9 4.8 copy-start.39
  277.2 5.3 copy-start.22
  277.2 5.3 copy-start.24
  282.4 6.3 copy-start.11
  282.5 6.3 copy-start.31
  282.5 6.3 copy-start.32
  282.6 1.1 copy-start.15
  283.7 1.2 copy-start
  284.1 13.8 copy-start.29
  285.3 17.0 copy-start.7
  288.8 1.0 copy-start.4
  289.4 13.0 copy-start.44
  312.0 213.7 %all-to-all-start = ((bf16[32,3,32,1536]{3,2,1,0:T(8,128)(2,1)}), bf16[32,3,32,1536]{3,2,1,0:T(8,128)(2,1)}, u32[]{:S(2)}, u32[]{:S(2)}) async-start(bf16[32,3,32,1536]{3,2,1,0:T(8,128)(2,1)} %bitcast.327), calls=%async_computation | async-start | bytes 18874368 | tf_op jit(solution)/shard_map/all_to_all | solution.py:241
  559.2 4.1 copy-start.42
  559.2 389.9 %copy-start.9 = (bf16[128,1536]{1,0:T(8,128)(2,1)S(1)}, bf16[128,1536]{1,0:T(8,128)(2,1)}, u32[]{:S(2)}) copy-start(bf16[128,1536]{1,0:T(8,128)(2,1)} %param.17) | copy-start | bytes 1179652
  559.2 424.7 %all-to-all-start.2 = ((f32[32,3,32,1536]{3,2,1,0:T(8,128)}), f32[32,3,32,1536]{3,2,1,0:T(8,128)}, u32[]{:S(2)}, u32[]{:S(2)}) async-start(f32[32,3,32,1536]{3,2,1,0:T(8,128)} %fusion.31), calls=%async_computation.2 | async-start | bytes 37748736 | tf_op jit(solution)/shard_map/all_to_all | solution.py:250
  949.1 51.8 %copy-start.12 = (bf16[1536,40]{0,1:T(8,128)(2,1)}, bf16[1536,40]{0,1:T(8,128)(2,1)S(1)}, u32[]{:S(2)}) copy-start(bf16[1536,40]{0,1:T(8,128)(2,1)S(1)} %reshape.430) | copy-start | bytes 368644
  983.9 17.0 copy-start.35
  1031.9 13.2 copy-start.17
  1304.6 17.7 copy-start.6
  1344.9 426.3 %all-to-all-start.4 = ((f32[32,3,32,1536]{3,2,1,0:T(8,128)}), f32[32,3,32,1536]{3,2,1,0:T(8,128)}, u32[]{:S(2)}, u32[]{:S(2)}) async-start(f32[32,3,32,1536]{3,2,1,0:T(8,128)} %bitcast.321), calls=%async_computation.4 | async-start | bytes 37748736 | tf_op jit(solution)/shard_map/all_to_all | solution.py:295
  1349.0 554.3 %reduce-scatter.10.cloned.1.call-start = ((), (), s32[]{:S(2)}) async-start(), calls=%async_computation.13 | async-start | bytes 811008
  1350.5 1071.0 %reduce-scatter.8.cloned.1.call-start = ((), (), s32[]{:S(2)}) async-start(), calls=%async_computation.12 | async-start | bytes 9732096 | tf_op jit(solution)/shard_map/reduce_scatter | solution.py:392
  1771.3 17.0 copy-start.36
  1819.4 4.4 copy-start.5
  1819.4 4.4 copy-start.13
  1819.4 4.5 copy-start.34
  1819.4 4.5 copy-start.45
  1819.4 5.8 copy-start.10
  1819.4 5.8 copy-start.48
  1819.4 6.8 copy-start.8
  1878.5 451.2 %all-to-all-start.5 = ((f32[1536,3,640]{2,1,0:T(4,128)}), f32[1536,3,640]{2,1,0:T(4,128)}, u32[]{:S(2)}, u32[]{:S(2)}) async-start(f32[1536,3,640]{2,1,0:T(4,128)} %copy.182), calls=%async_computation.7 | async-start | bytes 31457280 | tf_op jit(solution)/shard_map/all_to_all | solution.py:306
  1882.4 6.7 copy-start.1
  1882.5 9.6 copy-start.23
  1882.5 539.0 %reduce-scatter.6.cloned.1.call-start = ((), (), s32[]{:S(2)}) async-start(), calls=%async_computation.11 | async-start | bytes 16220160 | tf_op jit(solution)/shard_map/reduce_scatter | solution.py:391
  1887.7 7.7 copy-start.3
  1888.9 5.1 copy-start.25
  1888.9 5.3 copy-start.30
  1888.9 6.4 copy-start.27
  1889.0 6.4 copy-start.40
  1892.9 1.9 copy-start.20
  2359.6 3.2 slice-start
  2362.9 14.6 slice-start.2
  2368.3 5.0 slice-start.1
  2368.3 9.2 slice-start.3
  2373.3 4.2 copy-start.19
  2373.3 4.2 copy-start.21
  2373.3 4.2 copy-start.28
  2373.3 4.2 copy-start.41
  2377.5 3.6 copy-start.37
  2377.5 41.8 %copy-start.47 = (f32[128]{0:T(128)S(1)}, f32[128]{0:T(128)}, u32[]{:S(2)}) copy-start(f32[128]{0:T(128)} %get-tuple-element.36) | copy-start | bytes 1540
  (2 other events, 1.3 us)
Sparse Core Ops, SparseCore 0:
  10.9 77.9 all-gather.3
  94.7 120.5 all-gather.5
  1354.9 212.6 reduce-scatter.9
  1831.4 269.9 reduce-scatter.7
  2108.8 238.7 reduce-scatter.5
where the time goes:
time: 2440 us; the launch traced here: 2430 us
  waiting for transfers between devices  1010 us (41%)
  blocking collectives  828 us (34%)
  local copies, waits for them, and re-layouts  324 us (13%)
  matrix products  183 us (8%)
  other arithmetic  44.3 us (2%)
    all_to_all x1, waiting for transfers between devices, on_device(): lax.all_to_all(owned_grads, 'fsdp', split_axis=0, concat_axis=2, tiled=True)  425 us
    all_to_all x1, waiting for transfers between devices, on_device(): lax.all_to_all(partial_back, 'fsdp', split_axis=0, concat_axis=0, tiled=T...  397 us
    all_gather x1, blocking collectives, on_device(): lax.all_gather(router, 'fsdp', axis=0, tiled=True)  385 us
    all_to_all x1, blocking collectives, on_device(): lax.all_to_all(send_grad, 'fsdp', split_axis=0, concat_axis=0, tiled=True)  235 us
    unnamed x2, blocking collectives  208 us
    all_to_all x1, waiting for transfers between devices, on_device(): lax.all_to_all(send_in, 'fsdp', split_axis=0, concat_axis=0, tiled=True)  152 us
    unnamed x123, local copies, waits for them, and re-layouts  115 us
  transfers between devices with their start and end apart: 10, of which 4 were waited for; matrix products, arithmetic and copies ran while one was open for 15% of the time, Pallas kernels for 0%

commit v1 on v0

--- a/solution.py
+++ b/solution.py
@@ -1,9 +1,11 @@
+import functools
 import math
-
 import jax
 import jax.numpy as jnp
 import numpy as np
 from jax import lax
+from jax.experimental import pallas as pl
+from jax.experimental.pallas import tpu as pltpu
 from jax.sharding import PartitionSpec as P
 
 MODEL_WIDTH = 1536
@@ -26,9 +28,8 @@
 def positions(sequence_ids):
     sequence_length = sequence_ids.shape[0]
     places = jnp.arange(sequence_length, dtype=jnp.int32)
-    starts_new = jnp.concatenate([jnp.ones((1,), jnp.bool_), sequence_ids[1:] != sequence_ids[:-1]])
-    begins = lax.cummax(jnp.where(starts_new, places, 0), axis=0)
-    return places - begins
+    same = (sequence_ids[:, None] == sequence_ids[None, :]) & (places[None, :] < places[:, None])
+    return jnp.sum(same.astype(jnp.int32), axis=1, dtype=jnp.int32)
 
 
 def rope_tables(places, head_size):
@@ -82,11 +83,14 @@
 
 
 def expert_slots(expert_ids, experts, capacity):
-    flat_ids = expert_ids.reshape(-1)
-    onehot = (flat_ids[:, None] == jnp.arange(experts, dtype=jnp.int32)[None, :]).astype(jnp.int32)
-    running = jnp.cumsum(onehot, axis=0, dtype=jnp.int32)
-    ranks = jnp.sum((running - 1) * onehot, axis=-1, dtype=jnp.int32)
-    return flat_ids * capacity + ranks
+    rows = expert_ids.shape[0]
+    picked = expert_ids[:, :, None] == jnp.arange(experts, dtype=jnp.int32)[None, None, :]
+    named = jnp.any(picked, axis=1).astype(jnp.bfloat16)
+    places = jnp.arange(rows, dtype=jnp.int32)
+    before = (places[None, :] < places[:, None]).astype(jnp.bfloat16)
+    ranks = jnp.dot(before, named, preferred_element_type=jnp.float32)
+    ranks = jnp.sum(jnp.where(picked, ranks[:, None, :], 0.0), axis=-1).astype(jnp.int32)
+    return (expert_ids * capacity + ranks).reshape(-1)
 
 
 def owner_tables(devices):
@@ -102,7 +106,10 @@
     padded = jnp.concatenate(
         [buffer_rows, jnp.zeros((1, CAP, MODEL_WIDTH), buffer_rows.dtype)], axis=0
     )
-    picked_rows = jnp.take(padded, jnp.asarray(send_table, dtype=jnp.int32), axis=0)
+    chosen = jnp.asarray(send_table[:, None] == np.arange(E + 1)[None, :], dtype=buffer_rows.dtype)
+    picked_rows = jnp.einsum(
+        "se,ecd->scd", chosen, padded, preferred_element_type=jnp.float32
+    ).astype(buffer_rows.dtype)
     return picked_rows.reshape(devices, span_count, CAP, MODEL_WIDTH)
 
 
@@ -406,34 +413,545 @@
     )
 
 
+MESH = pl.DeviceIdType.MESH
+
+def place():
+    me = lax.axis_index("fsdp")
+    return me // 8, lax.rem(me // 4, 2), lax.rem(me // 2, 2), lax.rem(me, 2)
+
+def dev(z, y, x, c):
+    return ((z * 2 + y) * 2 + x) * 2 + c
+
+def z_order(z, q):
+    table = ((0, 1, 2, 3), (1, 0, 2, 3), (2, 3, 1, 0), (3, 2, 1, 0))
+    v = jnp.int32(table[0][q])
+    for k in range(1, 4):
+        v = jnp.where(z == k, table[k][q], v)
+    return v
+
+def greet(z, near, up, down):
+    barrier = pltpu.get_barrier_semaphore()
+    for d in near:
+        pl.semaphore_signal(barrier, inc=1, device_id=(d,), device_id_type=MESH)
+    @pl.when(z < 3)
+    def _():
+        pl.semaphore_signal(barrier, inc=1, device_id=(up,), device_id_type=MESH)
+    @pl.when(z > 0)
+    def _():
+        pl.semaphore_signal(barrier, inc=1, device_id=(down,), device_id_type=MESH)
+    pl.semaphore_wait(barrier, len(near) + jnp.where(z < 3, 1, 0) + jnp.where(z > 0, 1, 0))
+
+def gather_kernel(parts, count, *refs):
+    shards, outs = refs[:count], refs[count:2 * count]
+    (local_sem, zs, zs2, zr, fs, fr, s1s, s1r, s2s, s2r, cs, cr) = refs[2 * count:]
+    z, y, x, c = place()
+    sib, xn, yn = dev(z, y, x, 1 - c), dev(z, y, 1 - x, c), dev(z, 1 - y, x, c)
+    up, down = dev(z + 1, y, x, c), dev(z - 1, y, x, c)
+    greet(z, (sib, xn, yn), up, down)
+
+    def at(p, d):
+        a, c0, w, _ = parts[p]
+        rows = shards[a].shape[0]
+        return outs[a].at[pl.ds(pl.multiple_of(d * rows, rows), rows), pl.ds(c0, w)]
+
+    def own(p):
+        a, c0, w, _ = parts[p]
+        return shards[a].at[:, pl.ds(c0, w)]
+
+    def rc(src, dst, ss, rs, to):
+        return pltpu.make_async_remote_copy(src_ref=src, dst_ref=dst, send_sem=ss, recv_sem=rs, device_id=(to,), device_id_type=MESH)
+
+    me = dev(z, y, x, c)
+    locals_ = []
+    for a in range(count):
+        rows = shards[a].shape[0]
+        l = pltpu.make_async_copy(shards[a], outs[a].at[pl.ds(pl.multiple_of(me * rows, rows), rows)], local_sem.at[a])
+        l.start(); locals_.append(l)
+    P = len(parts)
+    zq = [z_order(z, q) for q in range(4)]
+    sends = []
+    def go(copy):
+        copy.start(); sends.append(copy)
+
+    def stage1(q):
+        for p in range(P):
+            first, second = (xn, yn) if parts[p][3] == 0 else (yn, xn)
+            d = dev(zq[q], y, x, c)
+            here = at(p, d)
+            if q == 0:
+                src = own(p)
+                @pl.when(z < 3)
+                def _():
+                    rc(src, here, zs.at[0, p], zr.at[z, p], up).start()
+                @pl.when(z > 0)
+                def _():
+                    rc(src, here, zs2.at[p], zr.at[z, p], down).start()
+            else:
+                src = here
+                rc(here, here, zs.at[q, p], zr.at[zq[q], p], up).wait_recv()
+                @pl.when((zq[q] < z) & (z < 3))
+                def _():
+                    rc(src, here, zs.at[q, p], zr.at[zq[q], p], up).start()
+                @pl.when((zq[q] > z) & (z > 0))
+                def _():
+                    rc(src, here, zs.at[q, p], zr.at[zq[q], p], down).start()
+            go(rc(src, here, fs.at[q, p], fr.at[q, p], first))
+            go(rc(src, here, s1s.at[q, p], s1r.at[q, p], second))
+            go(rc(src, here, cs.at[0, q, p], cr.at[0, q, p], sib))
+
+    def near(q, p):
+        return dev(zq[q], y, 1 - x, c) if parts[p][3] == 0 else dev(zq[q], 1 - y, x, c)
+    def side(q, p):
+        return dev(zq[q], 1 - y, x, c) if parts[p][3] == 0 else dev(zq[q], y, 1 - x, c)
+
+    def stage2(q):
+        for p in range(P):
+            first, second = (xn, yn) if parts[p][3] == 0 else (yn, xn)
+            there = at(p, near(q, p))
+            rc(there, there, fs.at[q, p], fr.at[q, p], first).wait_recv()
+            go(rc(there, there, s2s.at[q, p], s2r.at[q, p], second))
+            go(rc(there, there, cs.at[1, q, p], cr.at[1, q, p], sib))
+
+    def stage3(q):
+        for p in range(P):
+            there = at(p, side(q, p))
+            rc(there, there, s1s.at[q, p], s1r.at[q, p], sib).wait_recv()
+            go(rc(there, there, cs.at[2, q, p], cr.at[2, q, p], sib))
+        for p in range(P):
+            there = at(p, dev(zq[q], 1 - y, 1 - x, c))
+            rc(there, there, s2s.at[q, p], s2r.at[q, p], sib).wait_recv()
+            go(rc(there, there, cs.at[3, q, p], cr.at[3, q, p], sib))
+
+    stage1(0); stage1(1); stage2(0); stage1(2); stage2(1); stage3(0); stage1(3); stage2(2); stage3(1); stage2(3); stage3(2); stage3(3)
+    for q in range(4):
+        for p in range(P):
+            for k, where in enumerate((dev(zq[q], y, x, 1 - c), None, None, None)):
+                if k == 0: d = dev(zq[q], y, x, 1 - c)
+                elif k == 1: d = near(q, p) + 1 - 2 * c
+                elif k == 2: d = side(q, p) + 1 - 2 * c
+                else: d = dev(zq[q], 1 - y, 1 - x, 1 - c)
+                there = at(p, d)
+                rc(there, there, cs.at[k, q, p], cr.at[k, q, p], sib).wait_recv()
+    for copy in sends: copy.wait_send()
+    for p in range(P):
+        here = at(p, me)
+        @pl.when(z < 3)
+        def _():
+            rc(here, here, zs.at[0, p], zr.at[z, p], up).wait_send()
+        @pl.when(z > 0)
+        def _():
+            rc(here, here, zs2.at[p], zr.at[z, p], down).wait_send()
+        for q in range(1, 4):
+            @pl.when(((zq[q] < z) & (z < 3)) | ((zq[q] > z) & (z > 0)))
+            def _():
+                rc(here, here, zs.at[q, p], zr.at[zq[q], p], up).wait_send()
+    for l in locals_: l.wait()
+
+def gather(arrays, parts, collective_id):
+    n = 32; k = len(arrays); P = len(parts)
+    dma = pltpu.SemaphoreType.DMA
+    return pl.pallas_call(
+        functools.partial(gather_kernel, parts, k),
+        out_shape=[jax.ShapeDtypeStruct((n * a.shape[0],) + a.shape[1:], a.dtype) for a in arrays],
+        in_specs=[pl.BlockSpec(memory_space=pl.ANY)] * k,
+        out_specs=[pl.BlockSpec(memory_space=pl.ANY)] * k,
+        scratch_shapes=[dma((k,)), dma((4, P)), dma((P,)), dma((4, P)), dma((4, P)), dma((4, P)), dma((4, P)), dma((4, P)), dma((4, P)), dma((4, P)), dma((4, 4, P)), dma((4, 4, P))],
+        compiler_params=pltpu.CompilerParams(collective_id=collective_id, has_side_effects=True),
+    )(*arrays)
+
+
+def scatter_kernel(parts, count, rows, *refs):
+    fulls, outs = refs[:count], refs[count:2 * count]
+    refs = refs[2 * count:]
+    held, r0, r1, r2, r3 = (refs[i * count:(i + 1) * count] for i in range(5))
+    (ls, s0, e0, s1, e1, s2, e2, s3, e3) = refs[5 * count:]
+    z, y, x, c = place()
+    sib, xn, yn = dev(z, y, x, 1 - c), dev(z, y, 1 - x, c), dev(z, 1 - y, x, c)
+    up, down = dev(z + 1, y, x, c), dev(z - 1, y, x, c)
+    greet(z, (sib, xn, yn), up, down)
+
+    P = len(parts)
+    zq = [z_order(z, q) for q in range(4)]
+    sends = []
+    def rc(src, dst, ss, rs, to):
+        return pltpu.make_async_remote_copy(src_ref=src, dst_ref=dst, send_sem=ss, recv_sem=rs, device_id=(to,), device_id_type=MESH)
+    def go(copy):
+        copy.start(); sends.append(copy)
+    def cut(p):
+        return pl.ds(parts[p][1], parts[p][2])
+    def spot(p, k):
+        if parts[p][3] == 0:
+            return ((1 - y, 1 - x), (1 - y, x), (y, 1 - x), (y, x))[k]
+        return ((1 - y, 1 - x), (y, 1 - x), (1 - y, x), (y, x))[k]
+    def slot(q, yy, xx):
+        return (yy * 2 + xx) * 4 + zq[q]
+    def source(p, q, k, core):
+        a = parts[p][0]
+        yy, xx = spot(p, k)
+        d = dev(zq[q], yy, xx, core)
+        return fulls[a].at[pl.ds(pl.multiple_of(d * rows[a], rows[a]), rows[a]), cut(p)]
+
+    loads = {}
+    for q in (3, 2, 1, 0):
+        for k in range(4):
+            for p in range(P):
+                a = parts[p][0]
+                go(rc(source(p, q, k, 1 - c), r0[a].at[slot(q, *spot(p, k)), :, cut(p)], s0.at[q, k, p], e0.at[q, k, p], sib))
+                l = pltpu.make_async_copy(source(p, q, k, c), held[a].at[slot(q, *spot(p, k)), :, cut(p)], ls.at[q, k, p])
+                l.start(); loads[q, k, p] = l
+
+    def add(p, dst, s_dst, src, s_src, more=None, out=None):
+        a, c0, w, _ = parts[p]
+        step = 16
+        def body(i, carry):
+            r = pl.ds(pl.multiple_of(i * step, step), step)
+            v = dst[s_dst, r, c0:c0 + w].astype(jnp.float32) + src[s_src, r, c0:c0 + w].astype(jnp.float32)
+            dst[s_dst, r, c0:c0 + w] = v.astype(dst.dtype)
+            return carry
+        lax.fori_loop(0, rows[a] // step, body, 0)
+
+    def stage1(q):
+        for k in range(4):
+            for p in range(P):
+                a = parts[p][0]
+                first = yn if parts[p][3] == 0 else xn
+                s = slot(q, *spot(p, k))
+                here = held[a].at[s, :, cut(p)]
+                rc(here, r0[a].at[s, :, cut(p)], s0.at[q, k, p], e0.at[q, k, p], sib).wait_recv()
+                loads[q, k, p].wait()
+                add(p, held[a], s, r0[a], s)
+                if k < 2:
+                    go(rc(here, r1[a].at[q * 2 + k, :, cut(p)], s1.at[q, k, p], e1.at[q, k, p], first))
+
+    def stage2(q):
+        for k in range(2):
+            for p in range(P):
+                a = parts[p][0]
+                second = xn if parts[p][3] == 0 else yn
+                s = slot(q, *spot(p, k + 2))
+                here = held[a].at[s, :, cut(p)]
+                rc(here, r1[a].at[q * 2 + k, :, cut(p)], s1.at[q, k, p], e1.at[q, k, p], sib).wait_recv()
+                add(p, held[a], s, r1[a], q * 2 + k)
+                if k == 0:
+                    go(rc(here, r2[a].at[q, :, cut(p)], s2.at[q, p], e2.at[q, p], second))
+
+    def stage3(q):
+        for p in range(P):
+            a = parts[p][0]
+            s = slot(q, y, x)
+            here = held[a].at[s, :, cut(p)]
+            rc(here, r2[a].at[q, :, cut(p)], s2.at[q, p], e2.at[q, p], sib).wait_recv()
+            add(p, held[a], s, r2[a], q)
+            if q > 0:
+                @pl.when((zq[q] > z) & (z > 0) | (zq[q] < z) & (z < 3))
+                def _():
+                    land = r3[a].at[zq[q], :, cut(p)]
+                    rc(here, land, s3.at[q, p], e3.at[zq[q], p], sib).wait_recv()
+                    add(p, held[a], s, r3[a], zq[q])
+                @pl.when(zq[q] > z)
+                def _():
+                    rc(here, r3[a].at[zq[q], :, cut(p)], s3.at[q, p], e3.at[zq[q], p], up).start()
+                @pl.when((zq[q] < z) & (zq[q] == z - 1))
+                def _():
+                    rc(here, r3[a].at[4, :, cut(p)], s3.at[q, p], e3.at[4, p], down).start()
+                @pl.when(zq[q] < z - 1)
+                def _():
+                    rc(here, r3[a].at[zq[q], :, cut(p)], s3.at[q, p], e3.at[zq[q], p], down).start()
+            else:
+                @pl.when(z > 0)
+                def _():
+                    rc(here, r3[a].at[z, :, cut(p)], s3.at[q, p], e3.at[z, p], sib).wait_recv()
+                @pl.when(z < 3)
+                def _():
+                    rc(here, r3[a].at[4, :, cut(p)], s3.at[q, p], e3.at[4, p], sib).wait_recv()
+                a_, c0, w, _m = parts[p]
+                step = 16
+                zero = jnp.float32(0)
+                def body(i, carry):
+                    r = pl.ds(pl.multiple_of(i * step, step), step)
+                    v = held[a][s, r, c0:c0 + w].astype(jnp.float32)
+                    outs[a][r, c0:c0 + w] = v.astype(outs[a].dtype)
+                    return carry
+                lax.fori_loop(0, rows[a] // step, body, 0)
+                for cond, where in ((z > 0, z), (z < 3, 4)):
+                    @pl.when(cond)
+                    def _():
+                        def more(i, carry):
+                            r = pl.ds(pl.multiple_of(i * step, step), step)
+                            outs[a][r, c0:c0 + w] += r3[a][where, r, c0:c0 + w].astype(jnp.float32)
+                            return carry
+                        lax.fori_loop(0, rows[a] // step, more, 0)
+
+    for f, q in ((1, 3), (1, 2), (2, 3), (1, 1), (2, 2), (3, 3), (1, 0), (2, 1), (3, 2), (2, 0), (3, 1), (3, 0)):
+        (stage1, stage2, stage3)[f - 1](q)
+    for copy in sends: copy.wait_send()
+    for q in range(1, 4):
+        for p in range(P):
+            a = parts[p][0]
+            here = held[a].at[slot(q, y, x), :, cut(p)]
+            rc(here, here, s3.at[q, p], e3.at[0, p], sib).wait_send()
+
+def scatter(arrays, parts, collective_id):
+    k = len(arrays); P = len(parts)
+    dma = pltpu.SemaphoreType.DMA
+    rows = [a.shape[0] // 32 for a in arrays]
+    scr = []
+    for cnt in (16, 16, 8, 4, 5):
+        scr += [pltpu.VMEM((cnt, a.shape[0] // 32, a.shape[1]), a.dtype) for a in arrays]
+    return pl.pallas_call(
+        functools.partial(scatter_kernel, parts, k, rows),
+        out_shape=[jax.ShapeDtypeStruct((a.shape[0] // 32, a.shape[1]), jnp.float32) for a in arrays],
+        in_specs=[pl.BlockSpec(memory_space=pl.ANY)] * k,
+        out_specs=[pl.BlockSpec(memory_space=pltpu.VMEM)] * k,
+        scratch_shapes=scr + [dma((4, 4, P)), dma((4, 4, P)), dma((4, 4, P)), dma((4, 2, P)), dma((4, 2, P)), dma((4, P)), dma((4, P)), dma((4, P)), dma((5, P))],
+        compiler_params=pltpu.CompilerParams(collective_id=collective_id, has_side_effects=True, vmem_limit_bytes=60 * 2**20),
+    )(*arrays)
+
+
+D = MODEL_WIDTH
+SRC = 8
+STEPS = 4
+M = SRC * CAP
+F32, BF16 = jnp.float32, jnp.bfloat16
+HALVES = ((0, 512, 1280), (1024, 128, 1792))
+
+def nt(a, b):
+    return lax.dot_general(a, b, (((1,), (1,)), ((), ())), preferred_element_type=F32)
+def nn(a, b):
+    return lax.dot_general(a, b, (((1,), (0,)), ((), ())), preferred_element_type=F32)
+def tn(a, b):
+    return lax.dot_general(a, b, (((0,), (0,)), ((), ())), preferred_element_type=F32)
+
+def expert_kernel(own_ref, t_ref, c_ref, pick_ref, router_ref, w_ref, out_ref, gin_ref, gg_ref, dw_ref,
+                  x_ref, g_ref, rw_ref, act_ref, dgu_ref, actq_ref, dguq_ref, ow_ref, gi_ref):
+    i = pl.program_id(0)
+    mine = (own_ref[0], own_ref[1])
+    logits = nt(router_ref[...], t_ref[...])
+    row = lax.broadcasted_iota(jnp.int32, logits.shape, 0)
+    logits = jnp.where(row < E, logits, -jnp.inf)
+    e = jnp.exp(logits - jnp.max(logits, axis=0, keepdims=True))
+    probs = e / jnp.sum(e, axis=0, keepdims=True)
+    mineprob = [jnp.sum(jnp.where(row == m, probs, 0.0), axis=0, keepdims=True) for m in mine]
+    at = pl.ds(pl.multiple_of(i * M, M), M)
+    for s in range(SRC):
+        pick = pick_ref[s * 64:s * 64 + 64, :]
+        xs = nn(pick, t_ref[s * 128:s * 128 + 128, :]).astype(BF16)
+        gs = nn(pick, c_ref[s * 128:s * 128 + 128, :]).astype(BF16)
+        wide = pick.astype(F32)
+        for k in range(2):
+            to = pl.ds(pl.multiple_of(i * M + s * CAP, CAP), CAP)
+            x_ref[k, to, :] = xs[k * 32:k * 32 + 32]
+            g_ref[k, to, :] = gs[k * 32:k * 32 + 32]
+            rw_ref[k, s * CAP:s * CAP + CAP, :] = jnp.broadcast_to(jnp.sum(wide[k * 32:k * 32 + 32] * mineprob[k][:, s * 128:(s + 1) * 128], axis=1, keepdims=True), (CAP, 128))
+    gws = []
+    for k, acts, dgus in ((0, act_ref, dgu_ref), (1, actq_ref, dguq_ref)):
+        g0, w, d0 = HALVES[k]
+        pre = nn(x_ref[k, at, :], w_ref[:, g0:g0 + 2 * w])
+        gate, up = pre[:, :w], pre[:, w:]
+        sig = jax.nn.sigmoid(gate)
+        silu = gate * sig
+        act = (silu * up).astype(BF16)
+        acts[at, :] = act
+        rw = rw_ref[k, :, 0:1]
+        out = nt(act, w_ref[:, d0:d0 + w])
+        mix = g_ref[k, at, :].astype(F32) * 0.22
+        gws.append(jnp.sum(mix * out, axis=1, keepdims=True))
+        ow_ref[k] = (rw * out).astype(BF16)
+        g = (rw * mix).astype(BF16)
+        g_ref[k, at, :] = g
+        da = nn(g, w_ref[:, d0:d0 + w])
+        dgu = jnp.concatenate([(da * up * sig * (1.0 + gate * (1.0 - sig))).astype(BF16), (da * silu).astype(BF16)], axis=1)
+        dgus[at, :] = dgu
+        gi_ref[k] = nt(dgu, w_ref[:, g0:g0 + 2 * w]).astype(BF16)
+    for s in range(SRC):
+        r = slice(s * CAP, s * CAP + CAP)
+        pick = pick_ref[s * 64:s * 64 + 64, :]
+        to = slice(s * 128, s * 128 + 128)
+        out_ref[to, :] = tn(pick, jnp.concatenate([ow_ref[0, r, :], ow_ref[1, r, :]], axis=0)).astype(BF16)
+        gin_ref[to, :] = tn(pick, jnp.concatenate([gi_ref[0, r, :], gi_ref[1, r, :]], axis=0)).astype(BF16)
+        wide = pick.astype(F32)
+        for k in range(2):
+            gg_ref[s, k:k + 1, :] = jnp.sum(wide[k * 32:k * 32 + 32] * gws[k][r], axis=0, keepdims=True)
+        gg_ref[s, 2:8, :] = jnp.zeros((6, 128), F32)
+
+    @pl.when(i == STEPS - 1)
+    def _():
+        def body(j, carry):
+            c = pl.ds(pl.multiple_of(j * 256, 256), 256)
+            for k, acts, dgus in ((0, act_ref, dgu_ref), (1, actq_ref, dguq_ref)):
+                g0, w, d0 = HALVES[k]
+                dw_ref[c, g0:g0 + 2 * w] = tn(x_ref[k, :, c], dgus[...]).astype(BF16)
+                dw_ref[c, d0:d0 + w] = tn(g_ref[k, :, c], acts[...]).astype(BF16)
+            return carry
+        lax.fori_loop(0, D // 256, body, 0)
+
+def experts(owned, tokens, cot, picks, router_t, w):
+    R = SRC * 128
+    return pl.pallas_call(
+        expert_kernel,
+        grid=(STEPS,),
+        in_specs=[
+            pl.BlockSpec(memory_space=pltpu.SMEM),
+            pl.BlockSpec((R, D), lambda i: (i, 0)),
+            pl.BlockSpec((R, D), lambda i: (i, 0)),
+            pl.BlockSpec((SRC * 64, 128), lambda i: (i, 0)),
+            pl.BlockSpec((64, D), lambda i: (0, 0), pipeline_mode=pl.Buffered(1)),
+            pl.BlockSpec((D, 1920), lambda i: (0, 0), pipeline_mode=pl.Buffered(1)),
+        ],
+        out_specs=[
+            pl.BlockSpec((R, D), lambda i: (i, 0)),
+            pl.BlockSpec((R, D), lambda i: (i, 0)),
+            pl.BlockSpec((SRC, 8, 128), lambda i: (i, 0, 0)),
+            pl.BlockSpec((D, 1920), lambda i: (0, 0), pipeline_mode=pl.Buffered(1)),
+        ],
+        out_shape=[
+            jax.ShapeDtypeStruct((4096, D), BF16), jax.ShapeDtypeStruct((4096, D), BF16),
+            jax.ShapeDtypeStruct((32, 8, 128), F32), jax.ShapeDtypeStruct((D, 1920), BF16),
+        ],
+        scratch_shapes=[
+            pltpu.VMEM((2, 1024, D), BF16), pltpu.VMEM((2, 1024, D), BF16), pltpu.VMEM((2, M, 128), F32),
+            pltpu.VMEM((1024, 512), BF16), pltpu.VMEM((1024, 1024), BF16), pltpu.VMEM((1024, 128), BF16), pltpu.VMEM((1024, 256), BF16),
+            pltpu.VMEM((2, M, D), BF16), pltpu.VMEM((2, M, D), BF16),
+        ],
+        compiler_params=pltpu.CompilerParams(vmem_limit_bytes=62 * 2**20),
+        cost_estimate=pl.CostEstimate(flops=22 * 10**9, bytes_accessed=62 * 10**6, transcendentals=0),
+    )(owned, tokens, cot, picks, router_t, w)
+
+
+GATHER_DENSE = ((0, 0, 1280, 0), (0, 1280, 1280, 1), (1, 0, 768, 0), (1, 768, 896, 1), (2, 0, 128, 0))
+TOKEN_HALVES = ((0, 0, 768, 0), (0, 768, 768, 1))
+GATHER_TOKENS = TOKEN_HALVES + ((1, 0, 768, 0), (1, 768, 768, 1))
+SCATTER_LAST = ((0, 0, 1280, 0), (0, 1280, 1280, 1), (1, 0, 768, 0), (1, 768, 896, 1), (2, 0, 768, 0), (2, 768, 768, 1))
+
+
+def fast(
+    layer_input, cotangent, sequence_ids, expert_ids, attention_gain, qkv_weight, output_weight, moe_gain, router, gate_up, down_proj
+):
+    n, own_rows, T = 32, gate_up.shape[0], layer_input.shape[0]
+    group = QUERY_HEADS // KEY_VALUE_HEADS
+    q_width, k_width = QUERY_HEADS * HEAD_WIDTH, KEY_VALUE_HEADS * HEAD_WIDTH
+    me = lax.axis_index("fsdp")
+    small = jnp.concatenate(
+        [router, attention_gain[:, None], moe_gain[:, None], jnp.zeros((own_rows, 86), BF16)], axis=1
+    )
+    qkv_full, out_small, ids_all = gather(
+        [qkv_weight, jnp.concatenate([output_weight, small], axis=1), expert_ids.T], GATHER_DENSE, 0
+    )
+    out_full, small_full = out_small[:, :D], out_small[:, D:]
+    router_full, gain_one, gain_two = small_full[:, :E], small_full[:, E].astype(F32), small_full[:, E + 1].astype(F32)
+
+    gu = jnp.transpose(gate_up, (1, 0, 2)).reshape(8, 5, own_rows, 2 * F)
+    dp = jnp.transpose(down_proj, (1, 0, 2)).reshape(8, 5, own_rows, F)
+    gu_q = jnp.transpose(gu[:, 4].reshape(8, own_rows, 2, 4, 128), (0, 3, 1, 2, 4)).reshape(n, own_rows, 256)
+    dp_q = jnp.transpose(dp[:, 4].reshape(8, own_rows, 4, 128), (0, 2, 1, 3)).reshape(n, own_rows, 128)
+    pack = jnp.concatenate(
+        [gu[:, :4].reshape(n, own_rows, 2 * F), gu_q, dp[:, :4].reshape(n, own_rows, F), dp_q], axis=2
+    )
+    pack, qkv_full = lax.optimization_barrier((pack, qkv_full))
+    w = lax.all_to_all(pack, "fsdp", split_axis=0, concat_axis=0, tiled=True).reshape(D, 1920)
+
+    inputs = layer_input.astype(F32)
+    scale_one = norm_scale(inputs)
+    normed_one = (inputs * scale_one * gain_one).astype(BF16)
+    joined = jnp.dot(normed_one, qkv_full, preferred_element_type=F32)
+    cosine, sine = rope_tables(positions(sequence_ids), HEAD_WIDTH)
+    queries = apply_rotary(joined[:, :q_width].reshape(T, QUERY_HEADS, HEAD_WIDTH), cosine, sine).astype(BF16)
+    queries = queries.reshape(T, KEY_VALUE_HEADS, group, HEAD_WIDTH)
+    keys = apply_rotary(joined[:, q_width : q_width + k_width].reshape(T, KEY_VALUE_HEADS, HEAD_WIDTH), cosine, sine).astype(BF16)
+    values = joined[:, q_width + k_width :].reshape(T, KEY_VALUE_HEADS, HEAD_WIDTH).astype(BF16)
+    place_in = jnp.arange(T, dtype=jnp.int32)
+    allowed = (sequence_ids[:, None] == sequence_ids[None, :]) & (place_in[None, :] <= place_in[:, None])
+    scores = jnp.einsum("qkgd,tkd->kgqt", queries, keys, preferred_element_type=F32) * ATTN_SCALE
+    scores = jnp.where(allowed, scores, -jnp.inf)
+    peak = jnp.max(scores, axis=-1, keepdims=True)
+    log_total = peak + jnp.log(jnp.sum(jnp.exp(scores - peak), axis=-1, keepdims=True))
+    probs = jnp.exp(scores - log_total)
+    probs_half = probs.astype(BF16)
+    attended = jnp.einsum("kgqt,tkd->qkgd", probs_half, values, preferred_element_type=F32).reshape(T, q_width).astype(BF16)
+    middle = inputs + RESIDUAL_SCALE * jnp.dot(attended, out_full, preferred_element_type=F32)
+    scale_two = norm_scale(middle)
+    normed_two = (middle * scale_two * gain_two).astype(BF16)
+
+    tokens, cots = gather([normed_two, cotangent], GATHER_TOKENS, 1)
+    whole, fifth = (me // 4) * 5 + lax.rem(me, 4), (me // 4) * 5 + 4
+    owned = jnp.stack([whole, fifth])
+    named = jnp.any(ids_all.reshape(n, TOP, T)[:, :, None, :] == owned[None, None, :, None], axis=1)
+    before = (place_in[:, None] < place_in[None, :]).astype(BF16)
+    ranks = jnp.dot(named.astype(BF16).reshape(2 * n, T), before, preferred_element_type=F32).reshape(n, 2, 1, T)
+    picks = ((ranks == jnp.arange(CAP, dtype=F32)[:, None]) & named[:, :, None, :]).astype(BF16).reshape(n * 64, T)
+    router_t = jnp.pad(router_full.T, ((0, 64 - E), (0, 0)))
+    out_part, gin_part, gg, dw = experts(owned, tokens, cots, picks, router_t, w)
+    gg_all = lax.all_to_all(gg, "fsdp", split_axis=0, concat_axis=0, tiled=True).reshape(8, 4, 8, T)
+    grad_gates = jnp.concatenate([gg_all[:, :, 0], jnp.sum(gg_all[:, :, 1], axis=1, keepdims=True)], axis=1).reshape(E, T).T
+    [gin] = scatter([gin_part], TOKEN_HALVES, 2)
+    dw, gin = lax.optimization_barrier((dw, gin))
+    dw = lax.all_to_all(dw.reshape(n, own_rows, 1920), "fsdp", split_axis=0, concat_axis=0, tiled=True)
+
+    upstream = cotangent.astype(F32)
+    logits = jnp.dot(normed_two, router_full, preferred_element_type=F32)
+    gate_probs = jax.nn.softmax(logits, axis=-1)
+    grad_logits = gate_probs * (grad_gates - jnp.sum(gate_probs * grad_gates, axis=-1, keepdims=True))
+    grad_normed = gin + jnp.einsum("te,de->td", grad_logits, router_full.astype(F32), precision=PRECISE_ARITHMETIC)
+    router_part = jnp.einsum("td,te->de", normed_two.astype(F32), grad_logits, precision=PRECISE_ARITHMETIC)
+    grad_middle, gain_two_part = norm_back(middle, gain_two, scale_two, grad_normed)
+    grad_middle = grad_middle + upstream
+    grad_branch = (RESIDUAL_SCALE * grad_middle).astype(BF16)
+
+    out_grad_part = jnp.einsum("tq,td->qd", attended, grad_branch, preferred_element_type=F32)
+    grad_attended = jnp.einsum("td,qd->tq", grad_branch, out_full, preferred_element_type=F32).astype(BF16)
+    grad_heads = grad_attended.reshape(T, KEY_VALUE_HEADS, group, HEAD_WIDTH)
+    row_delta = jnp.sum(grad_heads.astype(F32) * attended.reshape(grad_heads.shape).astype(F32), axis=-1)
+    row_delta = jnp.transpose(row_delta, (1, 2, 0))[..., None]
+    grad_values = jnp.einsum("kgqt,qkgd->tkd", probs_half, grad_heads, preferred_element_type=F32)
+    grad_probs = jnp.einsum("qkgd,tkd->kgqt", grad_heads, values, preferred_element_type=F32)
+    grad_scores = (probs * (grad_probs - row_delta) * ATTN_SCALE).astype(BF16)
+    grad_queries = jnp.einsum("kgqt,tkd->qkgd", grad_scores, keys, preferred_element_type=F32)
+    grad_keys = jnp.einsum("kgqt,qkgd->tkd", grad_scores, queries, preferred_element_type=F32)
+    grad_joined = jnp.concatenate(
+        [
+            rotate_back(grad_queries.reshape(T, QUERY_HEADS, HEAD_WIDTH), cosine, sine).reshape(T, q_width),
+            rotate_back(grad_keys, cosine, sine).reshape(T, k_width),
+            grad_values.reshape(T, k_width),
+        ],
+        axis=-1,
+    ).astype(BF16)
+    qkv_part = jnp.einsum("td,tm->dm", normed_one, grad_joined, preferred_element_type=F32)
+    grad_normed_one = jnp.einsum("tm,dm->td", grad_joined, qkv_full, preferred_element_type=F32)
+    grad_inputs, gain_one_part = norm_back(inputs, gain_one, scale_one, grad_normed_one)
+    input_grad = (grad_inputs + grad_middle).astype(BF16)
+
+    out_small_part = jnp.concatenate(
+        [out_grad_part, router_part, gain_one_part[:, None], gain_two_part[:, None], jnp.zeros((D, 86), F32)], axis=1
+    ).astype(BF16)
+    qkv_grad, out_small_grad, combined = scatter([qkv_part.astype(BF16), out_small_part, out_part], SCATTER_LAST, 3)
+    layer_output = (middle + RESIDUAL_SCALE * combined).astype(BF16)
+
+    part = lambda c0, c1: dw[:, :, c0:c1]
+    gu_w = part(0, 1024).reshape(8, 4, own_rows, 1024)
+    gu_f = jnp.transpose(part(1024, 1280).reshape(8, 4, own_rows, 2, 128), (0, 2, 3, 1, 4)).reshape(8, 1, own_rows, 1024)
+    gate_up_grad = jnp.transpose(jnp.concatenate([gu_w, gu_f], axis=1).reshape(E, own_rows, 1024), (1, 0, 2)).astype(F32)
+    dp_w = part(1280, 1792).reshape(8, 4, own_rows, F)
+    dp_f = jnp.transpose(part(1792, 1920).reshape(8, 4, own_rows, 128), (0, 2, 1, 3)).reshape(8, 1, own_rows, F)
+    down_grad = jnp.transpose(jnp.concatenate([dp_w, dp_f], axis=1).reshape(E, own_rows, F), (1, 0, 2)).astype(F32)
+    return (
+        layer_output,
+        input_grad,
+        out_small_grad[:, D + E],
+        qkv_grad,
+        out_small_grad[:, :D],
+        out_small_grad[:, D + E + 1],
+        out_small_grad[:, D : D + E],
+        gate_up_grad,
+        down_grad,
+    )
+
+
 def solution(mesh):
-    placed = (
-        P("fsdp", None),
-        P("fsdp", None),
-        P("fsdp"),
-        P("fsdp", None),
-        P("fsdp"),
-        P("fsdp", None),
-        P("fsdp", None),
-        P("fsdp"),
-        P("fsdp", None),
-        P("fsdp", None, None),
-        P("fsdp", None, None),
-    )
+    rows, flat, cube = P("fsdp", None), P("fsdp"), P("fsdp", None, None)
     return jax.shard_map(
-        on_device,
+        fast if mesh.shape["fsdp"] == 32 else on_device,
         mesh=mesh,
-        in_specs=placed,
-        out_specs=(
-            P("fsdp", None),
-            P("fsdp", None),
-            P("fsdp"),
-            P("fsdp", None),
-            P("fsdp", None),
-            P("fsdp"),
-            P("fsdp", None),
-            P("fsdp", None, None),
-            P("fsdp", None, None),
-        ),
+        in_specs=(rows, rows, flat, rows, flat, rows, rows, flat, rows, cube, cube),
+        out_specs=(rows, rows, flat, rows, rows, flat, rows, cube, cube),
         check_vma=False,
     )

time: 2440 us -> 669 us (0.27)
  waiting for transfers between devices: 1010 us -> 0.01 us
  blocking collectives: 828 us -> 0 us
  Pallas kernels: 0 us -> 508 us
  local copies, waits for them, and re-layouts: 324 us -> 72.4 us
  matrix products: 183 us -> 36.8 us
  other arithmetic: 44.3 us -> 18.2 us
    all_to_all x5 -> x3, waiting for transfers between devices: 1010 us -> 0.01 us  [the longest x1 0.01 us: fast(): lax.all_to_all(pack, 'fsdp', split_axis=0, concat_axis=0, tiled=True)]
    pallas_call x0 -> x5, Pallas kernels: none -> 508 us  [the longest x2 241 us: gather(): pl.pallas_call(functools.partial(gather_kernel, parts, k), out_shape=[jax...]
    all_gather x1 -> x0, blocking collectives: 385 us -> none  [on_device(): lax.all_gather(router, 'fsdp', axis=0, tiled=True)]
    all_to_all x1 -> x0, blocking collectives: 235 us -> none  [on_device(): lax.all_to_all(send_grad, 'fsdp', split_axis=0, concat_axis=0, tiled=True)]
    unnamed x2 -> x0, blocking collectives: 208 us -> none
    dot_general x26 -> x16, matrix products: 181 us -> 36.8 us  [the longest x1 6.96 us: fast(): jnp.einsum('tm,dm->td', grad_joined, qkv_full, preferred_element_type=F32)]
    unnamed x123 -> x71, local copies, waits for them, and re-layouts: 115 us -> 21.7 us
    all_to_all x3 -> x0, local copies, waits for them, and re-layouts: 54.6 us -> none  [the longest x2 29.9 us: on_device(): lax.all_to_all(owned_grads, 'fsdp', split_axis=0, concat_axis=2, tiled=True)]
  transfers between devices with their start and end apart: 10 -> 3, of which waited for: 4 -> 0; matrix products, arithmetic and copies ran while one was open for 15% -> 11% of each run, Pallas kernels for 0% -> 60%
where the time goes in v1:
time: 669 us; the launch traced here: 661 us
  Pallas kernels  508 us (76%)
  local copies, waits for them, and re-layouts  72.4 us (11%)
  matrix products  36.8 us (6%)
  starting transfers between devices  24.3 us (4%)
  other arithmetic  18.2 us (3%)
    pallas_call x2, Pallas kernels, gather(): pl.pallas_call(functools.partial(gather_kernel, parts, k), out_shape=[jax...  241 us
    pallas_call x2, Pallas kernels, scatter(): pl.pallas_call(functools.partial(scatter_kernel, parts, k, rows), out_sha...  217 us
    pallas_call x1, Pallas kernels, experts(): pl.pallas_call(expert_kernel, grid=(STEPS,), in_specs=[pl.BlockSpec(memor...  49.9 us
    unnamed x71, local copies, waits for them, and re-layouts  21.7 us
    all_to_all x1, starting transfers between devices, fast(): lax.all_to_all(dw.reshape(n, own_rows, 1920), 'fsdp', split_axis=0, conca...  14.1 us
  transfers between devices with their start and end apart: 3, of which 0 were waited for; matrix products, arithmetic and copies ran while one was open for 11% of the time, Pallas kernels for 60%

profile of v1, /device:TPU:0, one launch (start us, length us, event | category | flops | bytes accessed | tf_op | source)
XLA Modules:
  0.0 661.0 jit_solution(18177031422005830836)
XLA Ops:
  0.6 4.3 copy.143
  5.3 0.9 slice.122
  6.2 0.6 copy-done.8
  6.8 0.6 copy.145
  7.4 1.3 slice.123
  8.7 0.7 copy.140
  9.5 1.3 copy.142
  10.9 2.6 reshape_squeeze.6
  13.5 2.7 copy.144
  16.2 3.1 reshape.244
  19.3 0.8 reshape_squeeze.7
  20.2 1.1 copy.146
  21.2 0.6 broadcast_in_dim.26
  21.8 1.7 concatenate.44.refs_1_
  23.5 62.5 %shard_map.178 = (bf16[1536,2560]{1,0:T(8,128)(2,1)}, bf16[1536,1664]{1,0:T(8,128)(2,1)}, s32[256,128]{1,0:T(8,128)}) custom-call(bf16[48,2560]{1,0:T(8,128)(2,1)} %refs_0_.1, bf16[48,1664]{1,0:T(8,128)(2,1)} %concatenate.44.refs_1_, s32[8,128]{1,0:T(8,128)} %bitcast.174), custom_call_target="tpu_custom_call" | custom-call | tf_op jit(solution)/shard_map/pallas_call | solution.py:553
  86.0 4.4 pad_maximum_fusion
  90.5 5.4 all-to-all-start
  96.0 1.7 convert_reduce_fusion
  97.7 0.6 multiply_multiply_fusion
  98.3 4.5 fusion.34
  103.0 7.8 %copy.153 = bf16[1536,1664]{0,1:T(8,128)(2,1)} copy(bf16[1536,1664]{1,0:T(8,128)(2,1)} %get-tuple-element.25) | data formatting | bytes 10223616 | tf_op jit(solution)/shard_map/pallas_call | solution.py:553
  111.9 0.7 eq.65
  112.6 0.9 slice_bitcast_fusion
  113.5 0.7 pad.4.router_ref
  115.9 0.7 copy-done.6
  116.6 3.3 multiply_reduce_fusion.3
  119.9 0.6 multiply_multiply_fusion.1
  120.8 0.9 multiply_convert_fusion.1.refs_0_
  121.7 178.5 %shard_map.179 = (bf16[4096,1536]{1,0:T(8,128)(2,1)}, bf16[4096,1536]{1,0:T(8,128)(2,1)}) custom-call(bf16[128,1536]{1,0:T(8,128)(2,1)} %multiply_convert_fusion.1.refs_0_, bf16[128,1536]{1,0:T(8,128)(2,1)} %refs_1_.1), custom_call_target="tpu_custom_call" | custom-call | tf_op jit(solution)/shard_map/pallas_call | solution.py:553
  300.2 1.2 fusion.19.pick_ref
  301.3 49.9 %shard_map.180 = (bf16[4096,1536]{1,0:T(8,128)(2,1)}, bf16[4096,1536]{1,0:T(8,128)(2,1)}, f32[32,8,128]{2,1,0:T(8,128)}, bf16[1536,1920]{1,0:T(8,128)(2,1)}) custom-call(s32[2]{0:T(128)} %copy-done.29, bf16[4096,1536]{1,0:T(8,128)(2,1)} %get-tuple-element.28.t_ref, bf16[4096,1536]{1,0:T(8,128)(2,1)} %get-tuple-element.29.c_ref, ...), custom_call_target="tpu_custom_call" | custom-call | flops 22000001024 | bytes 62000000 | tf_op jit(solution)/shard_map/pallas_call | solution.py:790
  351.3 4.8 all-to-all-start.1
  356.1 66.1 %shard_map.181 = f32[128,1536]{1,0:T(8,128)} custom-call(bf16[4096,1536]{1,0:T(8,128)(2,1)} %get-tuple-element.33.refs_0_), custom_call_target="tpu_custom_call" | custom-call | tf_op jit(solution)/shard_map/pallas_call | solution.py:701
  422.3 14.1 %all-to-all-start.2 = ((bf16[32,48,1920]{2,1,0:T(8,128)(2,1)}), bf16[32,48,1920]{2,1,0:T(8,128)(2,1)}, u32[]{:S(2)}, u32[]{:S(2)}) async-start(bf16[32,48,1920]{2,1,0:T(8,128)(2,1)} %bitcast.144), calls=%async_computation.2 | async-start | bytes 11796480 | tf_op jit(solution)/shard_map/all_to_all | solution.py:888
  436.4 1.1 fusion.61
  438.0 0.9 copy.160
  439.0 2.0 multiply_reduce_fusion
  440.9 1.3 convert_add_fusion
  442.2 0.9 copy-done.3
  443.1 4.8 fusion.10
  447.9 1.2 copy.155
  449.1 1.2 multiply_reduce_fusion.1
  450.8 1.5 convolution_bitcast_fusion.1
  453.4 7.0 %fusion.29 = (f32[128]{0:T(128)S(1)}, bf16[1536]{0:T(1024)(128)(2,1)S(1)}, f32[128,1536]{1,0:T(8,128)}) fusion(bf16[128,1536]{1,0:T(8,128)(2,1)S(1)} %copy-done.2, f32[1536]{0:T(1024)S(1)} %get-tuple-element.87, f32[128]{0:T(128)S(1)} %copy-done.23, bf16[1536,2560]{1,0:T(8,128)(2,1)} %get-tuple-element.27, bf16[128,512]{0,1:T(8,128)(2,1)S(1)} %bitcast.165, ...), kind=kOutput, calls=%fused_computation.45 | convolution fusion | flops 1009973632 | bytes 9709568 | tf_op jit(solution)/shard_map/tm,dm->td/dot_general | solution.py:919
  460.9 3.6 convolution_convert_fusion.1
  464.5 9.1 %concatenate.54.refs_1_ = bf16[1536,1664]{1,0:T(8,128)(2,1)} concatenate(bf16[1536,1536]{1,0:T(8,128)(2,1)} %convolution_convert_fusion.1, bf16[1536,40]{1,0:T(8,128)(2,1)} %copy.160, bf16[1536,1]{1,0:T(8,128)(2,1)S(1)} %broadcast_in_dim.33, bf16[1536,1]{1,0:T(8,128)(2,1)S(1)} %broadcast_in_dim.34, bf16[1536,86]{1,0:T(8,128)(2,1)S(1)} %broadcast_in_dim.32), dimensions={1} | concatenate | bytes 10223616 | tf_op jit(solution)/shard_map/concatenate | solution.py:923
  473.6 6.6 convolution_convert_fusion.refs_0_
  480.2 150.5 %shard_map.182 = (f32[48,2560]{1,0:T(8,128)}, f32[48,1664]{1,0:T(8,128)}, f32[128,1536]{1,0:T(8,128)}) custom-call(bf16[1536,2560]{1,0:T(8,128)(2,1)} %convolution_convert_fusion.refs_0_, bf16[1536,1664]{1,0:T(8,128)(2,1)} %concatenate.54.refs_1_, bf16[4096,1536]{1,0:T(8,128)(2,1)} %get-tuple-element.36.refs_2_), custom_call_target="tpu_custom_call" | custom-call | tf_op jit(solution)/shard_map/pallas_call | solution.py:701
  630.7 1.7 slice.114
  632.4 0.7 slice.116
  633.1 0.7 copy.167
  633.8 1.5 slice_reduce_fusion
  635.3 2.4 fusion.28
  637.8 1.0 slice.142
  639.1 1.5 slice.141
  640.8 0.7 convert_bitcast_fusion.1
  641.5 4.2 copy.169
  645.7 1.2 slice.140
  647.1 0.6 copy.163
  647.7 0.6 reshape.261
  648.3 2.2 slice.139
  650.8 1.2 convert_bitcast_fusion
  652.1 7.8 %copy.168 = f32[48,40,1024]{2,1,0:T(8,128)} copy(f32[48,40,1024]{2,0,1:T(8,128)S(1)} %convert_bitcast_fusion) | data formatting | bytes 15728640
  659.9 0.8 copy.183
  (113 shorter events, 7.2 us)
Async XLA Ops:
  4.9 1.8 copy-start.8
  6.8 2.0 copy-start.24
  6.8 2.7 copy-start.30
  90.5 5.4 copy-start.2
  90.5 210.9 %all-to-all-start = ((bf16[32,48,1920]{2,1,0:T(8,128)(2,1)}), bf16[32,48,1920]{2,1,0:T(8,128)(2,1)}, u32[]{:S(2)}, u32[]{:S(2)}) async-start(bf16[32,48,1920]{2,1,0:T(8,128)(2,1)} %pad_maximum_fusion), calls=%async_computation | async-start | bytes 11796480 | tf_op jit(solution)/shard_map/all_to_all | solution.py:851
  98.3 4.5 copy-start.22
  103.0 8.1 %copy-start.27 = (s32[128]{0:T(128)S(1)}, s32[128]{0:T(128)}, u32[]{:S(2)}) copy-start(s32[128]{0:T(128)} %param.13) | copy-start | bytes 1540
  103.0 8.6 %copy-start.20 = (s32[256,128]{1,0:T(8,128)S(1)}, s32[256,128]{1,0:T(8,128)}, u32[]{:S(2)}) copy-start(s32[256,128]{1,0:T(8,128)} %get-tuple-element.30) | copy-start | bytes 393220
  111.5 4.4 copy-start.10
  111.6 3.6 copy-start.29
  114.5 5.4 copy-start.16
  114.5 5.4 copy-start.18
  114.6 5.2 copy-start.13
  114.7 5.2 copy-start.14
  115.8 0.7 copy-start.6
  116.6 183.6 %copy-start.21 = (f32[2048]{0:T(1024)S(1)}, f32[2048]{0:T(1024)}, u32[]{:S(2)}) copy-start(f32[2048]{0:T(1024)} %eq.65) | copy-start | bytes 24580
  119.9 0.9 copy-start
  120.5 180.9 %copy-start.25 = (f32[128]{0:T(128)}, f32[128]{0:T(128)S(1)}, u32[]{:S(2)}) copy-start(f32[128]{0:T(128)S(1)} %get-tuple-element.109) | copy-start | bytes 1540
  351.3 71.0 %all-to-all-start.1 = ((f32[32,8,128]{2,1,0:T(8,128)}), f32[32,8,128]{2,1,0:T(8,128)S(1)}, u32[]{:S(2)}, u32[]{:S(2)}) async-start(f32[32,8,128]{2,1,0:T(8,128)} %get-tuple-element.35), calls=%async_computation.1 | async-start | bytes 262144 | tf_op jit(solution)/shard_map/all_to_all | solution.py:884
  422.3 14.2 %copy-start.5 = (bf16[128,1536]{1,0:T(8,128)(2,1)S(1)}, bf16[128,1536]{1,0:T(8,128)(2,1)}, u32[]{:S(2)}) copy-start(bf16[128,1536]{1,0:T(8,128)(2,1)} %multiply_convert_fusion.1.refs_0_) | copy-start | bytes 1179652
  422.3 16.7 %copy-start.1 = (f32[128,1536]{1,0:T(8,128)S(1)}, f32[128,1536]{1,0:T(8,128)}, u32[]{:S(2)}) copy-start(f32[128,1536]{1,0:T(8,128)} %copy-done) | copy-start | bytes 2359300
  422.3 16.7 %copy-start.26 = (f32[128]{0:T(128)S(1)}, f32[128]{0:T(128)}, u32[]{:S(2)}) copy-start(f32[128]{0:T(128)} %copy-done.25) | copy-start | bytes 1540
  422.3 215.5 %all-to-all-start.2 = ((bf16[32,48,1920]{2,1,0:T(8,128)(2,1)}), bf16[32,48,1920]{2,1,0:T(8,128)(2,1)}, u32[]{:S(2)}, u32[]{:S(2)}) async-start(bf16[32,48,1920]{2,1,0:T(8,128)(2,1)} %bitcast.144), calls=%async_computation.2 | async-start | bytes 11796480 | tf_op jit(solution)/shard_map/all_to_all | solution.py:888
  436.4 4.5 copy-start.31
  442.2 0.9 copy-start.3
  443.1 7.2 %copy-start.11 = (bf16[128,512]{0,1:T(8,128)(2,1)S(1)}, bf16[128,512]{0,1:T(8,128)(2,1)}, u32[]{:S(2)}) copy-start(bf16[128,512]{0,1:T(8,128)(2,1)} %copy-done.10) | copy-start | bytes 393220
  449.1 3.3 copy-start.17
  449.1 3.3 copy-start.19
  450.8 2.5 copy-start.23
  452.9 7.5 %copy-start.9 = (bf16[128,24,64]{0,2,1:T(8,128)(2,1)}, bf16[128,24,64]{0,2,1:T(8,128)(2,1)S(1)}, u32[]{:S(2)}) copy-start(bf16[128,24,64]{0,2,1:T(8,128)(2,1)S(1)} %pad_maximum_fusion.5) | copy-start | bytes 1179652
  453.4 7.5 %copy-start.4 = (f32[128,1536]{1,0:T(8,128)S(1)}, f32[128,1536]{1,0:T(8,128)}, u32[]{:S(2)}) copy-start(f32[128,1536]{1,0:T(8,128)} %copy-done.3) | copy-start | bytes 2359300
  453.4 7.5 %copy-start.7 = (bf16[8,64,3,128]{3,1,2,0:T(8,128)(2,1)S(1)}, bf16[8,64,3,128]{3,1,2,0:T(8,128)(2,1)}, u32[]{:S(2)}) copy-start(bf16[8,64,3,128]{3,1,2,0:T(8,128)(2,1)} %copy-done.6) | copy-start | bytes 1179652
  480.2 155.1 %copy-start.12 = (f32[128,1536]{1,0:T(8,128)S(1)}, f32[128,1536]{1,0:T(8,128)}, u32[]{:S(2)}) copy-start(f32[128,1536]{1,0:T(8,128)} %get-tuple-element.117) | copy-start | bytes 2359300
  480.2 155.1 %copy-start.28 = (f32[128]{0:T(128)S(1)}, f32[128]{0:T(128)}, u32[]{:S(2)}) copy-start(f32[128]{0:T(128)} %get-tuple-element.106) | copy-start | bytes 1540
  652.1 7.8 %copy-start.15 = (f32[48,2560]{1,0:T(8,128)S(1)}, f32[48,2560]{1,0:T(8,128)}, u32[]{:S(2)}) copy-start(f32[48,2560]{1,0:T(8,128)} %get-tuple-element.132) | copy-start | bytes 1474564

commit v2 on v1

--- a/solution.py
+++ b/solution.py
@@ -414,6 +414,8 @@
 
 
 MESH = pl.DeviceIdType.MESH
+DEVICES = 32
+TURNS = tuple(sorted(range(1, DEVICES), key=lambda k: (k % 8 * 5 % 8, k)))
 
 def place():
     me = lax.axis_index("fsdp")
@@ -441,13 +443,64 @@
         pl.semaphore_signal(barrier, inc=1, device_id=(down,), device_id_type=MESH)
     pl.semaphore_wait(barrier, len(near) + jnp.where(z < 3, 1, 0) + jnp.where(z > 0, 1, 0))
 
-def gather_kernel(parts, count, *refs):
-    shards, outs = refs[:count], refs[count:2 * count]
-    (local_sem, zs, zs2, zr, fs, fr, s1s, s1r, s2s, s2r, cs, cr) = refs[2 * count:]
+def greet_all():
+    me = lax.axis_index("fsdp")
+    barrier = pltpu.get_barrier_semaphore()
+    for k in range(1, DEVICES):
+        pl.semaphore_signal(barrier, inc=1, device_id=(lax.rem(me + k, DEVICES),), device_id_type=MESH)
+    pl.semaphore_wait(barrier, DEVICES - 1)
+
+def rc(src, dst, ss, rs, to):
+    return pltpu.make_async_remote_copy(src_ref=src, dst_ref=dst, send_sem=ss, recv_sem=rs, device_id=(to,), device_id_type=MESH)
+
+class Direct:
+    def __init__(self, pieces, refs, sems):
+        self.pieces, self.refs, (self.ss, self.rs, self.ls) = pieces, refs, sems
+        self.me = lax.axis_index("fsdp")
+
+    def own(self):
+        self.local = [pltpu.make_async_copy(a, b, self.ls.at[i]) for i, (a, b) in enumerate(self.pieces(self.me, self.me, self.refs))]
+        for l in self.local:
+            l.start()
+
+    def start(self, turns):
+        for k in turns:
+            to = lax.rem(self.me + k, DEVICES)
+            for i, (a, b) in enumerate(self.pieces(self.me, to, self.refs)):
+                rc(a, b, self.ss.at[k, i], self.rs.at[k, i], to).start()
+
+    def finish(self):
+        for k in TURNS:
+            src = lax.rem(self.me + DEVICES - k, DEVICES)
+            for i, (a, b) in enumerate(self.pieces(src, self.me, self.refs)):
+                rc(a, b, self.ss.at[k, i], self.rs.at[k, i], src).wait_recv()
+        for k in TURNS:
+            to = lax.rem(self.me + k, DEVICES)
+            for i, (a, b) in enumerate(self.pieces(self.me, to, self.refs)):
+                rc(a, b, self.ss.at[k, i], self.rs.at[k, i], to).wait_send()
+        for l in self.local:
+            l.wait()
+
+    @staticmethod
+    def scratch(count):
+        dma = pltpu.SemaphoreType.DMA
+        return [dma((DEVICES, count)), dma((DEVICES, count)), dma((count,))]
+
+def gather_kernel(parts, count, extra, *refs):
+    pieces, n_in, n_out, batches = extra or (None, 0, 0, ())
+    shards, refs = refs[:count], refs[count:]
+    extra_in, refs = refs[:n_in], refs[n_in:]
+    outs, refs = refs[:count], refs[count:]
+    extra_out, refs = refs[:n_out], refs[n_out:]
+    (local_sem, zs, zs2, zr, fs, fr, s1s, s1r, s2s, s2r, cs, cr), sems = refs[:12], refs[12:]
     z, y, x, c = place()
     sib, xn, yn = dev(z, y, x, 1 - c), dev(z, y, 1 - x, c), dev(z, 1 - y, x, c)
     up, down = dev(z + 1, y, x, c), dev(z - 1, y, x, c)
-    greet(z, (sib, xn, yn), up, down)
+    if extra:
+        greet_all()
+        direct = Direct(pieces, extra_in + extra_out, sems)
+    else:
+        greet(z, (sib, xn, yn), up, down)
 
     def at(p, d):
         a, c0, w, _ = parts[p]
@@ -458,26 +511,18 @@
         a, c0, w, _ = parts[p]
         return shards[a].at[:, pl.ds(c0, w)]
 
-    def rc(src, dst, ss, rs, to):
-        return pltpu.make_async_remote_copy(src_ref=src, dst_ref=dst, send_sem=ss, recv_sem=rs, device_id=(to,), device_id_type=MESH)
-
     me = dev(z, y, x, c)
-    locals_ = []
-    for a in range(count):
-        rows = shards[a].shape[0]
-        l = pltpu.make_async_copy(shards[a], outs[a].at[pl.ds(pl.multiple_of(me * rows, rows), rows)], local_sem.at[a])
-        l.start(); locals_.append(l)
     P = len(parts)
     zq = [z_order(z, q) for q in range(4)]
     sends = []
     def go(copy):
-        copy.start(); sends.append(copy)
+        copy.start()
+        sends.append(copy)
 
     def stage1(q):
         for p in range(P):
             first, second = (xn, yn) if parts[p][3] == 0 else (yn, xn)
-            d = dev(zq[q], y, x, c)
-            here = at(p, d)
+            here = at(p, dev(zq[q], y, x, c))
             if q == 0:
                 src = own(p)
                 @pl.when(z < 3)
@@ -499,40 +544,46 @@
             go(rc(src, here, s1s.at[q, p], s1r.at[q, p], second))
             go(rc(src, here, cs.at[0, q, p], cr.at[0, q, p], sib))
 
-    def near(q, p):
-        return dev(zq[q], y, 1 - x, c) if parts[p][3] == 0 else dev(zq[q], 1 - y, x, c)
-    def side(q, p):
-        return dev(zq[q], 1 - y, x, c) if parts[p][3] == 0 else dev(zq[q], y, 1 - x, c)
+    def spot(p, q, k, core):
+        flip_x, flip_y = ((0, 0), (1, 0), (0, 1), (1, 1))[k] if parts[p][3] == 0 else ((0, 0), (0, 1), (1, 0), (1, 1))[k]
+        return at(p, dev(zq[q], 1 - y if flip_y else y, 1 - x if flip_x else x, core))
 
     def stage2(q):
         for p in range(P):
-            first, second = (xn, yn) if parts[p][3] == 0 else (yn, xn)
-            there = at(p, near(q, p))
-            rc(there, there, fs.at[q, p], fr.at[q, p], first).wait_recv()
+            second = yn if parts[p][3] == 0 else xn
+            there = spot(p, q, 1, c)
+            rc(there, there, fs.at[q, p], fr.at[q, p], second).wait_recv()
             go(rc(there, there, s2s.at[q, p], s2r.at[q, p], second))
             go(rc(there, there, cs.at[1, q, p], cr.at[1, q, p], sib))
 
     def stage3(q):
-        for p in range(P):
-            there = at(p, side(q, p))
-            rc(there, there, s1s.at[q, p], s1r.at[q, p], sib).wait_recv()
-            go(rc(there, there, cs.at[2, q, p], cr.at[2, q, p], sib))
-        for p in range(P):
-            there = at(p, dev(zq[q], 1 - y, 1 - x, c))
-            rc(there, there, s2s.at[q, p], s2r.at[q, p], sib).wait_recv()
-            go(rc(there, there, cs.at[3, q, p], cr.at[3, q, p], sib))
-
-    stage1(0); stage1(1); stage2(0); stage1(2); stage2(1); stage3(0); stage1(3); stage2(2); stage3(1); stage2(3); stage3(2); stage3(3)
+        for k, (ss, rs) in ((2, (s1s, s1r)), (3, (s2s, s2r))):
+            for p in range(P):
+                there = spot(p, q, k, c)
+                rc(there, there, ss.at[q, p], rs.at[q, p], sib).wait_recv()
+                go(rc(there, there, cs.at[k, q, p], cr.at[k, q, p], sib))
+
+    locals_ = []
+    for step, (f, q) in enumerate(((1, 0), (1, 1), (2, 0), (1, 2), (2, 1), (3, 0), (1, 3), (2, 2), (3, 1), (2, 3), (3, 2), (3, 3))):
+        (stage1, stage2, stage3)[f - 1](q)
+        if step == 0:
+            for a in range(count):
+                rows = shards[a].shape[0]
+                l = pltpu.make_async_copy(shards[a], outs[a].at[pl.ds(pl.multiple_of(me * rows, rows), rows)], local_sem.at[a])
+                l.start()
+                locals_.append(l)
+            if extra:
+                direct.own()
+        if extra and step < len(batches):
+            lo = sum(batches[:step])
+            direct.start(TURNS[lo:lo + batches[step]])
     for q in range(4):
-        for p in range(P):
-            for k, where in enumerate((dev(zq[q], y, x, 1 - c), None, None, None)):
-                if k == 0: d = dev(zq[q], y, x, 1 - c)
-                elif k == 1: d = near(q, p) + 1 - 2 * c
-                elif k == 2: d = side(q, p) + 1 - 2 * c
-                else: d = dev(zq[q], 1 - y, 1 - x, 1 - c)
-                there = at(p, d)
+        for k in range(4):
+            for p in range(P):
+                there = spot(p, q, k, 1 - c)
                 rc(there, there, cs.at[k, q, p], cr.at[k, q, p], sib).wait_recv()
-    for copy in sends: copy.wait_send()
+    for copy in sends:
+        copy.wait_send()
     for p in range(P):
         here = at(p, me)
         @pl.when(z < 3)
@@ -545,38 +596,51 @@
             @pl.when(((zq[q] < z) & (z < 3)) | ((zq[q] > z) & (z > 0)))
             def _():
                 rc(here, here, zs.at[q, p], zr.at[zq[q], p], up).wait_send()
-    for l in locals_: l.wait()
-
-def gather(arrays, parts, collective_id):
-    n = 32; k = len(arrays); P = len(parts)
+    for l in locals_:
+        l.wait()
+    if extra:
+        direct.finish()
+
+def gather(arrays, parts, collective_id, extra=None, extra_in=(), extra_out=()):
+    k, P = len(arrays), len(parts)
     dma = pltpu.SemaphoreType.DMA
+    if extra:
+        pieces, count, batches = extra
+        extra = (pieces, len(extra_in), len(extra_out), batches)
     return pl.pallas_call(
-        functools.partial(gather_kernel, parts, k),
-        out_shape=[jax.ShapeDtypeStruct((n * a.shape[0],) + a.shape[1:], a.dtype) for a in arrays],
-        in_specs=[pl.BlockSpec(memory_space=pl.ANY)] * k,
-        out_specs=[pl.BlockSpec(memory_space=pl.ANY)] * k,
-        scratch_shapes=[dma((k,)), dma((4, P)), dma((P,)), dma((4, P)), dma((4, P)), dma((4, P)), dma((4, P)), dma((4, P)), dma((4, P)), dma((4, P)), dma((4, 4, P)), dma((4, 4, P))],
+        functools.partial(gather_kernel, parts, k, extra),
+        out_shape=[jax.ShapeDtypeStruct((DEVICES * a.shape[0],) + a.shape[1:], a.dtype) for a in arrays] + list(extra_out),
+        in_specs=[pl.BlockSpec(memory_space=pl.ANY)] * (k + len(extra_in)),
+        out_specs=[pl.BlockSpec(memory_space=pl.ANY)] * (k + len(extra_out)),
+        scratch_shapes=[dma((k,)), dma((4, P)), dma((P,))] + [dma((4, P))] * 7 + [dma((4, 4, P))] * 2 + (Direct.scratch(count) if extra else []),
         compiler_params=pltpu.CompilerParams(collective_id=collective_id, has_side_effects=True),
-    )(*arrays)
-
-
-def scatter_kernel(parts, count, rows, *refs):
-    fulls, outs = refs[:count], refs[count:2 * count]
-    refs = refs[2 * count:]
+    )(*arrays, *extra_in)
+
+
+def scatter_kernel(parts, count, rows, extra, *refs):
+    pieces, n_in, n_out, batches = extra or (None, 0, 0, ())
+    fulls, refs = refs[:count], refs[count:]
+    extra_in, refs = refs[:n_in], refs[n_in:]
+    outs, refs = refs[:count], refs[count:]
+    extra_out, refs = refs[:n_out], refs[n_out:]
     held, r0, r1, r2, r3 = (refs[i * count:(i + 1) * count] for i in range(5))
-    (ls, s0, e0, s1, e1, s2, e2, s3, e3) = refs[5 * count:]
+    refs = refs[5 * count:]
+    (ls, s0, e0, s1, e1, s2, e2, s3, e3), sems = refs[:9], refs[9:]
     z, y, x, c = place()
     sib, xn, yn = dev(z, y, x, 1 - c), dev(z, y, 1 - x, c), dev(z, 1 - y, x, c)
     up, down = dev(z + 1, y, x, c), dev(z - 1, y, x, c)
-    greet(z, (sib, xn, yn), up, down)
+    if extra:
+        greet_all()
+        direct = Direct(pieces, extra_in + extra_out, sems)
+    else:
+        greet(z, (sib, xn, yn), up, down)
 
     P = len(parts)
     zq = [z_order(z, q) for q in range(4)]
     sends = []
-    def rc(src, dst, ss, rs, to):
-        return pltpu.make_async_remote_copy(src_ref=src, dst_ref=dst, send_sem=ss, recv_sem=rs, device_id=(to,), device_id_type=MESH)
     def go(copy):
-        copy.start(); sends.append(copy)
+        copy.start()
+        sends.append(copy)
     def cut(p):
         return pl.ds(parts[p][1], parts[p][2])
     def spot(p, k):
@@ -596,19 +660,28 @@
         for k in range(4):
             for p in range(P):
                 a = parts[p][0]
-                go(rc(source(p, q, k, 1 - c), r0[a].at[slot(q, *spot(p, k)), :, cut(p)], s0.at[q, k, p], e0.at[q, k, p], sib))
-                l = pltpu.make_async_copy(source(p, q, k, c), held[a].at[slot(q, *spot(p, k)), :, cut(p)], ls.at[q, k, p])
-                l.start(); loads[q, k, p] = l
-
-    def add(p, dst, s_dst, src, s_src, more=None, out=None):
+                s = slot(q, *spot(p, k))
+                go(rc(source(p, q, k, 1 - c), r0[a].at[s, :, cut(p)], s0.at[q, k, p], e0.at[q, k, p], sib))
+                l = pltpu.make_async_copy(source(p, q, k, c), held[a].at[s, :, cut(p)], ls.at[q, k, p])
+                l.start()
+                loads[q, k, p] = l
+    if extra:
+        direct.own()
+
+    STEP = 16
+    def chunks(a, body):
+        def one(i, carry):
+            body(pl.ds(pl.multiple_of(i * STEP, STEP), STEP))
+            return carry
+        lax.fori_loop(0, rows[a] // STEP, one, 0)
+
+    def add(p, s, src, s_src):
         a, c0, w, _ = parts[p]
-        step = 16
-        def body(i, carry):
-            r = pl.ds(pl.multiple_of(i * step, step), step)
-            v = dst[s_dst, r, c0:c0 + w].astype(jnp.float32) + src[s_src, r, c0:c0 + w].astype(jnp.float32)
-            dst[s_dst, r, c0:c0 + w] = v.astype(dst.dtype)
-            return carry
-        lax.fori_loop(0, rows[a] // step, body, 0)
+        dst = held[a]
+        def body(r):
+            v = dst[s, r, c0:c0 + w].astype(jnp.float32) + src[s_src, r, c0:c0 + w].astype(jnp.float32)
+            dst[s, r, c0:c0 + w] = v.astype(dst.dtype)
+        chunks(a, body)
 
     def stage1(q):
         for k in range(4):
@@ -619,7 +692,7 @@
                 here = held[a].at[s, :, cut(p)]
                 rc(here, r0[a].at[s, :, cut(p)], s0.at[q, k, p], e0.at[q, k, p], sib).wait_recv()
                 loads[q, k, p].wait()
-                add(p, held[a], s, r0[a], s)
+                add(p, s, r0[a], s)
                 if k < 2:
                     go(rc(here, r1[a].at[q * 2 + k, :, cut(p)], s1.at[q, k, p], e1.at[q, k, p], first))
 
@@ -631,23 +704,23 @@
                 s = slot(q, *spot(p, k + 2))
                 here = held[a].at[s, :, cut(p)]
                 rc(here, r1[a].at[q * 2 + k, :, cut(p)], s1.at[q, k, p], e1.at[q, k, p], sib).wait_recv()
-                add(p, held[a], s, r1[a], q * 2 + k)
+                add(p, s, r1[a], q * 2 + k)
                 if k == 0:
                     go(rc(here, r2[a].at[q, :, cut(p)], s2.at[q, p], e2.at[q, p], second))
 
     def stage3(q):
         for p in range(P):
-            a = parts[p][0]
+            a, c0, w, _ = parts[p]
             s = slot(q, y, x)
             here = held[a].at[s, :, cut(p)]
             rc(here, r2[a].at[q, :, cut(p)], s2.at[q, p], e2.at[q, p], sib).wait_recv()
-            add(p, held[a], s, r2[a], q)
+            add(p, s, r2[a], q)
             if q > 0:
                 @pl.when((zq[q] > z) & (z > 0) | (zq[q] < z) & (z < 3))
                 def _():
                     land = r3[a].at[zq[q], :, cut(p)]
                     rc(here, land, s3.at[q, p], e3.at[zq[q], p], sib).wait_recv()
-                    add(p, held[a], s, r3[a], zq[q])
+                    add(p, s, r3[a], zq[q])
                 @pl.when(zq[q] > z)
                 def _():
                     rc(here, r3[a].at[zq[q], :, cut(p)], s3.at[q, p], e3.at[zq[q], p], up).start()
@@ -658,54 +731,51 @@
                 def _():
                     rc(here, r3[a].at[zq[q], :, cut(p)], s3.at[q, p], e3.at[zq[q], p], down).start()
             else:
-                @pl.when(z > 0)
-                def _():
-                    rc(here, r3[a].at[z, :, cut(p)], s3.at[q, p], e3.at[z, p], sib).wait_recv()
-                @pl.when(z < 3)
-                def _():
-                    rc(here, r3[a].at[4, :, cut(p)], s3.at[q, p], e3.at[4, p], sib).wait_recv()
-                a_, c0, w, _m = parts[p]
-                step = 16
-                zero = jnp.float32(0)
-                def body(i, carry):
-                    r = pl.ds(pl.multiple_of(i * step, step), step)
-                    v = held[a][s, r, c0:c0 + w].astype(jnp.float32)
-                    outs[a][r, c0:c0 + w] = v.astype(outs[a].dtype)
-                    return carry
-                lax.fori_loop(0, rows[a] // step, body, 0)
+                def first_sum(r):
+                    outs[a][r, c0:c0 + w] = held[a][s, r, c0:c0 + w].astype(jnp.float32)
+                chunks(a, first_sum)
                 for cond, where in ((z > 0, z), (z < 3, 4)):
                     @pl.when(cond)
                     def _():
-                        def more(i, carry):
-                            r = pl.ds(pl.multiple_of(i * step, step), step)
+                        rc(here, r3[a].at[where, :, cut(p)], s3.at[q, p], e3.at[where, p], sib).wait_recv()
+                        def more(r):
                             outs[a][r, c0:c0 + w] += r3[a][where, r, c0:c0 + w].astype(jnp.float32)
-                            return carry
-                        lax.fori_loop(0, rows[a] // step, more, 0)
-
-    for f, q in ((1, 3), (1, 2), (2, 3), (1, 1), (2, 2), (3, 3), (1, 0), (2, 1), (3, 2), (2, 0), (3, 1), (3, 0)):
+                        chunks(a, more)
+
+    for step, (f, q) in enumerate(((1, 3), (1, 2), (2, 3), (1, 1), (2, 2), (3, 3), (1, 0), (2, 1), (3, 2), (2, 0), (3, 1), (3, 0))):
         (stage1, stage2, stage3)[f - 1](q)
-    for copy in sends: copy.wait_send()
+        if extra and step < len(batches):
+            lo = sum(batches[:step])
+            direct.start(TURNS[lo:lo + batches[step]])
+    for copy in sends:
+        copy.wait_send()
     for q in range(1, 4):
         for p in range(P):
             a = parts[p][0]
             here = held[a].at[slot(q, y, x), :, cut(p)]
             rc(here, here, s3.at[q, p], e3.at[0, p], sib).wait_send()
-
-def scatter(arrays, parts, collective_id):
-    k = len(arrays); P = len(parts)
+    if extra:
+        direct.finish()
+
+def scatter(arrays, parts, collective_id, extra=None, extra_in=(), extra_out=()):
+    k, P = len(arrays), len(parts)
     dma = pltpu.SemaphoreType.DMA
-    rows = [a.shape[0] // 32 for a in arrays]
-    scr = []
+    rows = [a.shape[0] // DEVICES for a in arrays]
+    if extra:
+        pieces, number, batches = extra
+        extra = (pieces, len(extra_in), len(extra_out), batches)
+    spaces = []
     for cnt in (16, 16, 8, 4, 5):
-        scr += [pltpu.VMEM((cnt, a.shape[0] // 32, a.shape[1]), a.dtype) for a in arrays]
+        spaces += [pltpu.VMEM((cnt, r, a.shape[1]), a.dtype) for r, a in zip(rows, arrays)]
+    hbm, vmem = pl.BlockSpec(memory_space=pl.ANY), pl.BlockSpec(memory_space=pltpu.VMEM)
     return pl.pallas_call(
-        functools.partial(scatter_kernel, parts, k, rows),
-        out_shape=[jax.ShapeDtypeStruct((a.shape[0] // 32, a.shape[1]), jnp.float32) for a in arrays],
-        in_specs=[pl.BlockSpec(memory_space=pl.ANY)] * k,
-        out_specs=[pl.BlockSpec(memory_space=pltpu.VMEM)] * k,
-        scratch_shapes=scr + [dma((4, 4, P)), dma((4, 4, P)), dma((4, 4, P)), dma((4, 2, P)), dma((4, 2, P)), dma((4, P)), dma((4, P)), dma((4, P)), dma((5, P))],
+        functools.partial(scatter_kernel, parts, k, rows, extra),
+        out_shape=[jax.ShapeDtypeStruct((r, a.shape[1]), jnp.float32) for r, a in zip(rows, arrays)] + list(extra_out),
+        in_specs=[hbm] * (k + len(extra_in)),
+        out_specs=[vmem] * k + [hbm] * len(extra_out),
+        scratch_shapes=spaces + [dma((4, 4, P))] * 3 + [dma((4, 2, P))] * 2 + [dma((4, P))] * 3 + [dma((5, P))] + (Direct.scratch(number) if extra else []),
         compiler_params=pltpu.CompilerParams(collective_id=collective_id, has_side_effects=True, vmem_limit_bytes=60 * 2**20),
-    )(*arrays)
+    )(*arrays, *extra_in)
 
 
 D = MODEL_WIDTH
@@ -713,7 +783,6 @@
 STEPS = 4
 M = SRC * CAP
 F32, BF16 = jnp.float32, jnp.bfloat16
-HALVES = ((0, 512, 1280), (1024, 128, 1792))
 
 def nt(a, b):
     return lax.dot_general(a, b, (((1,), (1,)), ((), ())), preferred_element_type=F32)
@@ -722,7 +791,9 @@
 def tn(a, b):
     return lax.dot_general(a, b, (((0,), (0,)), ((), ())), preferred_element_type=F32)
 
-def expert_kernel(own_ref, t_ref, c_ref, pick_ref, router_ref, w_ref, out_ref, gin_ref, gg_ref, dw_ref,
+QUARTER, DOWN_WHOLE, DOWN_QUARTER, OWN_WIDTH = 0, 256, 768, 896
+
+def expert_kernel(own_ref, t_ref, c_ref, pick_ref, router_ref, wf_ref, wo_ref, out_ref, gin_ref, gg_ref, dwf_ref, dwo_ref,
                   x_ref, g_ref, rw_ref, act_ref, dgu_ref, actq_ref, dguq_ref, ow_ref, gi_ref):
     i = pl.program_id(0)
     mine = (own_ref[0], own_ref[1])
@@ -744,25 +815,26 @@
             g_ref[k, to, :] = gs[k * 32:k * 32 + 32]
             rw_ref[k, s * CAP:s * CAP + CAP, :] = jnp.broadcast_to(jnp.sum(wide[k * 32:k * 32 + 32] * mineprob[k][:, s * 128:(s + 1) * 128], axis=1, keepdims=True), (CAP, 128))
     gws = []
-    for k, acts, dgus in ((0, act_ref, dgu_ref), (1, actq_ref, dguq_ref)):
-        g0, w, d0 = HALVES[k]
-        pre = nn(x_ref[k, at, :], w_ref[:, g0:g0 + 2 * w])
+    sets = (
+        (act_ref, dgu_ref, 512, wf_ref[...], wo_ref[:, DOWN_WHOLE:DOWN_WHOLE + 512]),
+        (actq_ref, dguq_ref, 128, wo_ref[:, QUARTER:QUARTER + 256], wo_ref[:, DOWN_QUARTER:DOWN_QUARTER + 128]),
+    )
+    for k, (acts, dgus, w, w_gu, w_d) in enumerate(sets):
+        pre = nn(x_ref[k, at, :], w_gu)
         gate, up = pre[:, :w], pre[:, w:]
         sig = jax.nn.sigmoid(gate)
         silu = gate * sig
-        act = (silu * up).astype(BF16)
-        acts[at, :] = act
-        rw = rw_ref[k, :, 0:1]
-        out = nt(act, w_ref[:, d0:d0 + w])
-        mix = g_ref[k, at, :].astype(F32) * 0.22
-        gws.append(jnp.sum(mix * out, axis=1, keepdims=True))
-        ow_ref[k] = (rw * out).astype(BF16)
-        g = (rw * mix).astype(BF16)
-        g_ref[k, at, :] = g
-        da = nn(g, w_ref[:, d0:d0 + w])
+        act = silu * up
+        share = rw_ref[k, :, 0:1] * RESIDUAL_SCALE
+        scaled = (share * act).astype(BF16)
+        acts[at, :] = scaled
+        da = nn(g_ref[k, at, :], w_d)
+        gws.append(RESIDUAL_SCALE * jnp.sum(act.astype(BF16).astype(F32) * da, axis=1, keepdims=True))
+        ow_ref[k] = nt(scaled, w_d).astype(BF16)
+        da = share * da
         dgu = jnp.concatenate([(da * up * sig * (1.0 + gate * (1.0 - sig))).astype(BF16), (da * silu).astype(BF16)], axis=1)
         dgus[at, :] = dgu
-        gi_ref[k] = nt(dgu, w_ref[:, g0:g0 + 2 * w]).astype(BF16)
+        gi_ref[k] = nt(dgu, w_gu).astype(BF16)
     for s in range(SRC):
         r = slice(s * CAP, s * CAP + CAP)
         pick = pick_ref[s * 64:s * 64 + 64, :]
@@ -778,50 +850,74 @@
     def _():
         def body(j, carry):
             c = pl.ds(pl.multiple_of(j * 256, 256), 256)
-            for k, acts, dgus in ((0, act_ref, dgu_ref), (1, actq_ref, dguq_ref)):
-                g0, w, d0 = HALVES[k]
-                dw_ref[c, g0:g0 + 2 * w] = tn(x_ref[k, :, c], dgus[...]).astype(BF16)
-                dw_ref[c, d0:d0 + w] = tn(g_ref[k, :, c], acts[...]).astype(BF16)
+            dwf_ref[c, :] = tn(x_ref[0, :, c], dgu_ref[...]).astype(BF16)
+            dwo_ref[c, QUARTER:QUARTER + 256] = tn(x_ref[1, :, c], dguq_ref[...]).astype(BF16)
+            dwo_ref[c, DOWN_WHOLE:DOWN_WHOLE + 512] = tn(g_ref[0, :, c], act_ref[...]).astype(BF16)
+            dwo_ref[c, DOWN_QUARTER:DOWN_QUARTER + 128] = tn(g_ref[1, :, c], actq_ref[...]).astype(BF16)
             return carry
         lax.fori_loop(0, D // 256, body, 0)
 
-def experts(owned, tokens, cot, picks, router_t, w):
+def experts(owned, tokens, cot, picks, router_t, wf, wo):
     R = SRC * 128
+    once = lambda shape: pl.BlockSpec(shape, lambda i: (0, 0), pipeline_mode=pl.Buffered(1))
+    rows = pl.BlockSpec((R, D), lambda i: (i, 0))
+    vmem = lambda *shape, dtype=BF16: pltpu.VMEM(shape, dtype)
     return pl.pallas_call(
         expert_kernel,
         grid=(STEPS,),
         in_specs=[
-            pl.BlockSpec(memory_space=pltpu.SMEM),
-            pl.BlockSpec((R, D), lambda i: (i, 0)),
-            pl.BlockSpec((R, D), lambda i: (i, 0)),
-            pl.BlockSpec((SRC * 64, 128), lambda i: (i, 0)),
-            pl.BlockSpec((64, D), lambda i: (0, 0), pipeline_mode=pl.Buffered(1)),
-            pl.BlockSpec((D, 1920), lambda i: (0, 0), pipeline_mode=pl.Buffered(1)),
+            pl.BlockSpec(memory_space=pltpu.SMEM), rows, rows, pl.BlockSpec((SRC * 64, 128), lambda i: (i, 0)),
+            once((64, D)), once((D, 2 * F)), once((D, OWN_WIDTH)),
         ],
-        out_specs=[
-            pl.BlockSpec((R, D), lambda i: (i, 0)),
-            pl.BlockSpec((R, D), lambda i: (i, 0)),
-            pl.BlockSpec((SRC, 8, 128), lambda i: (i, 0, 0)),
-            pl.BlockSpec((D, 1920), lambda i: (0, 0), pipeline_mode=pl.Buffered(1)),
-        ],
+        out_specs=[rows, rows, pl.BlockSpec((SRC, 8, 128), lambda i: (i, 0, 0)), once((D, 2 * F)), once((D, OWN_WIDTH))],
         out_shape=[
-            jax.ShapeDtypeStruct((4096, D), BF16), jax.ShapeDtypeStruct((4096, D), BF16),
-            jax.ShapeDtypeStruct((32, 8, 128), F32), jax.ShapeDtypeStruct((D, 1920), BF16),
+            jax.ShapeDtypeStruct((4096, D), BF16), jax.ShapeDtypeStruct((4096, D), BF16), jax.ShapeDtypeStruct((32, 8, 128), F32),
+            jax.ShapeDtypeStruct((D, 2 * F), BF16), jax.ShapeDtypeStruct((D, OWN_WIDTH), BF16),
         ],
         scratch_shapes=[
-            pltpu.VMEM((2, 1024, D), BF16), pltpu.VMEM((2, 1024, D), BF16), pltpu.VMEM((2, M, 128), F32),
-            pltpu.VMEM((1024, 512), BF16), pltpu.VMEM((1024, 1024), BF16), pltpu.VMEM((1024, 128), BF16), pltpu.VMEM((1024, 256), BF16),
-            pltpu.VMEM((2, M, D), BF16), pltpu.VMEM((2, M, D), BF16),
+            vmem(2, 1024, D), vmem(2, 1024, D), vmem(2, M, 128, dtype=F32),
+            vmem(1024, 512), vmem(1024, 1024), vmem(1024, 128), vmem(1024, 256), vmem(2, M, D), vmem(2, M, D),
         ],
         compiler_params=pltpu.CompilerParams(vmem_limit_bytes=62 * 2**20),
         cost_estimate=pl.CostEstimate(flops=22 * 10**9, bytes_accessed=62 * 10**6, transcendentals=0),
-    )(owned, tokens, cot, picks, router_t, w)
-
-
-GATHER_DENSE = ((0, 0, 1280, 0), (0, 1280, 1280, 1), (1, 0, 768, 0), (1, 768, 896, 1), (2, 0, 128, 0))
+    )(owned, tokens, cot, picks, router_t, wf, wo)
+
+
 TOKEN_HALVES = ((0, 0, 768, 0), (0, 768, 768, 1))
-GATHER_TOKENS = TOKEN_HALVES + ((1, 0, 768, 0), (1, 768, 768, 1))
-SCATTER_LAST = ((0, 0, 1280, 0), (0, 1280, 1280, 1), (1, 0, 768, 0), (1, 768, 896, 1), (2, 0, 768, 0), (2, 768, 768, 1))
+GATHER_FIRST = ((0, 0, 1280, 0), (0, 1280, 1280, 1), (1, 0, 768, 0), (1, 768, 768, 1), (2, 0, 128, 1), (3, 0, 128, 0), (4, 0, 768, 0), (4, 768, 768, 1))
+SCATTER_LAST = ((0, 0, 1280, 0), (0, 1280, 1280, 1), (1, 0, 768, 0), (1, 768, 768, 1), (2, 0, 128, 0), (3, 0, 768, 0), (3, 768, 768, 1))
+OUT_BATCHES = (2, 2, 2, 3, 3, 3, 4, 4, 4, 4)
+BACK_BATCHES = (3, 3, 3, 3, 3, 3, 3, 3, 3, 4)
+
+
+def lanes(start):
+    return pl.ds(pl.multiple_of(start, 128), 128)
+
+
+def weights_out(src, dst, refs):
+    g_ref, d_ref, wo_ref = refs
+    group, quarter = dst // 4, lax.rem(dst, 4) * 128
+    rows = pl.ds(pl.multiple_of(src * 48, 48), 48)
+    fifth = group * 5 + 4
+    return (
+        (g_ref.at[fifth, :, lanes(quarter)], wo_ref.at[rows, pl.ds(QUARTER, 128)]),
+        (g_ref.at[fifth, :, lanes(F + quarter)], wo_ref.at[rows, pl.ds(QUARTER + 128, 128)]),
+        (d_ref.at[group * 5 + lax.rem(dst, 4)], wo_ref.at[rows, pl.ds(DOWN_WHOLE, F)]),
+        (d_ref.at[fifth, :, lanes(quarter)], wo_ref.at[rows, pl.ds(DOWN_QUARTER, 128)]),
+    )
+
+
+def grads_back(src, dst, refs):
+    dwo_ref, gates_ref, g_ref, d_ref, all_gates_ref = refs
+    group, quarter = src // 4, lax.rem(src, 4) * 128
+    rows = pl.ds(pl.multiple_of(dst * 48, 48), 48)
+    return (
+        (dwo_ref.at[rows, pl.ds(QUARTER, 128)], g_ref.at[group, :, lanes(quarter)]),
+        (dwo_ref.at[rows, pl.ds(QUARTER + 128, 128)], g_ref.at[group, :, lanes(F + quarter)]),
+        (dwo_ref.at[rows, pl.ds(DOWN_WHOLE, F)], d_ref.at[group * 5 + lax.rem(src, 4)]),
+        (dwo_ref.at[rows, pl.ds(DOWN_QUARTER, 128)], d_ref.at[group * 5 + 4, :, lanes(quarter)]),
+        (gates_ref.at[dst], all_gates_ref.at[src]),
+    )
 
 
 def fast(
@@ -834,21 +930,20 @@
     small = jnp.concatenate(
         [router, attention_gain[:, None], moe_gain[:, None], jnp.zeros((own_rows, 86), BF16)], axis=1
     )
-    qkv_full, out_small, ids_all = gather(
-        [qkv_weight, jnp.concatenate([output_weight, small], axis=1), expert_ids.T], GATHER_DENSE, 0
-    )
-    out_full, small_full = out_small[:, :D], out_small[:, D:]
+    gu = jnp.transpose(gate_up, (1, 0, 2))
+    dp = jnp.transpose(down_proj, (1, 0, 2))
+    qkv_full, out_full, small_full, ids_all, cots, wo = gather(
+        [qkv_weight, output_weight, small, expert_ids.T, cotangent],
+        GATHER_FIRST,
+        0,
+        (weights_out, 4, OUT_BATCHES),
+        (gu, dp),
+        (jax.ShapeDtypeStruct((D, OWN_WIDTH), BF16),),
+    )
     router_full, gain_one, gain_two = small_full[:, :E], small_full[:, E].astype(F32), small_full[:, E + 1].astype(F32)
-
-    gu = jnp.transpose(gate_up, (1, 0, 2)).reshape(8, 5, own_rows, 2 * F)
-    dp = jnp.transpose(down_proj, (1, 0, 2)).reshape(8, 5, own_rows, F)
-    gu_q = jnp.transpose(gu[:, 4].reshape(8, own_rows, 2, 4, 128), (0, 3, 1, 2, 4)).reshape(n, own_rows, 256)
-    dp_q = jnp.transpose(dp[:, 4].reshape(8, own_rows, 4, 128), (0, 2, 1, 3)).reshape(n, own_rows, 128)
-    pack = jnp.concatenate(
-        [gu[:, :4].reshape(n, own_rows, 2 * F), gu_q, dp[:, :4].reshape(n, own_rows, F), dp_q], axis=2
-    )
-    pack, qkv_full = lax.optimization_barrier((pack, qkv_full))
-    w = lax.all_to_all(pack, "fsdp", split_axis=0, concat_axis=0, tiled=True).reshape(D, 1920)
+    whole = gu.reshape(8, 5, own_rows, 2 * F)[:, :4].reshape(n, own_rows, 2 * F)
+    whole, qkv_full = lax.optimization_barrier((whole, qkv_full))
+    wf = lax.all_to_all(whole, "fsdp", split_axis=0, concat_axis=0, tiled=True).reshape(D, 2 * F)
 
     inputs = layer_input.astype(F32)
     scale_one = norm_scale(inputs)
@@ -872,20 +967,26 @@
     scale_two = norm_scale(middle)
     normed_two = (middle * scale_two * gain_two).astype(BF16)
 
-    tokens, cots = gather([normed_two, cotangent], GATHER_TOKENS, 1)
-    whole, fifth = (me // 4) * 5 + lax.rem(me, 4), (me // 4) * 5 + 4
-    owned = jnp.stack([whole, fifth])
+    [tokens] = gather([normed_two], TOKEN_HALVES, 1)
+    owned = jnp.stack([(me // 4) * 5 + lax.rem(me, 4), (me // 4) * 5 + 4])
     named = jnp.any(ids_all.reshape(n, TOP, T)[:, :, None, :] == owned[None, None, :, None], axis=1)
     before = (place_in[:, None] < place_in[None, :]).astype(BF16)
     ranks = jnp.dot(named.astype(BF16).reshape(2 * n, T), before, preferred_element_type=F32).reshape(n, 2, 1, T)
     picks = ((ranks == jnp.arange(CAP, dtype=F32)[:, None]) & named[:, :, None, :]).astype(BF16).reshape(n * 64, T)
     router_t = jnp.pad(router_full.T, ((0, 64 - E), (0, 0)))
-    out_part, gin_part, gg, dw = experts(owned, tokens, cots, picks, router_t, w)
-    gg_all = lax.all_to_all(gg, "fsdp", split_axis=0, concat_axis=0, tiled=True).reshape(8, 4, 8, T)
+    out_part, gin_part, gg, dwf, dwo = experts(owned, tokens, cots, picks, router_t, wf, wo)
+    gin, grad_fifth, grad_down, gg_all = scatter(
+        [gin_part],
+        TOKEN_HALVES,
+        2,
+        (grads_back, 5, BACK_BATCHES),
+        (dwo, gg),
+        (jax.ShapeDtypeStruct((8, own_rows, 2 * F), BF16), jax.ShapeDtypeStruct((E, own_rows, F), BF16), jax.ShapeDtypeStruct((n, 8, T), F32)),
+    )
+    gg_all = gg_all.reshape(8, 4, 8, T)
     grad_gates = jnp.concatenate([gg_all[:, :, 0], jnp.sum(gg_all[:, :, 1], axis=1, keepdims=True)], axis=1).reshape(E, T).T
-    [gin] = scatter([gin_part], TOKEN_HALVES, 2)
-    dw, gin = lax.optimization_barrier((dw, gin))
-    dw = lax.all_to_all(dw.reshape(n, own_rows, 1920), "fsdp", split_axis=0, concat_axis=0, tiled=True)
+    dwf, gin = lax.optimization_barrier((dwf, gin))
+    grad_whole = lax.all_to_all(dwf.reshape(n, own_rows, 2 * F), "fsdp", split_axis=0, concat_axis=0, tiled=True)
 
     upstream = cotangent.astype(F32)
     logits = jnp.dot(normed_two, router_full, preferred_element_type=F32)
@@ -920,27 +1021,25 @@
     grad_inputs, gain_one_part = norm_back(inputs, gain_one, scale_one, grad_normed_one)
     input_grad = (grad_inputs + grad_middle).astype(BF16)
 
-    out_small_part = jnp.concatenate(
-        [out_grad_part, router_part, gain_one_part[:, None], gain_two_part[:, None], jnp.zeros((D, 86), F32)], axis=1
+    small_part = jnp.concatenate(
+        [router_part, gain_one_part[:, None], gain_two_part[:, None], jnp.zeros((D, 86), F32)], axis=1
     ).astype(BF16)
-    qkv_grad, out_small_grad, combined = scatter([qkv_part.astype(BF16), out_small_part, out_part], SCATTER_LAST, 3)
-    layer_output = (middle + RESIDUAL_SCALE * combined).astype(BF16)
-
-    part = lambda c0, c1: dw[:, :, c0:c1]
-    gu_w = part(0, 1024).reshape(8, 4, own_rows, 1024)
-    gu_f = jnp.transpose(part(1024, 1280).reshape(8, 4, own_rows, 2, 128), (0, 2, 3, 1, 4)).reshape(8, 1, own_rows, 1024)
-    gate_up_grad = jnp.transpose(jnp.concatenate([gu_w, gu_f], axis=1).reshape(E, own_rows, 1024), (1, 0, 2)).astype(F32)
-    dp_w = part(1280, 1792).reshape(8, 4, own_rows, F)
-    dp_f = jnp.transpose(part(1792, 1920).reshape(8, 4, own_rows, 128), (0, 2, 1, 3)).reshape(8, 1, own_rows, F)
-    down_grad = jnp.transpose(jnp.concatenate([dp_w, dp_f], axis=1).reshape(E, own_rows, F), (1, 0, 2)).astype(F32)
+    qkv_grad, out_grad, small_grad, combined = scatter(
+        [qkv_part.astype(BF16), out_grad_part.astype(BF16), small_part, out_part], SCATTER_LAST, 3
+    )
+    layer_output = (middle + combined).astype(BF16)
+
+    grad_gu = jnp.concatenate([grad_whole.reshape(8, 4, own_rows, 2 * F), grad_fifth[:, None]], axis=1)
+    gate_up_grad = jnp.transpose(grad_gu.reshape(E, own_rows, 2 * F), (1, 0, 2)).astype(F32)
+    down_grad = jnp.transpose(grad_down, (1, 0, 2)).astype(F32)
     return (
         layer_output,
         input_grad,
-        out_small_grad[:, D + E],
+        small_grad[:, E],
         qkv_grad,
-        out_small_grad[:, :D],
-        out_small_grad[:, D + E + 1],
-        out_small_grad[:, D : D + E],
+        out_grad,
+        small_grad[:, E + 1],
+        small_grad[:, :E],
         gate_up_grad,
         down_grad,
     )

time: 669 us -> 635 us (0.949)
  local copies, waits for them, and re-layouts: 72.4 us -> 36.9 us
  Pallas kernels: 508 us -> 528 us
  starting transfers between devices: 24.3 us -> 8.28 us
    pallas_call x4, Pallas kernels: 458 us -> 481 us  [the longest x2 248 us: gather(): pl.pallas_call(functools.partial(gather_kernel, parts, k, extra), out_sha...]
    all_to_all x3 -> x2, starting transfers between devices: 24.3 us -> 8.28 us  [the longest x1 4.34 us: fast(): lax.all_to_all(dwf.reshape(n, own_rows, 2 * F), 'fsdp', split_axis=0, con...]
    concatenate x2 -> x1, local copies, waits for them, and re-layouts: 10.8 us -> 0.08 us  [fast(): jnp.concatenate([router, attention_gain[:, None], moe_gain[:, None], jnp....]
    slice x11 -> x2, local copies, waits for them, and re-layouts: 12.4 us -> 2.86 us  [the longest x1 2.16 us: fast(): whole = gu.reshape(8, 5, own_rows, 2 * F)[:, :4].reshape(n, own_rows, 2 * F)]
    pallas_call x1, local copies, waits for them, and re-layouts: 7.84 us -> 0.93 us  [gather(): pl.pallas_call(functools.partial(gather_kernel, parts, k, extra), out_sha...]
    unnamed x71 -> x120, local copies, waits for them, and re-layouts: 21.7 us -> 26.8 us
  transfers between devices with their start and end apart: 3 -> 2, of which waited for: 0 -> 0; matrix products, arithmetic and copies ran while one was open for 11% -> 10% of each run, Pallas kernels for 60% -> 36%
where the time goes in v2:
time: 635 us; the launch traced here: 628 us
  Pallas kernels  528 us (83%)
  local copies, waits for them, and re-layouts  36.9 us (6%)
  matrix products  34.2 us (5%)
  other arithmetic  18.4 us (3%)
  starting transfers between devices  8.28 us (1%)
    pallas_call x2, Pallas kernels, gather(): pl.pallas_call(functools.partial(gather_kernel, parts, k, extra), out_sha...  248 us
    pallas_call x2, Pallas kernels, scatter(): pl.pallas_call(functools.partial(scatter_kernel, parts, k, rows, extra),...  234 us
    pallas_call x1, Pallas kernels, experts(): pl.pallas_call(expert_kernel, grid=(STEPS,), in_specs=[pl.BlockSpec(memor...  47.1 us
    unnamed x120, local copies, waits for them, and re-layouts  26.8 us
  transfers between devices with their start and end apart: 2, of which 0 were waited for; matrix products, arithmetic and copies ran while one was open for 10% of the time, Pallas kernels for 36%

profile of v2, /device:TPU:0, one launch (start us, length us, event | category | flops | bytes accessed | tf_op | source)
XLA Modules:
  0.0 628.0 jit_solution(6363634828453480157)
XLA Ops:
  0.7 6.3 %copy.137 = bf16[48,40,1024]{2,0,1:T(8,128)(2,1)} copy(bf16[48,40,1024]{2,1,0:T(8,128)(2,1)} %param.20) | data formatting | bytes 7864320 | tf_op args[9]
  7.4 2.0 copy.136
  9.3 0.8 copy-done
  10.2 2.2 slice.81
  12.4 0.7 maximum_maximum_fusion.1.refs_2_
  13.1 150.4 %shard_map.178 = (bf16[1536,2560]{1,0:T(8,128)(2,1)}, bf16[1536,1536]{1,0:T(8,128)(2,1)}, bf16[1536,128]{1,0:T(8,128)(2,1)}, s32[256,128]{1,0:T(8,128)}, bf16[40...) custom-call(bf16[48,2560]{1,0:T(8,128)(2,1)} %refs_0_.1, bf16[48,1536]{1,0:T(8,128)(2,1)} %refs_1_.1, ...), custom_call_target="tpu_custom_call" | custom-call | tf_op jit(solution)/shard_map/pallas_call | solution.py:610
  163.5 3.9 all-to-all-start
  167.5 0.2 fusion.8
  167.6 1.0 convert_reduce_fusion
  168.7 0.6 multiply_multiply_fusion
  169.3 0.5 copy-done.41
  169.8 4.5 fusion.22
  174.4 0.9 copy.109
  175.4 0.2 compare_reduce_fusion
  175.7 0.6 copy.108
  176.4 0.7 eq.65
  177.1 0.3 copy.105
  178.2 0.4 fusion.48
  178.6 0.3 exponential_reduce_fusion
  179.0 0.4 convolution_convert_fusion.4
  179.4 3.4 multiply_reduce_fusion.3
  182.9 0.6 multiply_multiply_fusion.1
  183.4 0.3 copy-done.1
  183.8 0.2 copy-done.46
  183.9 0.9 multiply_convert_fusion.1.refs_0_
  184.8 97.2 %shard_map.179.t_ref = bf16[4096,1536]{1,0:T(8,128)(2,1)} custom-call(bf16[128,1536]{1,0:T(8,128)(2,1)} %multiply_convert_fusion.1.refs_0_), custom_call_target="tpu_custom_call" | custom-call | tf_op jit(solution)/shard_map/pallas_call | solution.py:610
  282.1 0.7 pad.4.router_ref
  282.8 1.2 fusion.7.pick_ref
  283.9 0.2 fusion.49
  284.2 0.5 fusion.35
  284.7 47.1 %shard_map.180 = (bf16[4096,1536]{1,0:T(8,128)(2,1)}, bf16[4096,1536]{1,0:T(8,128)(2,1)}, f32[32,8,128]{2,1,0:T(8,128)}, bf16[1536,1024]{1,0:T(8,128)(2,1)}, bf16[1536,896]{1,0:T(8,128)(2,1)}) custom-call(s32[2]{0:T(128)} %copy-done.52, bf16[4096,1536]{1,0:T(8,128)(2,1)} %shard_map.179.t_ref, bf16[4096,1536]{1,0:T(8,128)(2,1)} %get-tuple-element.36.c_ref, ...), custom_call_target="tpu_custom_call" | custom-call | flops 22000001024 | bytes 62000000 | tf_op jit(solution)/shard_map/pallas_call | solution.py:865
  331.8 105.8 %shard_map.181 = (f32[128,1536]{1,0:T(8,128)}, bf16[8,48,1024]{2,1,0:T(8,128)(2,1)}, bf16[40,48,512]{2,1,0:T(8,128)(2,1)}, f32[32,8,128]{2,1,0:T(8,128)}) custom-call(bf16[4096,1536]{1,0:T(8,128)(2,1)} %get-tuple-element.41.refs_0_, bf16[1536,896]{1,0:T(8,128)(2,1)} %get-tuple-element.42.refs_1_, f32[32,8,128]{2,1,0:T(8,128)} %get-tuple-element.43.refs_2_), custom_call_target="tpu_custom_call" | custom-call | tf_op jit(solution)/shard_map/pallas_call | solution.py:771
  437.7 4.3 all-to-all-start.1
  442.1 1.0 fusion.47
  443.2 0.3 convolution_convert_fusion.3
  443.4 1.0 copy.115
  444.4 2.0 multiply_reduce_fusion
  446.4 1.3 convert_add_fusion
  447.7 0.9 copy-done.4
  448.6 4.8 convolution_convert_fusion.2
  453.4 1.9 copy.111
  455.3 1.2 multiply_reduce_fusion.1
  456.5 1.5 fusion.3
  458.1 0.5 convolution_bitcast_fusion.1
  458.7 0.3 fusion.27
  459.1 0.5 copy-done.11
  459.6 0.5 fusion.5
  460.1 6.2 fusion.17
  466.3 0.3 broadcast_in_dim.36
  466.6 0.3 broadcast_in_dim.37
  466.9 3.5 convolution_convert_fusion.1.refs_1_
  470.4 5.6 convolution_convert_fusion.refs_0_
  476.0 1.1 maximum_maximum_fusion.refs_2_
  477.1 128.0 %shard_map.182 = (f32[48,2560]{1,0:T(8,128)}, f32[48,1536]{1,0:T(8,128)}, f32[48,128]{1,0:T(8,128)}, f32[128,1536]{1,0:T(8,128)}) custom-call(bf16[1536,2560]{1,0:T(8,128)(2,1)} %convolution_convert_fusion.refs_0_, bf16[1536,1536]{1,0:T(8,128)(2,1)} %convolution_convert_fusion.1.refs_1_, bf16[1536,128]{1,0:T(8,128)(2,1)} %maximum_maximum_fusion.refs_2_, ...), custom_call_target="tpu_custom_call" | custom-call | tf_op jit(solution)/shard_map/pallas_call | solution.py:771
  605.1 1.4 copy.119
  606.5 2.1 convert_bitcast_fusion.1
  608.6 4.2 copy.121
  612.8 0.7 slice_reduce_fusion
  613.5 1.3 fusion.16
  614.9 2.2 pad_maximum_fusion
  617.1 1.2 convert_bitcast_fusion
  618.4 7.8 %copy.120 = f32[48,40,1024]{2,1,0:T(8,128)} copy(f32[48,40,1024]{2,0,1:T(8,128)S(1)} %convert_bitcast_fusion) | data formatting | bytes 15728640
  626.2 0.8 copy.140
  626.9 0.7 copy.141
  (139 shorter events, 2.0 us)
Async XLA Ops:
  0.6 6.4 %copy-start.53 = (bf16[48]{0:T(256)(128)(2,1)S(1)}, bf16[48]{0:T(256)(128)(2,1)}, u32[]{:S(2)}) copy-start(bf16[48]{0:T(256)(128)(2,1)} %param.18) | copy-start | bytes 292
  0.7 6.5 %copy-start.44 = (bf16[48,40]{0,1:T(8,128)(2,1)S(1)}, bf16[48,40]{0,1:T(8,128)(2,1)}, u32[]{:S(2)}) copy-start(bf16[48,40]{0,1:T(8,128)(2,1)} %param.19) | copy-start | bytes 11524
  0.7 6.6 %copy-start.54 = (bf16[48]{0:T(256)(128)(2,1)S(1)}, bf16[48]{0:T(256)(128)(2,1)}, u32[]{:S(2)}) copy-start(bf16[48]{0:T(256)(128)(2,1)} %param.15) | copy-start | bytes 292
  0.7 6.7 %copy-start.13 = (bf16[48,40,512]{2,1,0:T(8,128)(2,1)S(1)}, bf16[48,40,512]{2,1,0:T(8,128)(2,1)}, u32[]{:S(2)}) copy-start(bf16[48,40,512]{2,1,0:T(8,128)(2,1)} %param.21) | copy-start | bytes 5898244
  7.3 2.8 copy-start
  12.4 151.0 %copy-start.48 = (bf16[128]{0:T(256)(128)(2,1)}, bf16[128]{0:T(256)(128)(2,1)S(1)}, u32[]{:S(2)}) copy-start(bf16[128]{0:T(256)(128)(2,1)S(1)} %pad.29.clone) | copy-start | bytes 772
  163.5 4.0 copy-start.3
  163.5 4.1 copy-start.12
  163.5 121.2 %all-to-all-start = ((bf16[32,48,1024]{2,1,0:T(8,128)(2,1)}), bf16[32,48,1024]{2,1,0:T(8,128)(2,1)}, u32[]{:S(2)}, u32[]{:S(2)}) async-start(bf16[32,48,1024]{2,1,0:T(8,128)(2,1)} %bitcast.6), calls=%async_computation | async-start | bytes 6291456 | tf_op jit(solution)/shard_map/all_to_all | solution.py:946
  169.3 0.5 copy-start.41
  174.3 1.1 copy-start.36
  174.3 3.0 copy-start.50
  175.4 2.3 copy-start.52
  175.6 0.8 copy-start.37
  177.7 1.3 copy-start.16
  178.0 0.9 copy-start.28
  178.1 0.9 copy-start.30
  178.2 0.8 copy-start.19
  178.2 0.8 copy-start.21
  179.0 3.8 copy-start.26
  179.4 3.4 copy-start.6
  179.4 4.5 copy-start.33
  182.9 0.9 copy-start.1
  183.4 0.5 copy-start.46
  184.8 97.2 %copy-start.15 = (bf16[1536,128]{0,1:T(8,128)(2,1)S(1)}, bf16[1536,128]{0,1:T(8,128)(2,1)}, u32[]{:S(2)}) copy-start(bf16[1536,128]{0,1:T(8,128)(2,1)} %copy.109) | copy-start | bytes 1179652
  184.8 98.0 %copy-start.35 = (f32[32,2,128]{2,1,0:T(2,128)S(1)}, f32[32,2,128]{2,1,0:T(2,128)}, u32[]{:S(2)}) copy-start(f32[32,2,128]{2,1,0:T(2,128)} %copy.108) | copy-start | bytes 98308
  184.8 98.0 %copy-start.38 = (pred[32,2,128]{2,1,0:T(4,128)(4,1)S(1)}, pred[32,2,128]{2,1,0:T(4,128)(4,1)}, u32[]{:S(2)}) copy-start(pred[32,2,128]{2,1,0:T(4,128)(4,1)} %copy-done.37) | copy-start | bytes 24580
  184.8 98.0 %copy-start.39 = (f32[2048]{0:T(1024)S(1)}, f32[2048]{0:T(1024)}, u32[]{:S(2)}) copy-start(f32[2048]{0:T(1024)} %eq.65) | copy-start | bytes 24580
  184.8 99.1 %copy-start.9 = (bf16[128,1536]{1,0:T(8,128)(2,1)S(1)}, bf16[128,1536]{1,0:T(8,128)(2,1)}, u32[]{:S(2)}) copy-start(bf16[128,1536]{1,0:T(8,128)(2,1)} %multiply_convert_fusion.1.refs_0_) | copy-start | bytes 1179652
  284.2 159.0 %copy-start.40 = (f32[128]{0:T(128)}, f32[128]{0:T(128)S(1)}, u32[]{:S(2)}) copy-start(f32[128]{0:T(128)S(1)} %get-tuple-element.121) | copy-start | bytes 1540
  437.6 5.5 copy-start.45
  437.6 5.5 copy-start.10
  437.7 6.8 %copy-start.2 = (f32[128,1536]{1,0:T(8,128)S(1)}, f32[128,1536]{1,0:T(8,128)}, u32[]{:S(2)}) copy-start(f32[128,1536]{1,0:T(8,128)} %copy-done.1) | copy-start | bytes 2359300
  437.7 6.8 %copy-start.34 = (f32[1536]{0:T(1024)S(1)}, f32[1536]{0:T(1024)}, u32[]{:S(2)}) copy-start(f32[1536]{0:T(1024)} %get-tuple-element.95) | copy-start | bytes 18436
  437.7 6.8 %copy-start.47 = (f32[128]{0:T(128)S(1)}, f32[128]{0:T(128)}, u32[]{:S(2)}) copy-start(f32[128]{0:T(128)} %copy-done.46) | copy-start | bytes 1540
  437.7 177.2 %all-to-all-start.1 = ((bf16[32,48,1024]{2,1,0:T(8,128)(2,1)}), bf16[32,48,1024]{2,1,0:T(8,128)(2,1)}, u32[]{:S(2)}, u32[]{:S(2)}) async-start(bf16[32,48,1024]{2,1,0:T(8,128)(2,1)} %bitcast.131), calls=%async_computation.1 | async-start | bytes 6291456 | tf_op jit(solution)/shard_map/all_to_all | solution.py:989
  442.0 4.4 copy-start.55
  447.7 0.9 copy-start.4
  448.6 6.7 %copy-start.7 = (bf16[8,64,3,128]{3,1,2,0:T(8,128)(2,1)S(1)}, bf16[8,64,3,128]{3,1,2,0:T(8,128)(2,1)}, u32[]{:S(2)}) copy-start(bf16[8,64,3,128]{3,1,2,0:T(8,128)(2,1)} %copy-done.6) | copy-start | bytes 1179652
  448.6 7.9 %copy-start.17 = (bf16[128,512]{0,1:T(8,128)(2,1)S(1)}, bf16[128,512]{0,1:T(8,128)(2,1)}, u32[]{:S(2)}) copy-start(bf16[128,512]{0,1:T(8,128)(2,1)} %copy-done.16) | copy-start | bytes 393220
  448.6 7.9 %copy-start.27 = (f32[8,3,128]{2,1,0:T(4,128)S(1)}, f32[8,3,128]{2,1,0:T(4,128)}, u32[]{:S(2)}) copy-start(f32[8,3,128]{2,1,0:T(4,128)} %copy-done.26) | copy-start | bytes 36868
  455.3 2.8 copy-start.20
  455.3 2.8 copy-start.22
  456.5 2.1 copy-start.29
  456.5 2.1 copy-start.31
  458.6 1.0 copy-start.11
  459.0 1.1 copy-start.42
  460.1 6.8 %copy-start.5 = (f32[128,1536]{1,0:T(8,128)S(1)}, f32[128,1536]{1,0:T(8,128)}, u32[]{:S(2)}) copy-start(f32[128,1536]{1,0:T(8,128)} %copy-done.4) | copy-start | bytes 2359300
  460.1 6.8 %copy-start.8 = (bf16[8,64,3,128]{3,1,2,0:T(8,128)(2,1)S(1)}, bf16[8,64,3,128]{3,1,2,0:T(8,128)(2,1)}, u32[]{:S(2)}) copy-start(bf16[8,64,3,128]{3,1,2,0:T(8,128)(2,1)} %copy-done.6) | copy-start | bytes 1179652
  470.4 5.6 copy-start.14
  470.4 5.6 copy-start.49
  608.6 4.2 copy-start.32
  608.6 4.9 copy-start.18
  608.6 4.9 copy-start.43
  608.6 4.9 copy-start.51
  613.5 1.3 copy-start.23
  618.4 7.8 %copy-start.24 = (f32[48,2560]{1,0:T(8,128)S(1)}, f32[48,2560]{1,0:T(8,128)}, u32[]{:S(2)}) copy-start(f32[48,2560]{1,0:T(8,128)} %get-tuple-element.139) | copy-start | bytes 1474564
  618.4 8.6 %copy-start.25 = (f32[48,1536]{1,0:T(8,128)S(1)}, f32[48,1536]{1,0:T(8,128)}, u32[]{:S(2)}) copy-start(f32[48,1536]{1,0:T(8,128)} %get-tuple-element.140) | copy-start | bytes 884740

commit v3 on v0

--- a/solution.py
+++ b/solution.py
@@ -1,9 +1,11 @@
+import functools
 import math
-
 import jax
 import jax.numpy as jnp
 import numpy as np
 from jax import lax
+from jax.experimental import pallas as pl
+from jax.experimental.pallas import tpu as pltpu
 from jax.sharding import PartitionSpec as P
 
 MODEL_WIDTH = 1536
@@ -26,9 +28,8 @@
 def positions(sequence_ids):
     sequence_length = sequence_ids.shape[0]
     places = jnp.arange(sequence_length, dtype=jnp.int32)
-    starts_new = jnp.concatenate([jnp.ones((1,), jnp.bool_), sequence_ids[1:] != sequence_ids[:-1]])
-    begins = lax.cummax(jnp.where(starts_new, places, 0), axis=0)
-    return places - begins
+    same = (sequence_ids[:, None] == sequence_ids[None, :]) & (places[None, :] < places[:, None])
+    return jnp.sum(same.astype(jnp.int32), axis=1, dtype=jnp.int32)
 
 
 def rope_tables(places, head_size):
@@ -82,11 +83,14 @@
 
 
 def expert_slots(expert_ids, experts, capacity):
-    flat_ids = expert_ids.reshape(-1)
-    onehot = (flat_ids[:, None] == jnp.arange(experts, dtype=jnp.int32)[None, :]).astype(jnp.int32)
-    running = jnp.cumsum(onehot, axis=0, dtype=jnp.int32)
-    ranks = jnp.sum((running - 1) * onehot, axis=-1, dtype=jnp.int32)
-    return flat_ids * capacity + ranks
+    rows = expert_ids.shape[0]
+    picked = expert_ids[:, :, None] == jnp.arange(experts, dtype=jnp.int32)[None, None, :]
+    named = jnp.any(picked, axis=1).astype(jnp.bfloat16)
+    places = jnp.arange(rows, dtype=jnp.int32)
+    before = (places[None, :] < places[:, None]).astype(jnp.bfloat16)
+    ranks = jnp.dot(before, named, preferred_element_type=jnp.float32)
+    ranks = jnp.sum(jnp.where(picked, ranks[:, None, :], 0.0), axis=-1).astype(jnp.int32)
+    return (expert_ids * capacity + ranks).reshape(-1)
 
 
 def owner_tables(devices):
@@ -102,7 +106,10 @@
     padded = jnp.concatenate(
         [buffer_rows, jnp.zeros((1, CAP, MODEL_WIDTH), buffer_rows.dtype)], axis=0
     )
-    picked_rows = jnp.take(padded, jnp.asarray(send_table, dtype=jnp.int32), axis=0)
+    chosen = jnp.asarray(send_table[:, None] == np.arange(E + 1)[None, :], dtype=buffer_rows.dtype)
+    picked_rows = jnp.einsum(
+        "se,ecd->scd", chosen, padded, preferred_element_type=jnp.float32
+    ).astype(buffer_rows.dtype)
     return picked_rows.reshape(devices, span_count, CAP, MODEL_WIDTH)
 
 
@@ -406,34 +413,975 @@
     )
 
 
+D = MODEL_WIDTH
+SRC = 8
+STEPS = 4
+M = SRC * CAP
+F32, BF16 = jnp.float32, jnp.bfloat16
+
+def nt(a, b):
+    return lax.dot_general(a, b, (((1,), (1,)), ((), ())), preferred_element_type=F32)
+def nn(a, b):
+    return lax.dot_general(a, b, (((1,), (0,)), ((), ())), preferred_element_type=F32)
+def tn(a, b):
+    return lax.dot_general(a, b, (((0,), (0,)), ((), ())), preferred_element_type=F32)
+
+QUARTER, DOWN_WHOLE, DOWN_QUARTER, OWN_WIDTH = 0, 256, 768, 896
+
+def expert_kernel(own_ref, t_ref, c_ref, pick_ref, router_ref, wf_ref, wo_ref, out_ref, gin_ref, gg_ref, dwf_ref, dwo_ref,
+                  x_ref, g_ref, rw_ref, act_ref, dgu_ref, actq_ref, dguq_ref, ow_ref, gi_ref):
+    i = pl.program_id(0)
+    mine = (own_ref[0], own_ref[1])
+    logits = nt(router_ref[...], t_ref[...])
+    row = lax.broadcasted_iota(jnp.int32, logits.shape, 0)
+    logits = jnp.where(row < E, logits, -jnp.inf)
+    e = jnp.exp(logits - jnp.max(logits, axis=0, keepdims=True))
+    probs = e / jnp.sum(e, axis=0, keepdims=True)
+    mineprob = [jnp.sum(jnp.where(row == m, probs, 0.0), axis=0, keepdims=True) for m in mine]
+    at = pl.ds(pl.multiple_of(i * M, M), M)
+    for s in range(SRC):
+        pick = pick_ref[s * 64:s * 64 + 64, :]
+        xs = nn(pick, t_ref[s * 128:s * 128 + 128, :]).astype(BF16)
+        gs = nn(pick, c_ref[s * 128:s * 128 + 128, :]).astype(BF16)
+        wide = pick.astype(F32)
+        for k in range(2):
+            to = pl.ds(pl.multiple_of(i * M + s * CAP, CAP), CAP)
+            x_ref[k, to, :] = xs[k * 32:k * 32 + 32]
+            g_ref[k, to, :] = gs[k * 32:k * 32 + 32]
+            rw_ref[k, s * CAP:s * CAP + CAP, :] = jnp.broadcast_to(jnp.sum(wide[k * 32:k * 32 + 32] * mineprob[k][:, s * 128:(s + 1) * 128], axis=1, keepdims=True), (CAP, 128))
+    gws = []
+    sets = (
+        (act_ref, dgu_ref, 512, wf_ref[...], wo_ref[:, DOWN_WHOLE:DOWN_WHOLE + 512]),
+        (actq_ref, dguq_ref, 128, wo_ref[:, QUARTER:QUARTER + 256], wo_ref[:, DOWN_QUARTER:DOWN_QUARTER + 128]),
+    )
+    for k, (acts, dgus, w, w_gu, w_d) in enumerate(sets):
+        pre = nn(x_ref[k, at, :], w_gu)
+        gate, up = pre[:, :w], pre[:, w:]
+        sig = jax.nn.sigmoid(gate)
+        silu = gate * sig
+        act = silu * up
+        share = rw_ref[k, :, 0:1] * RESIDUAL_SCALE
+        scaled = (share * act).astype(BF16)
+        acts[at, :] = scaled
+        da = nn(g_ref[k, at, :], w_d)
+        gws.append(RESIDUAL_SCALE * jnp.sum(act.astype(BF16).astype(F32) * da, axis=1, keepdims=True))
+        ow_ref[k] = nt(scaled, w_d).astype(BF16)
+        da = share * da
+        dgu = jnp.concatenate([(da * up * sig * (1.0 + gate * (1.0 - sig))).astype(BF16), (da * silu).astype(BF16)], axis=1)
+        dgus[at, :] = dgu
+        gi_ref[k] = nt(dgu, w_gu).astype(BF16)
+    for s in range(SRC):
+        r = slice(s * CAP, s * CAP + CAP)
+        pick = pick_ref[s * 64:s * 64 + 64, :]
+        to = slice(s * 128, s * 128 + 128)
+        out_ref[to, :] = tn(pick, jnp.concatenate([ow_ref[0, r, :], ow_ref[1, r, :]], axis=0)).astype(BF16)
+        gin_ref[to, :] = tn(pick, jnp.concatenate([gi_ref[0, r, :], gi_ref[1, r, :]], axis=0)).astype(BF16)
+        wide = pick.astype(F32)
+        for k in range(2):
+            gg_ref[s, k:k + 1, :] = jnp.sum(wide[k * 32:k * 32 + 32] * gws[k][r], axis=0, keepdims=True)
+        gg_ref[s, 2:8, :] = jnp.zeros((6, 128), F32)
+
+    @pl.when(i == STEPS - 1)
+    def _():
+        def body(j, carry):
+            c = pl.ds(pl.multiple_of(j * 256, 256), 256)
+            dwf_ref[c, :] = tn(x_ref[0, :, c], dgu_ref[...]).astype(BF16)
+            dwo_ref[c, QUARTER:QUARTER + 256] = tn(x_ref[1, :, c], dguq_ref[...]).astype(BF16)
+            dwo_ref[c, DOWN_WHOLE:DOWN_WHOLE + 512] = tn(g_ref[0, :, c], act_ref[...]).astype(BF16)
+            dwo_ref[c, DOWN_QUARTER:DOWN_QUARTER + 128] = tn(g_ref[1, :, c], actq_ref[...]).astype(BF16)
+            return carry
+        lax.fori_loop(0, D // 256, body, 0)
+
+def experts(owned, tokens, cot, picks, router_t, wf, wo):
+    R = SRC * 128
+    once = lambda shape: pl.BlockSpec(shape, lambda i: (0, 0), pipeline_mode=pl.Buffered(1))
+    rows = pl.BlockSpec((R, D), lambda i: (i, 0))
+    vmem = lambda *shape, dtype=BF16: pltpu.VMEM(shape, dtype)
+    return pl.pallas_call(
+        expert_kernel,
+        grid=(STEPS,),
+        in_specs=[
+            pl.BlockSpec(memory_space=pltpu.SMEM), rows, rows, pl.BlockSpec((SRC * 64, 128), lambda i: (i, 0)),
+            once((64, D)), once((D, 2 * F)), once((D, OWN_WIDTH)),
+        ],
+        out_specs=[rows, rows, pl.BlockSpec((SRC, 8, 128), lambda i: (i, 0, 0)), once((D, 2 * F)), once((D, OWN_WIDTH))],
+        out_shape=[
+            jax.ShapeDtypeStruct((4096, D), BF16), jax.ShapeDtypeStruct((4096, D), BF16), jax.ShapeDtypeStruct((32, 8, 128), F32),
+            jax.ShapeDtypeStruct((D, 2 * F), BF16), jax.ShapeDtypeStruct((D, OWN_WIDTH), BF16),
+        ],
+        scratch_shapes=[
+            vmem(2, 1024, D), vmem(2, 1024, D), vmem(2, M, 128, dtype=F32),
+            vmem(1024, 512), vmem(1024, 1024), vmem(1024, 128), vmem(1024, 256), vmem(2, M, D), vmem(2, M, D),
+        ],
+        compiler_params=pltpu.CompilerParams(vmem_limit_bytes=62 * 2**20),
+        cost_estimate=pl.CostEstimate(flops=22 * 10**9, bytes_accessed=62 * 10**6, transcendentals=0),
+    )(owned, tokens, cot, picks, router_t, wf, wo)
+
+
+MESH = pl.DeviceIdType.MESH
+DEVICES = 32
+TURNS = tuple(sorted(range(1, DEVICES), key=lambda k: (k % 8 * 5 % 8, k)))
+DMA = pltpu.SemaphoreType.DMA
+
+
+def dev(z, y, x, c):
+    return ((z * 2 + y) * 2 + x) * 2 + c
+
+
+class Place:
+    def __init__(self):
+        me = lax.axis_index("fsdp")
+        self.me = me
+        z, y, x, c = me // 8, lax.rem(me // 4, 2), lax.rem(me // 2, 2), lax.rem(me, 2)
+        self.z, self.y, self.x, self.c = z, y, x, c
+        self.sib, self.xn, self.yn = dev(z, y, x, 1 - c), dev(z, y, 1 - x, c), dev(z, 1 - y, x, c)
+        self.up, self.down = dev(z + 1, y, x, c), dev(z - 1, y, x, c)
+        table = ((0, 1, 2, 3), (1, 0, 2, 3), (2, 3, 1, 0), (3, 2, 1, 0))
+        self.zq = []
+        for q in range(4):
+            v = jnp.int32(table[0][q])
+            for k in range(1, 4):
+                v = jnp.where(z == k, table[k][q], v)
+            self.zq.append(v)
+
+
+def greet_all():
+    me = lax.axis_index("fsdp")
+    barrier = pltpu.get_barrier_semaphore()
+    for k in range(1, DEVICES):
+        pl.semaphore_signal(barrier, inc=1, device_id=(lax.rem(me + k, DEVICES),), device_id_type=MESH)
+    pl.semaphore_wait(barrier, DEVICES - 1)
+
+
+def rc(src, dst, ss, rs, to):
+    return pltpu.make_async_remote_copy(src_ref=src, dst_ref=dst, send_sem=ss, recv_sem=rs, device_id=(to,), device_id_type=MESH)
+
+
+class Direct:
+    def __init__(self, pieces, refs, sems):
+        self.pieces, self.refs, (self.ss, self.rs, self.ls) = pieces, refs, sems
+        self.me = lax.axis_index("fsdp")
+        self.left = list(TURNS)
+
+    @staticmethod
+    def scratch(count):
+        return [DMA((DEVICES, count)), DMA((DEVICES, count)), DMA((count,))]
+
+    def own(self):
+        self.local = [pltpu.make_async_copy(a, b, self.ls.at[i]) for i, (a, b) in enumerate(self.pieces(self.me, self.me, self.refs))]
+        for l in self.local:
+            l.start()
+
+    def start(self, number):
+        turns, self.left = self.left[:number], self.left[number:]
+        for k in turns:
+            to = lax.rem(self.me + k, DEVICES)
+            for i, (a, b) in enumerate(self.pieces(self.me, to, self.refs)):
+                rc(a, b, self.ss.at[k, i], self.rs.at[k, i], to).start()
+
+    def finish(self):
+        self.start(DEVICES)
+        for k in TURNS:
+            src = lax.rem(self.me + DEVICES - k, DEVICES)
+            for i, (a, b) in enumerate(self.pieces(src, self.me, self.refs)):
+                rc(a, b, self.ss.at[k, i], self.rs.at[k, i], src).wait_recv()
+        for k in TURNS:
+            to = lax.rem(self.me + k, DEVICES)
+            for i, (a, b) in enumerate(self.pieces(self.me, to, self.refs)):
+                rc(a, b, self.ss.at[k, i], self.rs.at[k, i], to).wait_send()
+        for l in self.local:
+            l.wait()
+
+
+class Gather:
+    ORDER = ((1, 0), (1, 1), (2, 0), (1, 2), (2, 1), (3, 0), (1, 3), (2, 2), (3, 1), (2, 3), (3, 2), (3, 3))
+
+    def __init__(self, p, parts, shards, outs, sems):
+        self.p, self.parts, self.shards, self.outs, self.sems = p, parts, shards, outs, sems
+        self.P, self.sends, self.locals = len(parts), [], []
+        self.left = list(self.ORDER)
+
+    @staticmethod
+    def scratch(arrays, parts):
+        P = len(parts)
+        return [DMA((arrays,)), DMA((4, P)), DMA((P,))] + [DMA((4, P))] * 7 + [DMA((4, 4, P))] * 2
+
+    def at(self, i, d):
+        a, c0, w, _ = self.parts[i]
+        rows = self.shards[a].shape[0]
+        return self.outs[a].at[pl.ds(pl.multiple_of(d * rows, rows), rows), pl.ds(c0, w)]
+
+    def spot(self, i, q, k, core):
+        p = self.p
+        flip_x, flip_y = ((0, 0), (1, 0), (0, 1), (1, 1))[k] if self.parts[i][3] == 0 else ((0, 0), (0, 1), (1, 0), (1, 1))[k]
+        return self.at(i, dev(p.zq[q], 1 - p.y if flip_y else p.y, 1 - p.x if flip_x else p.x, core))
+
+    def go(self, copy):
+        copy.start()
+        self.sends.append(copy)
+
+    def step(self, number=1):
+        for f, q in self.left[:number]:
+            (self.stage1, self.stage2, self.stage3)[f - 1](q)
+        self.left = self.left[number:]
+
+    def stage1(self, q):
+        p = self.p
+        _, zs, zs2, zr, fs, fr, s1s, s1r, s2s, s2r, cs, cr = self.sems
+        for i in range(self.P):
+            a, c0, w, mode = self.parts[i]
+            first, second = (p.xn, p.yn) if mode == 0 else (p.yn, p.xn)
+            here = self.spot(i, q, 0, p.c)
+            if q == 0:
+                src = self.shards[a].at[:, pl.ds(c0, w)]
+
+                @pl.when(p.z < 3)
+                def _():
+                    rc(src, here, zs.at[0, i], zr.at[p.z, i], p.up).start()
+
+                @pl.when(p.z > 0)
+                def _():
+                    rc(src, here, zs2.at[i], zr.at[p.z, i], p.down).start()
+            else:
+                src, zq = here, p.zq[q]
+                rc(here, here, zs.at[q, i], zr.at[zq, i], p.up).wait_recv()
+
+                @pl.when((zq < p.z) & (p.z < 3))
+                def _():
+                    rc(src, here, zs.at[q, i], zr.at[zq, i], p.up).start()
+
+                @pl.when((zq > p.z) & (p.z > 0))
+                def _():
+                    rc(src, here, zs.at[q, i], zr.at[zq, i], p.down).start()
+            self.go(rc(src, here, fs.at[q, i], fr.at[q, i], first))
+            self.go(rc(src, here, s1s.at[q, i], s1r.at[q, i], second))
+            self.go(rc(src, here, cs.at[0, q, i], cr.at[0, q, i], p.sib))
+        if q == 0:
+            for a, (shard, out) in enumerate(zip(self.shards, self.outs)):
+                rows = shard.shape[0]
+                l = pltpu.make_async_copy(shard, out.at[pl.ds(pl.multiple_of(p.me * rows, rows), rows)], self.sems[0].at[a])
+                l.start()
+                self.locals.append(l)
+
+    def stage2(self, q):
+        p = self.p
+        fs, fr, s2s, s2r, cs, cr = self.sems[4:6] + self.sems[8:12]
+        for i in range(self.P):
+            second = p.yn if self.parts[i][3] == 0 else p.xn
+            there = self.spot(i, q, 1, p.c)
+            rc(there, there, fs.at[q, i], fr.at[q, i], second).wait_recv()
+            self.go(rc(there, there, s2s.at[q, i], s2r.at[q, i], second))
+            self.go(rc(there, there, cs.at[1, q, i], cr.at[1, q, i], p.sib))
+
+    def stage3(self, q):
+        p = self.p
+        cs, cr = self.sems[10:12]
+        for k, (ss, rs) in ((2, self.sems[6:8]), (3, self.sems[8:10])):
+            for i in range(self.P):
+                there = self.spot(i, q, k, p.c)
+                rc(there, there, ss.at[q, i], rs.at[q, i], p.sib).wait_recv()
+                self.go(rc(there, there, cs.at[k, q, i], cr.at[k, q, i], p.sib))
+
+    def arrived(self):
+        self.step(12)
+        cs, cr = self.sems[10:12]
+        for q in range(4):
+            for k in range(4):
+                for i in range(self.P):
+                    there = self.spot(i, q, k, 1 - self.p.c)
+                    rc(there, there, cs.at[k, q, i], cr.at[k, q, i], self.p.sib).wait_recv()
+        for l in self.locals:
+            l.wait()
+
+    def finish(self):
+        p = self.p
+        zs, zs2, zr = self.sems[1:4]
+        for copy in self.sends:
+            copy.wait_send()
+        for i in range(self.P):
+            here = self.at(i, p.me)
+
+            @pl.when(p.z < 3)
+            def _():
+                rc(here, here, zs.at[0, i], zr.at[p.z, i], p.up).wait_send()
+
+            @pl.when(p.z > 0)
+            def _():
+                rc(here, here, zs2.at[i], zr.at[p.z, i], p.down).wait_send()
+
+            for q in range(1, 4):
+                zq = p.zq[q]
+
+                @pl.when(((zq < p.z) & (p.z < 3)) | ((zq > p.z) & (p.z > 0)))
+                def _():
+                    rc(here, here, zs.at[q, i], zr.at[zq, i], p.up).wait_send()
+
+
+class Scatter:
+    ORDER = ((1, 3), (1, 2), (2, 3), (1, 1), (2, 2), (3, 3), (1, 0), (2, 1), (3, 2), (2, 0), (3, 1), (3, 0))
+    STEP = 16
+
+    def __init__(self, p, parts, fulls, outs, spaces, sems, in_place=False):
+        self.p, self.parts, self.fulls, self.outs, self.sems, self.in_place = p, parts, fulls, outs, sems, in_place
+        count = len(fulls)
+        if in_place:
+            spaces = (None,) * count + tuple(spaces)
+        self.held, self.r0, self.r1, self.r2, self.r3 = (spaces[i * count : (i + 1) * count] for i in range(5))
+        self.rows = [f.shape[0] // DEVICES for f in fulls]
+        self.P, self.sends, self.loads = len(parts), [], {}
+        self.left = list(self.ORDER)
+
+    @staticmethod
+    def scratch(arrays, parts, in_place=False):
+        P = len(parts)
+        spaces = []
+        for cnt in (16, 8, 4, 5) if in_place else (16, 16, 8, 4, 5):
+            spaces += [pltpu.VMEM((cnt, a.shape[0] // DEVICES, a.shape[1]), a.dtype) for a in arrays]
+        return spaces, [DMA((4, 4, P))] * 3 + [DMA((4, 2, P))] * 2 + [DMA((4, P))] * 3 + [DMA((5, P))]
+
+    def go(self, copy):
+        copy.start()
+        self.sends.append(copy)
+
+    def cut(self, i):
+        return pl.ds(self.parts[i][1], self.parts[i][2])
+
+    def spot(self, i, k):
+        x, y = self.p.x, self.p.y
+        if self.parts[i][3] == 0:
+            return ((1 - y, 1 - x), (1 - y, x), (y, 1 - x), (y, x))[k]
+        return ((1 - y, 1 - x), (y, 1 - x), (1 - y, x), (y, x))[k]
+
+    def slot(self, q, yy, xx):
+        return (yy * 2 + xx) * 4 + self.p.zq[q]
+
+    def hold(self, a, q, yy, xx):
+        if self.in_place:
+            start = dev(self.p.zq[q], yy, xx, self.p.c) * self.rows[a]
+            return self.fulls[a].at[pl.ds(pl.multiple_of(start, self.rows[a]), self.rows[a])]
+        return self.held[a].at[self.slot(q, yy, xx)]
+
+    def source(self, i, q, k, core):
+        a = self.parts[i][0]
+        d = dev(self.p.zq[q], *self.spot(i, k), core)
+        return self.fulls[a].at[pl.ds(pl.multiple_of(d * self.rows[a], self.rows[a]), self.rows[a]), self.cut(i)]
+
+    def begin(self, only=None):
+        ls, s0, e0 = self.sems[:3]
+        for q in (3, 2, 1, 0):
+            for k in range(4):
+                for i in range(self.P):
+                    a = self.parts[i][0]
+                    if only is not None and a not in only:
+                        continue
+                    s = self.slot(q, *self.spot(i, k))
+                    self.go(rc(self.source(i, q, k, 1 - self.p.c), self.r0[a].at[s, :, self.cut(i)], s0.at[q, k, i], e0.at[q, k, i], self.p.sib))
+                    if not self.in_place:
+                        l = pltpu.make_async_copy(self.source(i, q, k, self.p.c), self.held[a].at[s, :, self.cut(i)], ls.at[q, k, i])
+                        l.start()
+                        self.loads[q, k, i] = l
+
+    def step(self, number=1):
+        for f, q in self.left[:number]:
+            (self.stage1, self.stage2, self.stage3)[f - 1](q)
+        self.left = self.left[number:]
+
+    def chunks(self, a, body):
+        def one(n, carry):
+            body(pl.ds(pl.multiple_of(n * self.STEP, self.STEP), self.STEP))
+            return carry
+
+        lax.fori_loop(0, self.rows[a] // self.STEP, one, 0)
+
+    def add(self, i, dst, src, s_src):
+        a, c0, w, _ = self.parts[i]
+
+        def body(r):
+            v = dst[r, c0 : c0 + w].astype(F32) + src[s_src, r, c0 : c0 + w].astype(F32)
+            dst[r, c0 : c0 + w] = v.astype(dst.dtype)
+
+        self.chunks(a, body)
+
+    def stage1(self, q):
+        p = self.p
+        _, s0, e0, s1, e1 = self.sems[:5]
+        for k in range(4):
+            for i in range(self.P):
+                a = self.parts[i][0]
+                first = p.yn if self.parts[i][3] == 0 else p.xn
+                s = self.slot(q, *self.spot(i, k))
+                sums = self.hold(a, q, *self.spot(i, k))
+                here = sums.at[:, self.cut(i)]
+                rc(here, self.r0[a].at[s, :, self.cut(i)], s0.at[q, k, i], e0.at[q, k, i], p.sib).wait_recv()
+                if not self.in_place:
+                    self.loads[q, k, i].wait()
+                self.add(i, sums, self.r0[a], s)
+                if k < 2:
+                    self.go(rc(here, self.r1[a].at[q * 2 + k, :, self.cut(i)], s1.at[q, k, i], e1.at[q, k, i], first))
+
+    def stage2(self, q):
+        p = self.p
+        s1, e1, s2, e2 = self.sems[3:7]
+        for k in range(2):
+            for i in range(self.P):
+                a = self.parts[i][0]
+                second = p.xn if self.parts[i][3] == 0 else p.yn
+                sums = self.hold(a, q, *self.spot(i, k + 2))
+                here = sums.at[:, self.cut(i)]
+                rc(here, self.r1[a].at[q * 2 + k, :, self.cut(i)], s1.at[q, k, i], e1.at[q, k, i], p.sib).wait_recv()
+                self.add(i, sums, self.r1[a], q * 2 + k)
+                if k == 0:
+                    self.go(rc(here, self.r2[a].at[q, :, self.cut(i)], s2.at[q, i], e2.at[q, i], second))
+
+    def stage3(self, q):
+        p = self.p
+        s2, e2, s3, e3 = self.sems[5:9]
+        zq, z = p.zq[q], p.z
+        for i in range(self.P):
+            a, c0, w, _ = self.parts[i]
+            r3, out, sums = self.r3[a], self.outs[a], self.hold(a, q, p.y, p.x)
+            here = sums.at[:, self.cut(i)]
+            rc(here, self.r2[a].at[q, :, self.cut(i)], s2.at[q, i], e2.at[q, i], p.sib).wait_recv()
+            self.add(i, sums, self.r2[a], q)
+            if q > 0:
+
+                @pl.when((zq > z) & (z > 0) | (zq < z) & (z < 3))
+                def _():
+                    rc(here, r3.at[zq, :, self.cut(i)], s3.at[q, i], e3.at[zq, i], p.sib).wait_recv()
+                    self.add(i, sums, r3, zq)
+
+                @pl.when(zq > z)
+                def _():
+                    rc(here, r3.at[zq, :, self.cut(i)], s3.at[q, i], e3.at[zq, i], p.up).start()
+
+                @pl.when((zq < z) & (zq == z - 1))
+                def _():
+                    rc(here, r3.at[4, :, self.cut(i)], s3.at[q, i], e3.at[4, i], p.down).start()
+
+                @pl.when(zq < z - 1)
+                def _():
+                    rc(here, r3.at[zq, :, self.cut(i)], s3.at[q, i], e3.at[zq, i], p.down).start()
+            else:
+
+                def first_sum(r):
+                    out[r, c0 : c0 + w] = sums[r, c0 : c0 + w].astype(F32)
+
+                self.chunks(a, first_sum)
+                for cond, where in ((z > 0, z), (z < 3, 4)):
+
+                    @pl.when(cond)
+                    def _():
+                        rc(here, r3.at[where, :, self.cut(i)], s3.at[q, i], e3.at[where, i], p.sib).wait_recv()
+
+                        def more(r):
+                            out[r, c0 : c0 + w] += r3[where, r, c0 : c0 + w].astype(F32)
+
+                        self.chunks(a, more)
+
+    def finish(self):
+        p = self.p
+        s3, e3 = self.sems[7:9]
+        for copy in self.sends:
+            copy.wait_send()
+        for q in range(1, 4):
+            for i in range(self.P):
+                here = self.hold(self.parts[i][0], q, p.y, p.x).at[:, self.cut(i)]
+                rc(here, here, s3.at[q, i], e3.at[0, i], p.sib).wait_send()
+
+
+HBM = pl.BlockSpec(memory_space=pl.ANY)
+VMEM = pl.BlockSpec(memory_space=pltpu.VMEM)
+
+
+def like(*shape, dtype=None):
+    return jax.ShapeDtypeStruct(shape, dtype or jnp.bfloat16)
+
+
+def cut_up(refs, *counts):
+    out, i = [], 0
+    for c in counts:
+        out.append(refs[i : i + c])
+        i += c
+    return out + [refs[i:]]
+
+
+GROUP = QUERY_HEADS // KEY_VALUE_HEADS
+Q_WIDTH, K_WIDTH = QUERY_HEADS * HEAD_WIDTH, KEY_VALUE_HEADS * HEAD_WIDTH
+TOK = 128
+
+
+def partner(v):
+    lane = lax.broadcasted_iota(jnp.int32, v.shape, 1) % HEAD_WIDTH
+    return jnp.where(lane < HEAD_WIDTH // 2, pltpu.roll(v, 96, 1), pltpu.roll(v, 32, 1))
+
+
+def attention_forward(x_ref, cos_ref, sin_ref, bias_ref, qkv_ref, out_ref, small_ref, r):
+    def norm_one():
+        r.small_t[...] = nt(jnp.eye(TOK, dtype=BF16), small_ref[...])
+        x = x_ref[...].astype(F32)
+        r.n1[...] = (x * norm_scale(x) * r.small_t[E : E + 1, :]).astype(BF16)
+
+    def project(t):
+        def run():
+            tile = nn(r.n1[...], qkv_ref[:, t * 512 : t * 512 + 512])
+            for b in range(4):
+                col = t * 512 + b * 128
+                v = tile[:, b * 128 : b * 128 + 128]
+                if col < Q_WIDTH + K_WIDTH:
+                    v = v * cos_ref[...] + partner(v) * sin_ref[...]
+                v = v.astype(BF16)
+                for half in range(2):
+                    piece = v[:, half * 64 : half * 64 + 64]
+                    head = col // 64 + half
+                    if col < Q_WIDTH:
+                        r.q[head // GROUP, head % GROUP * TOK : head % GROUP * TOK + TOK, :] = piece
+                    elif col < Q_WIDTH + K_WIDTH:
+                        r.k[head - QUERY_HEADS] = piece
+                    else:
+                        r.v[head - QUERY_HEADS - KEY_VALUE_HEADS] = piece
+
+        return run
+
+    def attend(j):
+        def run():
+            s = nt(r.q[j], r.k[j]) * ATTN_SCALE
+            s = s + jnp.concatenate([bias_ref[...]] * GROUP, axis=0)
+            e = jnp.exp(s - jnp.max(s, axis=1, keepdims=True))
+            probs = e / jnp.sum(e, axis=1, keepdims=True)
+            r.probs[j] = probs
+            o = nn(probs.astype(BF16), r.v[j]).astype(BF16)
+            for g in range(GROUP):
+                h = j * GROUP + g
+                r.att[:, h * 64 : h * 64 + 64] = o[g * TOK : g * TOK + TOK]
+
+        return run
+
+    def output(t):
+        def run():
+            c = slice(t * 512, t * 512 + 512)
+            r.middle[:, c] = x_ref[:, c].astype(F32) + RESIDUAL_SCALE * nn(r.att[...], out_ref[:, c])
+
+        return run
+
+    def norm_two():
+        m = r.middle[...]
+        r.n2[...] = (m * norm_scale(m) * r.small_t[E + 1 : E + 2, :]).astype(BF16)
+
+    return (
+        [norm_one]
+        + [project(t) for t in range((Q_WIDTH + 2 * K_WIDTH) // 512)]
+        + [attend(j) for j in range(KEY_VALUE_HEADS)]
+        + [output(t) for t in range(D // 512)]
+        + [norm_two]
+    )
+
+
+def split_dot(form, a, b):
+    one = b.astype(BF16)
+    rest = b - one.astype(F32)
+    two = rest.astype(BF16)
+    three = (rest - two.astype(F32)).astype(BF16)
+    return form(a, one) + form(a, two) + form(a, three)
+
+
+def norm_back_rows(hidden, gain, upstream):
+    scale = norm_scale(hidden)
+    weighted = upstream * gain
+    inner = jnp.mean(weighted * hidden, axis=-1, keepdims=True)
+    return scale * weighted - hidden * scale**3 * inner, upstream * hidden * scale
+
+
+def attention_backward(x_ref, cot_ref, gin_ref, gates_ref, cos_ref, sin_ref, qkv_ref, out_ref, r, put_qkv, put_out, put_small):
+    def router():
+        m = r.middle[...]
+        logits = nt(r.small_t[:64, :].astype(BF16), r.n2[...])
+        row = lax.broadcasted_iota(jnp.int32, logits.shape, 0)
+        logits = jnp.where(row < E, logits, -jnp.inf)
+        e = jnp.exp(logits - jnp.max(logits, axis=0, keepdims=True))
+        probs = e / jnp.sum(e, axis=0, keepdims=True)
+        gates = gates_ref[...]
+        gl = probs * (gates - jnp.sum(probs * gates, axis=0, keepdims=True))
+        gl = jnp.where(row < E, gl, 0.0)
+        gl = jnp.concatenate([gl, jnp.zeros((64, TOK), F32)], axis=0).T
+        r.gl[...] = gl
+        back = nn(gl.astype(BF16), r.small_t[...].astype(BF16))
+        low = gl - gl.astype(BF16).astype(F32)
+        back = back + nn(low.astype(BF16), r.small_t[...].astype(BF16))
+        low = low - low.astype(BF16).astype(F32)
+        back = back + nn(low.astype(BF16), r.small_t[...].astype(BF16))
+        up = gin_ref[...] + back
+        gm, gain_rows = norm_back_rows(m, r.small_t[E + 1 : E + 2, :], up)
+        gm = gm + cot_ref[...].astype(F32)
+        r.gm[...] = gm
+        r.gain2[...] = gain_rows
+        r.branch[...] = (RESIDUAL_SCALE * gm).astype(BF16)
+
+    def attended(t):
+        def run():
+            c = slice(t * 512, t * 512 + 512)
+            r.ga[:, c] = nt(r.branch[...], out_ref[c, :]).astype(BF16)
+
+        return run
+
+    def out_part(t):
+        def run():
+            put_out(t, tn(r.att[:, t * 256 : t * 256 + 256], r.branch[...]).astype(BF16))
+
+        return run
+
+    def head(j):
+        def run():
+            cols = [slice((j * GROUP + g) * 64, (j * GROUP + g) * 64 + 64) for g in range(GROUP)]
+            ga = jnp.concatenate([r.ga[:, c] for c in cols], axis=0)
+            at = jnp.concatenate([r.att[:, c] for c in cols], axis=0)
+            delta = jnp.sum(ga.astype(F32) * at.astype(F32), axis=1, keepdims=True)
+            probs = r.probs[j]
+            ds = (probs * (nt(ga, r.v[j]) - delta) * ATTN_SCALE).astype(BF16)
+            gq = nn(ds, r.k[j])
+            for g, c in enumerate(cols):
+                r.gjf[:, c] = gq[g * TOK : g * TOK + TOK]
+            r.gjf[:, Q_WIDTH + j * 64 : Q_WIDTH + j * 64 + 64] = tn(ds, r.q[j])
+            r.gjf[:, Q_WIDTH + K_WIDTH + j * 64 : Q_WIDTH + K_WIDTH + j * 64 + 64] = tn(probs.astype(BF16), ga)
+
+        return run
+
+    def rotate():
+        for col in range(0, Q_WIDTH + 2 * K_WIDTH, 128):
+            v = r.gjf[:, col : col + 128]
+            if col < Q_WIDTH + K_WIDTH:
+                v = v * cos_ref[...] - partner(v) * sin_ref[...]
+            r.gj[:, col : col + 128] = v.astype(BF16)
+
+    def qkv_part(t):
+        def run():
+            put_qkv(t, tn(r.n1[:, t * 256 : t * 256 + 256], r.gj[...]).astype(BF16))
+
+        return run
+
+    def into_normed(t):
+        def run():
+            c = slice(t * 256, t * 256 + 256)
+            r.gn[:, c] = nt(r.gj[...], qkv_ref[c, :])
+
+        return run
+
+    def input_back():
+        x = x_ref[...].astype(F32)
+        gx, gain_rows = norm_back_rows(x, r.small_t[E : E + 1, :], r.gn[...])
+        r.input_grad[...] = (gx + r.gm[...]).astype(BF16)
+        lane = lax.broadcasted_iota(jnp.int32, (TOK, TOK), 1)
+        small = split_dot(tn, r.n2[...], r.gl[...])
+        for rows, at in ((gain_rows, E), (r.gain2[...], E + 1)):
+            ones = jnp.where(lane == at, 1.0, 0.0).astype(BF16)
+            hi = rows.astype(BF16)
+            lo = (rows - hi.astype(F32)).astype(BF16)
+            small = small + tn(hi, ones) + tn(lo, ones)
+        put_small(small.astype(BF16))
+
+    first = [router] + [attended(t) for t in range(3)] + [out_part(t) for t in range(6)]
+    heads = [head(j) for j in range(KEY_VALUE_HEADS)] + [rotate]
+    last = [into_normed(t) for t in range(6)] + [input_back] + [qkv_part(t) for t in range(6)]
+    return first, heads, last
+
+
+class Results:
+    pass
+
+
+ATT_NAMES = ("small_t", "n1", "q", "k", "v", "probs", "att", "middle", "n2")
+ATT_SHAPES = (
+    ((TOK, D), F32),
+    ((TOK, D), BF16),
+    ((KEY_VALUE_HEADS, GROUP * TOK, HEAD_WIDTH), BF16),
+    ((KEY_VALUE_HEADS, TOK, HEAD_WIDTH), BF16),
+    ((KEY_VALUE_HEADS, TOK, HEAD_WIDTH), BF16),
+    ((KEY_VALUE_HEADS, GROUP * TOK, TOK), F32),
+    ((TOK, Q_WIDTH), BF16),
+    ((TOK, D), F32),
+    ((TOK, D), BF16),
+)
+ROW_HALVES = ((0, 0, 768, 0), (0, 768, 768, 1))
+DENSE_PARTS = ((0, 0, 1280, 0), (0, 1280, 1280, 1), (1, 0, 768, 0), (1, 768, 768, 1), (2, 0, 128, 1))
+FIRST_PARTS = DENSE_PARTS + ((3, 0, 128, 0),)
+
+
+def lanes(start):
+    return pl.ds(pl.multiple_of(start, 128), 128)
+
+
+def weights_out(src, dst, refs):
+    g_ref, d_ref, wf_ref, wo_ref = refs
+    group, own, quarter = dst // 4, lax.rem(dst, 4), lax.rem(dst, 4) * 128
+    rows = pl.ds(pl.multiple_of(src * 48, 48), 48)
+    fifth = group * 5 + 4
+    return (
+        (g_ref.at[fifth, :, lanes(quarter)], wo_ref.at[rows, pl.ds(QUARTER, 128)]),
+        (g_ref.at[fifth, :, lanes(F + quarter)], wo_ref.at[rows, pl.ds(QUARTER + 128, 128)]),
+        (d_ref.at[group * 5 + own], wo_ref.at[rows, pl.ds(DOWN_WHOLE, F)]),
+        (d_ref.at[fifth, :, lanes(quarter)], wo_ref.at[rows, pl.ds(DOWN_QUARTER, 128)]),
+        (g_ref.at[group * 5 + own], wf_ref.at[rows]),
+    )
+
+
+def down_back(src, dst, refs):
+    dwo_ref, gates_ref, d_ref, all_gates_ref = refs
+    group, quarter = src // 4, lax.rem(src, 4) * 128
+    rows = pl.ds(pl.multiple_of(dst * 48, 48), 48)
+    return (
+        (gates_ref.at[dst], all_gates_ref.at[src]),
+        (dwo_ref.at[rows, pl.ds(DOWN_WHOLE, F)], d_ref.at[group * 5 + lax.rem(src, 4)]),
+        (dwo_ref.at[rows, pl.ds(DOWN_QUARTER, 128)], d_ref.at[group * 5 + 4, :, lanes(quarter)]),
+    )
+
+
+def gate_up_back(src, dst, refs):
+    dwf_ref, dwo_ref, g_ref = refs
+    group, quarter = src // 4, lax.rem(src, 4) * 128
+    rows = pl.ds(pl.multiple_of(dst * 48, 48), 48)
+    return (
+        (dwo_ref.at[rows, pl.ds(QUARTER, 128)], g_ref.at[group * 5 + 4, :, lanes(quarter)]),
+        (dwo_ref.at[rows, pl.ds(QUARTER + 128, 128)], g_ref.at[group * 5 + 4, :, lanes(F + quarter)]),
+        (dwf_ref.at[rows], g_ref.at[group * 5 + lax.rem(src, 4)]),
+    )
+
+
+def first_kernel(*refs):
+    (x, cos, sin, bias), dense, (cot,), experts_in, dense_out, (cots, tokens, wf, wo), results, weights, (load_sem,), refs = cut_up(
+        refs, 4, 4, 1, 2, 4, 4, 9, 3, 1
+    )
+    sems1, sems2, sems3, direct_sems, _ = cut_up(refs, 12, 12, 12, 3)
+    greet_all()
+    p = Place()
+    r = Results()
+    for name, ref in zip(ATT_NAMES, results):
+        setattr(r, name, ref)
+    g1 = Gather(p, FIRST_PARTS, dense, dense_out, sems1)
+    g2 = Gather(p, ROW_HALVES, [cot], [cots], sems2)
+    g3 = Gather(p, ROW_HALVES, [r.n2], [tokens], sems3)
+    direct = Direct(weights_out, tuple(experts_in) + (wf, wo), direct_sems)
+    g1.step()
+    direct.own()
+    for n in FIRST_BATCHES:
+        g1.step()
+        direct.start(n)
+    g2.step(2)
+    g1.arrived()
+    loads = [pltpu.make_async_copy(a, b, load_sem.at[i]) for i, (a, b) in enumerate(zip(dense_out[:3], weights))]
+    for l in loads:
+        l.start()
+    g2.step(2)
+    for l in loads:
+        l.wait()
+    for i, chunk in enumerate(attention_forward(x, cos, sin, bias, *weights, r)):
+        chunk()
+        if i % 2 == 1:
+            g2.step()
+            direct.start(SECOND_BATCH)
+    g3.step(2)
+    direct.start(SECOND_BATCH)
+    g2.arrived()
+    g3.step(2)
+    direct.start(DEVICES)
+    g3.arrived()
+    for g in (g1, g2, g3):
+        g.finish()
+    direct.finish()
+
+
+FIRST_BATCHES = (1, 1, 1, 1, 1, 1, 1, 1, 1, 1)
+SECOND_BATCH = 2
+
+
+def first(x, cos, sin, bias, dense, cot, gu, dp):
+    wide = lambda a: like(DEVICES * a.shape[0], a.shape[1], dtype=a.dtype)
+    dense_full = [wide(a) for a in dense]
+    return pl.pallas_call(
+        first_kernel,
+        in_specs=[VMEM] * 4 + [HBM] * 7,
+        out_specs=[HBM] * 8 + [VMEM] * 9,
+        out_shape=dense_full + [wide(cot), wide(cot), like(D, 2 * F), like(D, OWN_WIDTH)] + [like(*s, dtype=t) for s, t in ATT_SHAPES],
+        scratch_shapes=[pltpu.VMEM(a.shape, a.dtype) for a in dense_full[:3]]
+        + [DMA((3,))]
+        + Gather.scratch(4, FIRST_PARTS)
+        + Gather.scratch(1, ROW_HALVES) * 2
+        + Direct.scratch(5),
+        compiler_params=pltpu.CompilerParams(collective_id=0, has_side_effects=True, vmem_limit_bytes=60 * 2**20),
+    )(x, cos, sin, bias, *dense, cot, gu, dp)
+
+
+def middle_kernel(*refs):
+    (gin_part, dwo, gates), (gin, grad_down, all_gates), spaces, sems, direct_sems, _ = cut_up(refs, 3, 3, 5, 9, 3)
+    greet_all()
+    p = Place()
+    s = Scatter(p, ROW_HALVES, [gin_part], [gin], spaces, sems)
+    direct = Direct(down_back, (dwo, gates, grad_down, all_gates), direct_sems)
+    s.begin()
+    direct.own()
+    for n in MIDDLE_BATCHES:
+        s.step()
+        direct.start(n)
+    s.step(12)
+    direct.start(DEVICES)
+    s.finish()
+    direct.finish()
+
+
+MIDDLE_BATCHES = (3, 3, 3, 3, 3, 3, 3, 3, 3, 4)
+
+
+def middle(gin_part, dwo, gates):
+    spaces, sems = Scatter.scratch([gin_part], ROW_HALVES)
+    return pl.pallas_call(
+        middle_kernel,
+        in_specs=[HBM] * 3,
+        out_specs=[VMEM] + [HBM] * 2,
+        out_shape=[like(TOK, D, dtype=F32), like(E, D // DEVICES, F), like(DEVICES, 8, TOK, dtype=F32)],
+        scratch_shapes=spaces + sems + Direct.scratch(3),
+        compiler_params=pltpu.CompilerParams(collective_id=1, has_side_effects=True, vmem_limit_bytes=60 * 2**20),
+    )(gin_part, dwo, gates)
+
+
+WORK = (
+    ("gl", (TOK, TOK), F32),
+    ("gm", (TOK, D), F32),
+    ("gain2", (TOK, D), F32),
+    ("branch", (TOK, D), BF16),
+    ("ga", (TOK, D), BF16),
+    ("gjf", (TOK, Q_WIDTH + 2 * K_WIDTH), F32),
+    ("gj", (TOK, Q_WIDTH + 2 * K_WIDTH), BF16),
+    ("gn", (TOK, D), F32),
+)
+
+
+def last_kernel(*refs):
+    (x, cot, gin, gates, cos, sin), results, (qkv_full, out_full, out_part, dwf, dwo), outs, work, weights, (small_src, load_sem), refs = cut_up(
+        refs, 6, 9, 5, 6, len(WORK), 2, 2
+    )
+    input_grad, combined, qkv_grad, out_grad, small_grad, grad_gu = outs
+    spaces1, sems1, spaces2, sems2, direct_sems, _ = cut_up(refs, 5, 9, 12, 9, 3)
+    greet_all()
+    p = Place()
+    r = Results()
+    for name, ref in zip(ATT_NAMES + tuple(w[0] for w in WORK), tuple(results) + tuple(work)):
+        setattr(r, name, ref)
+    r.input_grad = input_grad
+    qkv_ref, out_ref = weights
+    s1 = Scatter(p, ROW_HALVES, [out_part], [combined], spaces1, sems1)
+    s2 = Scatter(p, DENSE_PARTS, [qkv_ref, out_ref, small_src], [qkv_grad, out_grad, small_grad], spaces2, sems2, in_place=True)
+    direct = Direct(gate_up_back, (dwf, dwo, grad_gu), direct_sems)
+    s1.begin()
+    loads = [pltpu.make_async_copy(a, b, load_sem.at[i]) for i, (a, b) in enumerate(((out_full, out_ref), (qkv_full, qkv_ref)))]
+    for l in loads:
+        l.start()
+    direct.own()
+    direct.start(2)
+
+    def put_qkv(t, value):
+        qkv_ref[t * 256 : t * 256 + 256, :] = value
+
+    def put_out(t, value):
+        out_ref[t * 256 : t * 256 + 256, :] = value
+
+    def put_small(value):
+        small_src[...] = value
+
+    begin, heads, end = attention_backward(x, cot, gin, gates, cos, sin, qkv_ref, out_ref, r, put_qkv, put_out, put_small)
+    for l in loads:
+        l.wait()
+    for i, chunk in enumerate(begin + heads + end):
+        chunk()
+        if i % 3 == 2:
+            s1.step()
+            direct.start(2)
+    s2.begin()
+    s1.step(12)
+    while s2.left:
+        s2.step()
+        direct.start(2)
+    direct.start(DEVICES)
+    s1.finish()
+    s2.finish()
+    direct.finish()
+
+
+def last(x, cot, gin, gates, cos, sin, results, qkv_full, out_full, out_part, dwf, dwo):
+    small = like(D, TOK)
+    spaces1, sems1 = Scatter.scratch([out_part], ROW_HALVES)
+    spaces2, sems2 = Scatter.scratch([qkv_full, out_full, small], DENSE_PARTS, in_place=True)
+    own = D // DEVICES
+    return pl.pallas_call(
+        last_kernel,
+        in_specs=[VMEM] * 15 + [HBM] * 5,
+        out_specs=[VMEM] * 5 + [HBM],
+        out_shape=[
+            like(TOK, D), like(TOK, D, dtype=F32), like(own, qkv_full.shape[1], dtype=F32), like(own, D, dtype=F32),
+            like(own, TOK, dtype=F32), like(E, own, 2 * F),
+        ],
+        scratch_shapes=[pltpu.VMEM(s, t) for _, s, t in WORK]
+        + [pltpu.VMEM(qkv_full.shape, BF16), pltpu.VMEM(out_full.shape, BF16), pltpu.VMEM(small.shape, BF16), DMA((2,))]
+        + spaces1 + sems1 + spaces2 + sems2
+        + Direct.scratch(3),
+        compiler_params=pltpu.CompilerParams(collective_id=2, has_side_effects=True, vmem_limit_bytes=63 * 2**20),
+    )(x, cot, gin, gates, cos, sin, *results, qkv_full, out_full, out_part, dwf, dwo)
+
+
+def fast(
+    layer_input, cotangent, sequence_ids, expert_ids, attention_gain, qkv_weight, output_weight, moe_gain, router, gate_up, down_proj
+):
+    n, own_rows, T = DEVICES, gate_up.shape[0], layer_input.shape[0]
+    me = lax.axis_index("fsdp")
+    small = jnp.concatenate(
+        [router, attention_gain[:, None], moe_gain[:, None], jnp.zeros((own_rows, 86), BF16)], axis=1
+    )
+    cosine, sine = rope_tables(positions(sequence_ids), HEAD_WIDTH)
+    cos = jnp.concatenate([cosine] * 4, axis=1)
+    sin = jnp.concatenate([-sine, sine] * 2, axis=1)
+    place_in = jnp.arange(T, dtype=jnp.int32)
+    allowed = (sequence_ids[:, None] == sequence_ids[None, :]) & (place_in[None, :] <= place_in[:, None])
+    bias = jnp.where(allowed, 0.0, -jnp.inf).astype(F32)
+
+    qkv_full, out_full, small_full, ids_all, cots, tokens, wf, wo, *results = first(
+        layer_input, cos, sin, bias, [qkv_weight, output_weight, small, expert_ids.T], cotangent,
+        jnp.transpose(gate_up, (1, 0, 2)), jnp.transpose(down_proj, (1, 0, 2)),
+    )
+
+    owned = jnp.stack([(me // 4) * 5 + lax.rem(me, 4), (me // 4) * 5 + 4])
+    named = jnp.any(ids_all.reshape(n, TOP, T)[:, :, None, :] == owned[None, None, :, None], axis=1)
+    before = (place_in[:, None] < place_in[None, :]).astype(BF16)
+    ranks = jnp.dot(named.astype(BF16).reshape(2 * n, T), before, preferred_element_type=F32).reshape(n, 2, 1, T)
+    picks = ((ranks == jnp.arange(CAP, dtype=F32)[:, None]) & named[:, :, None, :]).astype(BF16).reshape(n * 64, T)
+    router_t = results[0][:64].astype(BF16)
+    out_part, gin_part, gates, dwf, dwo = experts(owned, tokens, cots, picks, router_t, wf, wo)
+
+    gin, grad_down, gates = middle(gin_part, dwo, gates)
+    gates = gates.reshape(8, 4, 8, T)
+    gates = jnp.concatenate([gates[:, :, 0], jnp.sum(gates[:, :, 1], axis=1, keepdims=True)], axis=1).reshape(E, T)
+    gates = jnp.pad(gates, ((0, 64 - E), (0, 0)))
+    input_grad, combined, qkv_grad, out_grad, small_grad, grad_gu = last(
+        layer_input, cotangent, gin, gates, cos, sin, results, qkv_full, out_full, out_part, dwf, dwo
+    )
+    layer_output = (results[ATT_NAMES.index("middle")] + combined).astype(BF16)
+    gate_up_grad = jnp.transpose(grad_gu, (1, 0, 2)).astype(F32)
+    down_grad = jnp.transpose(grad_down, (1, 0, 2)).astype(F32)
+    return (
+        layer_output,
+        input_grad,
+        small_grad[:, E],
+        qkv_grad,
+        out_grad,
+        small_grad[:, E + 1],
+        small_grad[:, :E],
+        gate_up_grad,
+        down_grad,
+    )
+
+
 def solution(mesh):
-    placed = (
-        P("fsdp", None),
-        P("fsdp", None),
-        P("fsdp"),
-        P("fsdp", None),
-        P("fsdp"),
-        P("fsdp", None),
-        P("fsdp", None),
-        P("fsdp"),
-        P("fsdp", None),
-        P("fsdp", None, None),
-        P("fsdp", None, None),
-    )
+    rows, flat, cube = P("fsdp", None), P("fsdp"), P("fsdp", None, None)
     return jax.shard_map(
-        on_device,
+        fast if mesh.shape["fsdp"] == 32 else on_device,
         mesh=mesh,
-        in_specs=placed,
-        out_specs=(
-            P("fsdp", None),
-            P("fsdp", None),
-            P("fsdp"),
-            P("fsdp", None),
-            P("fsdp", None),
-            P("fsdp"),
-            P("fsdp", None),
-            P("fsdp", None, None),
-            P("fsdp", None, None),
-        ),
+        in_specs=(rows, rows, flat, rows, flat, rows, rows, flat, rows, cube, cube),
+        out_specs=(rows, rows, flat, rows, rows, flat, rows, cube, cube),
         check_vma=False,
     )

time: 2440 us -> 627 us (0.26)
  waiting for transfers between devices: 1010 us -> 0 us
  blocking collectives: 828 us -> 0 us
  Pallas kernels: 0 us -> 574 us
  local copies, waits for them, and re-layouts: 324 us -> 29.6 us
  matrix products: 183 us -> 0.14 us
  other arithmetic: 44.3 us -> 12.6 us
    all_to_all x5 -> x0, waiting for transfers between devices: 1010 us -> none  [the longest x1 425 us: on_device(): lax.all_to_all(owned_grads, 'fsdp', split_axis=0, concat_axis=2, tiled=True)]
    pallas_call x0 -> x4, Pallas kernels: none -> 574 us  [the longest x1 255 us: first(): pl.pallas_call(first_kernel, in_specs=[VMEM] * 4 + [HBM] * 7, out_specs=[...]
    all_gather x1 -> x0, blocking collectives: 385 us -> none  [on_device(): lax.all_gather(router, 'fsdp', axis=0, tiled=True)]
    all_to_all x1 -> x0, blocking collectives: 235 us -> none  [on_device(): lax.all_to_all(send_grad, 'fsdp', split_axis=0, concat_axis=0, tiled=True)]
    unnamed x2 -> x0, blocking collectives: 208 us -> none
    dot_general x26 -> x1, matrix products: 181 us -> 0.14 us  [fast(): jnp.dot(named.astype(BF16).reshape(2 * n, T), before, preferred_element_t...]
    unnamed x123 -> x23, local copies, waits for them, and re-layouts: 115 us -> 24 us
    concatenate x4 -> x1, local copies, waits for them, and re-layouts: 56.8 us -> 0.08 us  [fast(): jnp.concatenate([router, attention_gain[:, None], moe_gain[:, None], jnp....]
  transfers between devices with their start and end apart: 10 -> 0, of which waited for: 4 -> 0; matrix products, arithmetic and copies ran while one was open for 15% -> 0% of each run, Pallas kernels for 0% -> 0%
where the time goes in v3:
time: 627 us; the launch traced here: 617 us
  Pallas kernels  574 us (92%)
  local copies, waits for them, and re-layouts  29.6 us (5%)
  other arithmetic  12.6 us (2%)
    pallas_call x1, Pallas kernels, first(): pl.pallas_call(first_kernel, in_specs=[VMEM] * 4 + [HBM] * 7, out_specs=[...  255 us
    pallas_call x1, Pallas kernels, last(): pl.pallas_call(last_kernel, in_specs=[VMEM] * 15 + [HBM] * 5, out_specs=[...  181 us
    pallas_call x1, Pallas kernels, middle(): pl.pallas_call(middle_kernel, in_specs=[HBM] * 3, out_specs=[VMEM] + [HBM...  91.2 us
    pallas_call x1, Pallas kernels, experts(): pl.pallas_call(expert_kernel, grid=(STEPS,), in_specs=[pl.BlockSpec(memor...  47 us
    unnamed x23, local copies, waits for them, and re-layouts  24 us

profile of v3, /device:TPU:0, one launch (start us, length us, event | category | flops | bytes accessed | tf_op | source)
XLA Modules:
  0.0 617.0 jit_solution(9544088084517945952)
XLA Ops:
  0.7 0.1 pad_add_fusion.own_ref
  0.7 0.0 copy-start.6
  0.7 0.9 convert_reduce_fusion
  1.7 0.1 pad.12.clone
  1.7 0.8 copy.55
  2.5 0.8 copy.56
  3.3 0.8 copy.54
  4.1 0.7 maximum_maximum_fusion.refs_6_
  4.8 0.1 eq.65
  4.9 0.0 copy-start
  4.9 1.5 fusion.2.refs_3_
  6.4 0.3 fusion.7
  6.7 0.8 pad_maximum_fusion
  7.5 3.5 copy.71
  11.0 0.0 copy-done
  11.0 4.1 copy.70
  15.1 254.9 %shard_map.178 = (bf16[1536,2560]{1,0:T(8,128)(2,1)}, bf16[1536,1536]{1,0:T(8,128)(2,1)}, bf16[1536,128]{1,0:T(8,128)(2,1)}, s32[256,128]{1,0:T(8,128)}, bf16[40...) custom-call(bf16[128,1536]{1,0:T(8,128)(2,1)} %refs_0_.3, ...), custom_call_target="tpu_custom_call" | custom-call | tf_op jit(solution)/shard_map/pallas_call | solution.py:1198
  270.0 0.0 copy-done.6
  270.0 1.1 compare_reduce_fusion
  271.1 0.1 fusion.4
  271.2 1.7 slice.32.router_ref
  272.9 1.1 fusion.1.pick_ref
  274.1 47.0 %shard_map.179 = (bf16[4096,1536]{1,0:T(8,128)(2,1)}, bf16[4096,1536]{1,0:T(8,128)(2,1)}, f32[32,8,128]{2,1,0:T(8,128)}, bf16[1536,1024]{1,0:T(8,128)(2,1)}, bf16[1536,896]{1,0:T(8,128)(2,1)}) custom-call(s32[2]{0:T(128)} %copy-done.6, bf16[4096,1536]{1,0:T(8,128)(2,1)} %get-tuple-element.40.t_ref, bf16[4096,1536]{1,0:T(8,128)(2,1)} %get-tuple-element.41.c_ref, ...), custom_call_target="tpu_custom_call" | custom-call | flops 22000001024 | bytes 62000000 | tf_op jit(solution)/shard_map/pallas_call | solution.py:500
  321.1 91.2 %shard_map.180 = (f32[128,1536]{1,0:T(8,128)}, bf16[40,48,512]{2,1,0:T(8,128)(2,1)}, f32[32,8,128]{2,1,0:T(8,128)}) custom-call(bf16[4096,1536]{1,0:T(8,128)(2,1)} %get-tuple-element.46.refs_0_, bf16[1536,896]{1,0:T(8,128)(2,1)} %get-tuple-element.47.refs_1_.refs_19_, f32[32,8,128]{2,1,0:T(8,128)} %get-tuple-element.48.refs_2_), custom_call_target="tpu_custom_call" | custom-call | tf_op jit(solution)/shard_map/pallas_call | solution.py:1234
  412.3 1.0 fusion.8
  413.3 0.6 pad.4.refs_3_
  414.0 0.0 copy-start.2
  414.0 180.6 %shard_map.181 = (bf16[128,1536]{1,0:T(8,128)(2,1)}, f32[128,1536]{1,0:T(8,128)}, f32[48,2560]{1,0:T(8,128)}, f32[48,1536]{1,0:T(8,128)}, f32[48,128]{1,0:T(8,128)}, /*index=5*/bf16[40,48,1024]{2,1,0:T(8,128)(2,1)}) custom-call(bf16[128,1536]{1,0:T(8,128)(2,1)} %refs_0_.3, bf16[128,1536]{1,0:T(8,128)(2,1)} %refs_1_.1, ...), custom_call_target="tpu_custom_call" | custom-call | tf_op jit(solution)/shard_map/pallas_call | solution.py:1312
  594.5 0.0 copy-done.2
  594.6 2.0 add_convert_fusion
  596.5 1.5 slice_reduce_fusion
  598.0 1.4 copy.62
  599.5 2.1 convert_bitcast_fusion.1
  601.5 0.0 copy-start.1
  601.6 4.2 copy.64
  605.8 0.0 copy-done.1
  605.8 1.0 convert_bitcast_fusion
  606.7 0.0 copy-start.4
  606.7 0.0 copy-start.3
  606.7 0.0 copy-start.5
  606.8 7.8 %copy.63 = f32[48,40,1024]{2,1,0:T(8,128)} copy(f32[48,40,1024]{2,0,1:T(8,128)S(1)} %convert_bitcast_fusion) | data formatting | bytes 15728640
  614.5 0.0 copy-done.4
  614.5 0.7 copy.75
  615.3 0.0 copy-done.3
  615.3 0.8 copy.76
  616.1 0.0 copy-done.5
  616.1 0.7 copy.77
  (7 shorter events, 0.1 us)
Async XLA Ops:
  0.7 269.2 %copy-start.6 = (s32[2]{0:T(128)}, s32[2]{0:T(128)S(1)}, u32[]{:S(2)}) copy-start(s32[2]{0:T(128)S(1)} %pad_add_fusion.own_ref) | copy-start | bytes 28
  4.9 6.1 copy-start
  414.0 180.6 %copy-start.2 = (f32[128,1536]{1,0:T(8,128)S(1)}, f32[128,1536]{1,0:T(8,128)}, u32[]{:S(2)}) copy-start(f32[128,1536]{1,0:T(8,128)} %get-tuple-element.39.refs_13_) | copy-start | bytes 2359300
  601.5 4.2 copy-start.1
  606.7 7.8 %copy-start.4 = (bf16[128,1536]{1,0:T(8,128)(2,1)S(1)}, bf16[128,1536]{1,0:T(8,128)(2,1)}, u32[]{:S(2)}) copy-start(bf16[128,1536]{1,0:T(8,128)(2,1)} %get-tuple-element.124) | copy-start | bytes 1179652
  606.7 8.5 %copy-start.3 = (f32[48,2560]{1,0:T(8,128)S(1)}, f32[48,2560]{1,0:T(8,128)}, u32[]{:S(2)}) copy-start(f32[48,2560]{1,0:T(8,128)} %get-tuple-element.126) | copy-start | bytes 1474564
  606.7 9.3 %copy-start.5 = (f32[48,1536]{1,0:T(8,128)S(1)}, f32[48,1536]{1,0:T(8,128)}, u32[]{:S(2)}) copy-start(f32[48,1536]{1,0:T(8,128)} %get-tuple-element.127) | copy-start | bytes 884740

commit v4 on v3

--- a/solution.py
+++ b/solution.py
@@ -428,94 +428,88 @@
 
 QUARTER, DOWN_WHOLE, DOWN_QUARTER, OWN_WIDTH = 0, 256, 768, 896
 
-def expert_kernel(own_ref, t_ref, c_ref, pick_ref, router_ref, wf_ref, wo_ref, out_ref, gin_ref, gg_ref, dwf_ref, dwo_ref,
-                  x_ref, g_ref, rw_ref, act_ref, dgu_ref, actq_ref, dguq_ref, ow_ref, gi_ref):
-    i = pl.program_id(0)
-    mine = (own_ref[0], own_ref[1])
-    logits = nt(router_ref[...], t_ref[...])
-    row = lax.broadcasted_iota(jnp.int32, logits.shape, 0)
-    logits = jnp.where(row < E, logits, -jnp.inf)
-    e = jnp.exp(logits - jnp.max(logits, axis=0, keepdims=True))
-    probs = e / jnp.sum(e, axis=0, keepdims=True)
-    mineprob = [jnp.sum(jnp.where(row == m, probs, 0.0), axis=0, keepdims=True) for m in mine]
-    at = pl.ds(pl.multiple_of(i * M, M), M)
-    for s in range(SRC):
-        pick = pick_ref[s * 64:s * 64 + 64, :]
-        xs = nn(pick, t_ref[s * 128:s * 128 + 128, :]).astype(BF16)
-        gs = nn(pick, c_ref[s * 128:s * 128 + 128, :]).astype(BF16)
-        wide = pick.astype(F32)
-        for k in range(2):
-            to = pl.ds(pl.multiple_of(i * M + s * CAP, CAP), CAP)
-            x_ref[k, to, :] = xs[k * 32:k * 32 + 32]
-            g_ref[k, to, :] = gs[k * 32:k * 32 + 32]
-            rw_ref[k, s * CAP:s * CAP + CAP, :] = jnp.broadcast_to(jnp.sum(wide[k * 32:k * 32 + 32] * mineprob[k][:, s * 128:(s + 1) * 128], axis=1, keepdims=True), (CAP, 128))
-    gws = []
-    sets = (
-        (act_ref, dgu_ref, 512, wf_ref[...], wo_ref[:, DOWN_WHOLE:DOWN_WHOLE + 512]),
-        (actq_ref, dguq_ref, 128, wo_ref[:, QUARTER:QUARTER + 256], wo_ref[:, DOWN_QUARTER:DOWN_QUARTER + 128]),
-    )
-    for k, (acts, dgus, w, w_gu, w_d) in enumerate(sets):
-        pre = nn(x_ref[k, at, :], w_gu)
-        gate, up = pre[:, :w], pre[:, w:]
-        sig = jax.nn.sigmoid(gate)
-        silu = gate * sig
-        act = silu * up
-        share = rw_ref[k, :, 0:1] * RESIDUAL_SCALE
-        scaled = (share * act).astype(BF16)
-        acts[at, :] = scaled
-        da = nn(g_ref[k, at, :], w_d)
-        gws.append(RESIDUAL_SCALE * jnp.sum(act.astype(BF16).astype(F32) * da, axis=1, keepdims=True))
-        ow_ref[k] = nt(scaled, w_d).astype(BF16)
-        da = share * da
-        dgu = jnp.concatenate([(da * up * sig * (1.0 + gate * (1.0 - sig))).astype(BF16), (da * silu).astype(BF16)], axis=1)
-        dgus[at, :] = dgu
-        gi_ref[k] = nt(dgu, w_gu).astype(BF16)
-    for s in range(SRC):
-        r = slice(s * CAP, s * CAP + CAP)
-        pick = pick_ref[s * 64:s * 64 + 64, :]
-        to = slice(s * 128, s * 128 + 128)
-        out_ref[to, :] = tn(pick, jnp.concatenate([ow_ref[0, r, :], ow_ref[1, r, :]], axis=0)).astype(BF16)
-        gin_ref[to, :] = tn(pick, jnp.concatenate([gi_ref[0, r, :], gi_ref[1, r, :]], axis=0)).astype(BF16)
-        wide = pick.astype(F32)
-        for k in range(2):
-            gg_ref[s, k:k + 1, :] = jnp.sum(wide[k * 32:k * 32 + 32] * gws[k][r], axis=0, keepdims=True)
-        gg_ref[s, 2:8, :] = jnp.zeros((6, 128), F32)
-
-    @pl.when(i == STEPS - 1)
-    def _():
-        def body(j, carry):
-            c = pl.ds(pl.multiple_of(j * 256, 256), 256)
-            dwf_ref[c, :] = tn(x_ref[0, :, c], dgu_ref[...]).astype(BF16)
-            dwo_ref[c, QUARTER:QUARTER + 256] = tn(x_ref[1, :, c], dguq_ref[...]).astype(BF16)
-            dwo_ref[c, DOWN_WHOLE:DOWN_WHOLE + 512] = tn(g_ref[0, :, c], act_ref[...]).astype(BF16)
-            dwo_ref[c, DOWN_QUARTER:DOWN_QUARTER + 128] = tn(g_ref[1, :, c], actq_ref[...]).astype(BF16)
-            return carry
-        lax.fori_loop(0, D // 256, body, 0)
-
-def experts(owned, tokens, cot, picks, router_t, wf, wo):
-    R = SRC * 128
-    once = lambda shape: pl.BlockSpec(shape, lambda i: (0, 0), pipeline_mode=pl.Buffered(1))
-    rows = pl.BlockSpec((R, D), lambda i: (i, 0))
-    vmem = lambda *shape, dtype=BF16: pltpu.VMEM(shape, dtype)
-    return pl.pallas_call(
-        expert_kernel,
-        grid=(STEPS,),
-        in_specs=[
-            pl.BlockSpec(memory_space=pltpu.SMEM), rows, rows, pl.BlockSpec((SRC * 64, 128), lambda i: (i, 0)),
-            once((64, D)), once((D, 2 * F)), once((D, OWN_WIDTH)),
-        ],
-        out_specs=[rows, rows, pl.BlockSpec((SRC, 8, 128), lambda i: (i, 0, 0)), once((D, 2 * F)), once((D, OWN_WIDTH))],
-        out_shape=[
-            jax.ShapeDtypeStruct((4096, D), BF16), jax.ShapeDtypeStruct((4096, D), BF16), jax.ShapeDtypeStruct((32, 8, 128), F32),
-            jax.ShapeDtypeStruct((D, 2 * F), BF16), jax.ShapeDtypeStruct((D, OWN_WIDTH), BF16),
-        ],
-        scratch_shapes=[
-            vmem(2, 1024, D), vmem(2, 1024, D), vmem(2, M, 128, dtype=F32),
-            vmem(1024, 512), vmem(1024, 1024), vmem(1024, 128), vmem(1024, 256), vmem(2, M, D), vmem(2, M, D),
-        ],
-        compiler_params=pltpu.CompilerParams(vmem_limit_bytes=62 * 2**20),
-        cost_estimate=pl.CostEstimate(flops=22 * 10**9, bytes_accessed=62 * 10**6, transcendentals=0),
-    )(owned, tokens, cot, picks, router_t, wf, wo)
+class Experts:
+    NAMES = ("x", "c", "rw", "gw", "act", "dgu", "actq", "dguq", "ow", "gi")
+
+    @staticmethod
+    def scratch():
+        R = STEPS * M
+        return [
+            pltpu.VMEM((2, R, D), BF16), pltpu.VMEM((2, R, D), BF16), pltpu.VMEM((2, M, 128), F32), pltpu.VMEM((2, M, 128), F32),
+            pltpu.VMEM((R, F), BF16), pltpu.VMEM((R, 2 * F), BF16), pltpu.VMEM((R, 128), BF16), pltpu.VMEM((R, 256), BF16),
+            pltpu.VMEM((2, M, D), BF16), pltpu.VMEM((2, M, D), BF16),
+        ]
+
+    def __init__(self, refs, wf_ref, wo_ref, pick_ref, prob_ref, gates_ref):
+        for name, ref in zip(self.NAMES, refs):
+            setattr(self, name, ref)
+        self.wf, self.wo, self.pick, self.prob, self.gates = wf_ref, wo_ref, pick_ref, prob_ref, gates_ref
+
+    def picks(self, plane, s):
+        return self.pick[pl.ds(pl.multiple_of(plane * (SRC * 64) + s * 64, 64), 64), :]
+
+    def load(self, step, plane, t_ref, c_ref):
+        def one(s):
+            pick = self.picks(plane, s)
+            block = pl.ds(pl.multiple_of(s * 128, 128), 128)
+            xs = nn(pick, t_ref[block, :]).astype(BF16)
+            cs = nn(pick, c_ref[block, :]).astype(BF16)
+            share = pick.astype(F32) * self.prob[pl.ds(pl.multiple_of(plane * (SRC * 64) + s * 64, 64), 64), :]
+            share = jnp.sum(share, axis=1, keepdims=True) * RESIDUAL_SCALE
+            here = pl.ds(pl.multiple_of(s * CAP, CAP), CAP)
+            to = pl.ds(pl.multiple_of(step * M + s * CAP, CAP), CAP)
+            for k in range(2):
+                self.x[k, to, :] = xs[k * CAP:k * CAP + CAP]
+                self.c[k, to, :] = cs[k * CAP:k * CAP + CAP]
+                self.rw[k, here, :] = jnp.broadcast_to(share[k * CAP:k * CAP + CAP], (CAP, 128))
+        for s in range(SRC):
+            one(s)
+
+    def run(self, step):
+        at = slice(step * M, step * M + M)
+        sets = (
+            (self.act, self.dgu, 512, lambda: self.wf[...], DOWN_WHOLE),
+            (self.actq, self.dguq, 128, lambda: self.wo[:, QUARTER:QUARTER + 256], DOWN_QUARTER),
+        )
+        for k, (acts, dgus, w, w_gu, d0) in enumerate(sets):
+            pre = nn(self.x[k, at, :], w_gu())
+            gate, up = pre[:, :w], pre[:, w:]
+            sig = jax.nn.sigmoid(gate)
+            silu = gate * sig
+            act = silu * up
+            share = self.rw[k, :, 0:1]
+            scaled = (share * act).astype(BF16)
+            acts[at, :] = scaled
+            da = nn(self.c[k, at, :], self.wo[:, d0:d0 + w])
+            gw = RESIDUAL_SCALE * jnp.sum(act.astype(BF16).astype(F32) * da, axis=1, keepdims=True)
+            self.gw[k] = jnp.broadcast_to(gw, (M, 128))
+            self.ow[k] = nt(scaled, self.wo[:, d0:d0 + w]).astype(BF16)
+            da = share * da
+            dgus[at, :w] = (da * up * sig * (1.0 + gate * (1.0 - sig))).astype(BF16)
+            dgus[at, w:] = (da * silu).astype(BF16)
+            self.gi[k] = nt(dgus[at, :], w_gu()).astype(BF16)
+
+    def give(self, plane, out_ref, gin_ref):
+        def one(s):
+            r = pl.ds(pl.multiple_of(s * CAP, CAP), CAP)
+            pick = self.picks(plane, s)
+            to = pl.ds(pl.multiple_of(s * 128, 128), 128)
+            out_ref[to, :] = tn(pick, jnp.concatenate([self.ow[0, r, :], self.ow[1, r, :]], axis=0)).astype(BF16)
+            gin_ref[to, :] = tn(pick, jnp.concatenate([self.gi[0, r, :], self.gi[1, r, :]], axis=0)).astype(BF16)
+            wide = pick.astype(F32)
+            rows = [jnp.sum(wide[k * CAP:k * CAP + CAP] * self.gw[k, r, :], axis=0, keepdims=True) for k in range(2)]
+            self.gates[plane * SRC + s] = jnp.concatenate(rows + [jnp.zeros((6, 128), F32)], axis=0)
+        for s in range(SRC):
+            one(s)
+
+    def own_grads(self, j, ref):
+        c = slice(j * 256, j * 256 + 256)
+        ref[:, QUARTER:QUARTER + 256] = tn(self.x[1, :, c], self.dguq[...]).astype(BF16)
+        ref[:, DOWN_WHOLE:DOWN_WHOLE + 512] = tn(self.c[0, :, c], self.act[...]).astype(BF16)
+        ref[:, DOWN_QUARTER:DOWN_QUARTER + 128] = tn(self.c[1, :, c], self.actq[...]).astype(BF16)
+
+    def whole_grads(self, j, ref):
+        ref[...] = tn(self.x[0, :, j * 256:j * 256 + 256], self.dgu[...]).astype(BF16)
 
 
 MESH = pl.DeviceIdType.MESH
@@ -721,15 +715,19 @@
     ORDER = ((1, 3), (1, 2), (2, 3), (1, 1), (2, 2), (3, 3), (1, 0), (2, 1), (3, 2), (2, 0), (3, 1), (3, 0))
     STEP = 16
 
-    def __init__(self, p, parts, fulls, outs, spaces, sems, in_place=False):
+    def __init__(self, p, parts, fulls, outs, spaces, sems, in_place=False, by_plane=False):
+        self.by_plane, self.reads = by_plane, []
         self.p, self.parts, self.fulls, self.outs, self.sems, self.in_place = p, parts, fulls, outs, sems, in_place
         count = len(fulls)
         if in_place:
             spaces = (None,) * count + tuple(spaces)
         self.held, self.r0, self.r1, self.r2, self.r3 = (spaces[i * count : (i + 1) * count] for i in range(5))
-        self.rows = [f.shape[0] // DEVICES for f in fulls]
-        self.P, self.sends, self.loads = len(parts), [], {}
+        self.rows = [f.shape[0] // (8 if by_plane else DEVICES) for f in fulls]
+        self.P, self.sends = len(parts), []
         self.left = list(self.ORDER)
+
+    def begin_all(self):
+        self.reads = self.begin()
 
     @staticmethod
     def scratch(arrays, parts, in_place=False):
@@ -763,23 +761,25 @@
 
     def source(self, i, q, k, core):
         a = self.parts[i][0]
-        d = dev(self.p.zq[q], *self.spot(i, k), core)
+        d = dev(0 if self.by_plane else self.p.zq[q], *self.spot(i, k), core)
         return self.fulls[a].at[pl.ds(pl.multiple_of(d * self.rows[a], self.rows[a]), self.rows[a]), self.cut(i)]
 
-    def begin(self, only=None):
+    def begin(self, planes=(3, 2, 1, 0)):
         ls, s0, e0 = self.sems[:3]
-        for q in (3, 2, 1, 0):
+        made = []
+        for q in planes:
             for k in range(4):
                 for i in range(self.P):
                     a = self.parts[i][0]
-                    if only is not None and a not in only:
-                        continue
                     s = self.slot(q, *self.spot(i, k))
-                    self.go(rc(self.source(i, q, k, 1 - self.p.c), self.r0[a].at[s, :, self.cut(i)], s0.at[q, k, i], e0.at[q, k, i], self.p.sib))
+                    copy = rc(self.source(i, q, k, 1 - self.p.c), self.r0[a].at[s, :, self.cut(i)], s0.at[q, k, i], e0.at[q, k, i], self.p.sib)
+                    copy.start()
+                    made.append(copy.wait_send)
                     if not self.in_place:
                         l = pltpu.make_async_copy(self.source(i, q, k, self.p.c), self.held[a].at[s, :, self.cut(i)], ls.at[q, k, i])
                         l.start()
-                        self.loads[q, k, i] = l
+                        made.append(l.wait)
+        return made
 
     def step(self, number=1):
         for f, q in self.left[:number]:
@@ -813,11 +813,14 @@
                 sums = self.hold(a, q, *self.spot(i, k))
                 here = sums.at[:, self.cut(i)]
                 rc(here, self.r0[a].at[s, :, self.cut(i)], s0.at[q, k, i], e0.at[q, k, i], p.sib).wait_recv()
-                if not self.in_place:
-                    self.loads[q, k, i].wait()
+                if self.reads and not self.in_place:
+                    self.reads[self.reading(q, k, i) * 2 + 1]()
                 self.add(i, sums, self.r0[a], s)
                 if k < 2:
                     self.go(rc(here, self.r1[a].at[q * 2 + k, :, self.cut(i)], s1.at[q, k, i], e1.at[q, k, i], first))
+
+    def reading(self, q, k, i):
+        return ((3 - q) * 4 + k) * self.P + i
 
     def stage2(self, q):
         p = self.p
@@ -881,6 +884,8 @@
     def finish(self):
         p = self.p
         s3, e3 = self.sems[7:9]
+        for wait in self.reads[:: 1 if self.in_place else 2]:
+            wait()
         for copy in self.sends:
             copy.wait_send()
         for q in range(1, 4):
@@ -991,17 +996,20 @@
     return scale * weighted - hidden * scale**3 * inner, upstream * hidden * scale
 
 
+def gate_probs(r):
+    logits = nt(r.small_t[:64, :].astype(BF16), r.n2[...])
+    row = lax.broadcasted_iota(jnp.int32, logits.shape, 0)
+    logits = jnp.where(row < E, logits, -jnp.inf)
+    e = jnp.exp(logits - jnp.max(logits, axis=0, keepdims=True))
+    return e / jnp.sum(e, axis=0, keepdims=True)
+
+
 def attention_backward(x_ref, cot_ref, gin_ref, gates_ref, cos_ref, sin_ref, qkv_ref, out_ref, r, put_qkv, put_out, put_small):
     def router():
         m = r.middle[...]
-        logits = nt(r.small_t[:64, :].astype(BF16), r.n2[...])
-        row = lax.broadcasted_iota(jnp.int32, logits.shape, 0)
-        logits = jnp.where(row < E, logits, -jnp.inf)
-        e = jnp.exp(logits - jnp.max(logits, axis=0, keepdims=True))
-        probs = e / jnp.sum(e, axis=0, keepdims=True)
+        probs = gate_probs(r)
         gates = gates_ref[...]
         gl = probs * (gates - jnp.sum(probs * gates, axis=0, keepdims=True))
-        gl = jnp.where(row < E, gl, 0.0)
         gl = jnp.concatenate([gl, jnp.zeros((64, TOK), F32)], axis=0).T
         r.gl[...] = gl
         back = nn(gl.astype(BF16), r.small_t[...].astype(BF16))
@@ -1102,6 +1110,7 @@
 )
 ROW_HALVES = ((0, 0, 768, 0), (0, 768, 768, 1))
 DENSE_PARTS = ((0, 0, 1280, 0), (0, 1280, 1280, 1), (1, 0, 768, 0), (1, 768, 768, 1), (2, 0, 128, 1))
+TOKEN_PARTS = ROW_HALVES + ((1, 0, 128, 1),)
 FIRST_PARTS = DENSE_PARTS + ((3, 0, 128, 0),)
 
 
@@ -1139,16 +1148,24 @@
     group, quarter = src // 4, lax.rem(src, 4) * 128
     rows = pl.ds(pl.multiple_of(dst * 48, 48), 48)
     return (
+        (dwf_ref.at[rows], g_ref.at[group * 5 + lax.rem(src, 4)]),
         (dwo_ref.at[rows, pl.ds(QUARTER, 128)], g_ref.at[group * 5 + 4, :, lanes(quarter)]),
         (dwo_ref.at[rows, pl.ds(QUARTER + 128, 128)], g_ref.at[group * 5 + 4, :, lanes(F + quarter)]),
-        (dwf_ref.at[rows], g_ref.at[group * 5 + lax.rem(src, 4)]),
-    )
+    )
+
+
+def route_weights(ids, r, rw):
+    probs = gate_probs(r)
+    row = lax.broadcasted_iota(jnp.int32, probs.shape, 0)
+    for k in range(TOP):
+        rw[k : k + 1, :] = jnp.sum(jnp.where(row == ids[k : k + 1, :], probs, 0.0), axis=0, keepdims=True)
 
 
 def first_kernel(*refs):
-    (x, cos, sin, bias), dense, (cot,), experts_in, dense_out, (cots, tokens, wf, wo), results, weights, (load_sem,), refs = cut_up(
-        refs, 4, 4, 1, 2, 4, 4, 9, 3, 1
-    )
+    (x, cos, sin, bias, ids), dense, (cot,), experts_in, dense_out, outs, results, weights, (rw, load_sem), refs = cut_up(
+        refs, 5, 4, 1, 2, 4, 5, 9, 3, 2
+    )
+    cots, tokens, shares, wf, wo = outs
     sems1, sems2, sems3, direct_sems, _ = cut_up(refs, 12, 12, 12, 3)
     greet_all()
     p = Place()
@@ -1157,7 +1174,7 @@
         setattr(r, name, ref)
     g1 = Gather(p, FIRST_PARTS, dense, dense_out, sems1)
     g2 = Gather(p, ROW_HALVES, [cot], [cots], sems2)
-    g3 = Gather(p, ROW_HALVES, [r.n2], [tokens], sems3)
+    g3 = Gather(p, TOKEN_PARTS, [r.n2, rw], [tokens, shares], sems3)
     direct = Direct(weights_out, tuple(experts_in) + (wf, wo), direct_sems)
     g1.step()
     direct.own()
@@ -1165,6 +1182,7 @@
         g1.step()
         direct.start(n)
     g2.step(2)
+    direct.start(DEVICES)
     g1.arrived()
     loads = [pltpu.make_async_copy(a, b, load_sem.at[i]) for i, (a, b) in enumerate(zip(dense_out[:3], weights))]
     for l in loads:
@@ -1176,12 +1194,9 @@
         chunk()
         if i % 2 == 1:
             g2.step()
-            direct.start(SECOND_BATCH)
+    route_weights(ids, r, rw)
     g3.step(2)
-    direct.start(SECOND_BATCH)
     g2.arrived()
-    g3.step(2)
-    direct.start(DEVICES)
     g3.arrived()
     for g in (g1, g2, g3):
         g.finish()
@@ -1189,56 +1204,117 @@
 
 
 FIRST_BATCHES = (1, 1, 1, 1, 1, 1, 1, 1, 1, 1)
-SECOND_BATCH = 2
-
-
-def first(x, cos, sin, bias, dense, cot, gu, dp):
+
+
+def first(x, cos, sin, bias, ids, dense, cot, gu, dp):
     wide = lambda a: like(DEVICES * a.shape[0], a.shape[1], dtype=a.dtype)
     dense_full = [wide(a) for a in dense]
     return pl.pallas_call(
         first_kernel,
-        in_specs=[VMEM] * 4 + [HBM] * 7,
-        out_specs=[HBM] * 8 + [VMEM] * 9,
-        out_shape=dense_full + [wide(cot), wide(cot), like(D, 2 * F), like(D, OWN_WIDTH)] + [like(*s, dtype=t) for s, t in ATT_SHAPES],
+        in_specs=[VMEM] * 5 + [HBM] * 7,
+        out_specs=[HBM] * 9 + [VMEM] * 9,
+        out_shape=dense_full + [wide(cot), wide(cot), like(DEVICES * TOP, TOK, dtype=F32), like(D, 2 * F), like(D, OWN_WIDTH)] + [like(*s, dtype=t) for s, t in ATT_SHAPES],
         scratch_shapes=[pltpu.VMEM(a.shape, a.dtype) for a in dense_full[:3]]
-        + [DMA((3,))]
+        + [pltpu.VMEM((TOP, TOK), F32), DMA((3,))]
         + Gather.scratch(4, FIRST_PARTS)
-        + Gather.scratch(1, ROW_HALVES) * 2
+        + Gather.scratch(1, ROW_HALVES)
+        + Gather.scratch(2, TOKEN_PARTS)
         + Direct.scratch(5),
         compiler_params=pltpu.CompilerParams(collective_id=0, has_side_effects=True, vmem_limit_bytes=60 * 2**20),
-    )(x, cos, sin, bias, *dense, cot, gu, dp)
+    )(x, cos, sin, bias, ids, *dense, cot, gu, dp)
 
 
 def middle_kernel(*refs):
-    (gin_part, dwo, gates), (gin, grad_down, all_gates), spaces, sems, direct_sems, _ = cut_up(refs, 3, 3, 5, 9, 3)
+    (picks, probs), (tokens, cots, wf_in, wo_in), (gin,), outs, blocks, work, refs = cut_up(refs, 2, 4, 1, 5, 9, 10)
+    out_part, dwf, dwo, all_gates, grad_down = outs
+    t, c, out_block, gin_block, wf, wo, gates, whole, own = blocks
+    (weight_sem, load_sem, out_sem, grad_sem), spaces, sems, direct_sems, _ = cut_up(refs, 4, 5, 9, 3)
     greet_all()
     p = Place()
-    s = Scatter(p, ROW_HALVES, [gin_part], [gin], spaces, sems)
+    s = Scatter(p, ROW_HALVES, [gin_block], [gin], spaces, sems, by_plane=True)
     direct = Direct(down_back, (dwo, gates, grad_down, all_gates), direct_sems)
-    s.begin()
-    direct.own()
-    for n in MIDDLE_BATCHES:
-        s.step()
-        direct.start(n)
+    e = Experts(work, wf, wo, picks, probs, gates)
+    R = SRC * TOK
+
+    def plane_rows(q):
+        return pl.ds(pl.multiple_of(p.zq[q] * R, R), R)
+
+    def load(q):
+        made = [pltpu.make_async_copy(src.at[plane_rows(q)], dst, load_sem.at[i]) for i, (src, dst) in enumerate(((tokens, t), (cots, c)))]
+        for l in made:
+            l.start()
+        return made
+
+    order = (3, 2, 1, 0)
+    loads = load(order[0])
+    weights = [pltpu.make_async_copy(a, b, weight_sem.at[i]) for i, (a, b) in enumerate(((wf_in, wf), (wo_in, wo)))]
+    for l in weights:
+        l.start()
+    reads, store = [], None
+    for step, q in enumerate(order):
+        for l in loads:
+            l.wait()
+        e.load(step, p.zq[q], t, c)
+        if step < 3:
+            loads = load(order[step + 1])
+        if step == 0:
+            for l in weights:
+                l.wait()
+        for wait in reads:
+            wait()
+        s.step(step)
+        e.run(step)
+        if store is not None:
+            store.wait()
+        e.give(p.zq[q], out_block, gin_block)
+        reads = s.begin((q,))
+        store = pltpu.make_async_copy(out_block, out_part.at[plane_rows(q)], out_sem)
+        store.start()
+    stores = []
+    for n in range(2 * (D // 256)):
+        a, j, b = n // (D // 256), n % (D // 256), n % 2
+        block, out, make = ((own, dwo, e.own_grads), (whole, dwf, e.whole_grads))[a]
+        if j >= 2:
+            stores[n - 2].wait()
+        make(j, block.at[b])
+        l = pltpu.make_async_copy(block.at[b], out.at[pl.ds(j * 256, 256)], grad_sem.at[b, a])
+        l.start()
+        stores.append(l)
+        if j == D // 256 - 1:
+            for l in stores[-2:]:
+                l.wait()
+            if a == 0:
+                direct.own()
+                direct.start(DEVICES)
+        if n == 1:
+            for wait in reads:
+                wait()
+        if n % 2 == 1:
+            s.step()
     s.step(12)
-    direct.start(DEVICES)
+    store.wait()
     s.finish()
     direct.finish()
 
 
-MIDDLE_BATCHES = (3, 3, 3, 3, 3, 3, 3, 3, 3, 4)
-
-
-def middle(gin_part, dwo, gates):
-    spaces, sems = Scatter.scratch([gin_part], ROW_HALVES)
+def middle(picks, probs, tokens, cots, wf, wo):
+    R = SRC * TOK
+    spaces, sems = Scatter.scratch([tokens], ROW_HALVES)
     return pl.pallas_call(
         middle_kernel,
-        in_specs=[HBM] * 3,
-        out_specs=[VMEM] + [HBM] * 2,
-        out_shape=[like(TOK, D, dtype=F32), like(E, D // DEVICES, F), like(DEVICES, 8, TOK, dtype=F32)],
-        scratch_shapes=spaces + sems + Direct.scratch(3),
-        compiler_params=pltpu.CompilerParams(collective_id=1, has_side_effects=True, vmem_limit_bytes=60 * 2**20),
-    )(gin_part, dwo, gates)
+        in_specs=[VMEM] * 2 + [HBM] * 4,
+        out_specs=[VMEM] + [HBM] * 5,
+        out_shape=[like(TOK, D, dtype=F32), like(DEVICES * TOK, D), like(D, 2 * F), like(D, OWN_WIDTH), like(DEVICES, 8, TOK, dtype=F32), like(E, D // DEVICES, F)],
+        scratch_shapes=[pltpu.VMEM((R, D), BF16)] * 4
+        + [
+            pltpu.VMEM((D, 2 * F), BF16), pltpu.VMEM((D, OWN_WIDTH), BF16), pltpu.VMEM((DEVICES, 8, TOK), F32),
+            pltpu.VMEM((2, 256, 2 * F), BF16), pltpu.VMEM((2, 256, OWN_WIDTH), BF16),
+        ]
+        + Experts.scratch()
+        + [DMA((2,)), DMA((2,)), DMA, DMA((2, 2))]
+        + spaces + sems + Direct.scratch(3),
+        compiler_params=pltpu.CompilerParams(collective_id=1, has_side_effects=True, vmem_limit_bytes=63 * 2**20),
+    )(picks, probs, tokens, cots, wf, wo)
 
 
 WORK = (
@@ -1269,12 +1345,12 @@
     s1 = Scatter(p, ROW_HALVES, [out_part], [combined], spaces1, sems1)
     s2 = Scatter(p, DENSE_PARTS, [qkv_ref, out_ref, small_src], [qkv_grad, out_grad, small_grad], spaces2, sems2, in_place=True)
     direct = Direct(gate_up_back, (dwf, dwo, grad_gu), direct_sems)
-    s1.begin()
+    s1.begin_all()
     loads = [pltpu.make_async_copy(a, b, load_sem.at[i]) for i, (a, b) in enumerate(((out_full, out_ref), (qkv_full, qkv_ref)))]
     for l in loads:
         l.start()
     direct.own()
-    direct.start(2)
+    direct.start(12)
 
     def put_qkv(t, value):
         qkv_ref[t * 256 : t * 256 + 256, :] = value
@@ -1293,7 +1369,7 @@
         if i % 3 == 2:
             s1.step()
             direct.start(2)
-    s2.begin()
+    s2.begin_all()
     s1.step(12)
     while s2.left:
         s2.step()
@@ -1340,20 +1416,21 @@
     allowed = (sequence_ids[:, None] == sequence_ids[None, :]) & (place_in[None, :] <= place_in[:, None])
     bias = jnp.where(allowed, 0.0, -jnp.inf).astype(F32)
 
-    qkv_full, out_full, small_full, ids_all, cots, tokens, wf, wo, *results = first(
-        layer_input, cos, sin, bias, [qkv_weight, output_weight, small, expert_ids.T], cotangent,
+    ids_t = expert_ids.T
+    qkv_full, out_full, small_full, ids_all, cots, tokens, shares, wf, wo, *results = first(
+        layer_input, cos, sin, bias, ids_t, [qkv_weight, output_weight, small, ids_t], cotangent,
         jnp.transpose(gate_up, (1, 0, 2)), jnp.transpose(down_proj, (1, 0, 2)),
     )
 
     owned = jnp.stack([(me // 4) * 5 + lax.rem(me, 4), (me // 4) * 5 + 4])
-    named = jnp.any(ids_all.reshape(n, TOP, T)[:, :, None, :] == owned[None, None, :, None], axis=1)
+    named = ids_all.reshape(n, TOP, T)[:, :, None, :] == owned[None, None, :, None]
+    probs = jnp.sum(jnp.where(named, shares.reshape(n, TOP, 1, T), 0.0), axis=1)
+    probs = jnp.broadcast_to(probs[:, :, None, :], (n, 2, CAP, T)).reshape(n * 64, T)
+    named = jnp.any(named, axis=1)
     before = (place_in[:, None] < place_in[None, :]).astype(BF16)
     ranks = jnp.dot(named.astype(BF16).reshape(2 * n, T), before, preferred_element_type=F32).reshape(n, 2, 1, T)
     picks = ((ranks == jnp.arange(CAP, dtype=F32)[:, None]) & named[:, :, None, :]).astype(BF16).reshape(n * 64, T)
-    router_t = results[0][:64].astype(BF16)
-    out_part, gin_part, gates, dwf, dwo = experts(owned, tokens, cots, picks, router_t, wf, wo)
-
-    gin, grad_down, gates = middle(gin_part, dwo, gates)
+    gin, out_part, dwf, dwo, gates, grad_down = middle(picks, probs, tokens, cots, wf, wo)
     gates = gates.reshape(8, 4, 8, T)
     gates = jnp.concatenate([gates[:, :, 0], jnp.sum(gates[:, :, 1], axis=1, keepdims=True)], axis=1).reshape(E, T)
     gates = jnp.pad(gates, ((0, 64 - E), (0, 0)))

time: 627 us -> 597 us (0.952)
  Pallas kernels: 574 us -> 544 us
    pallas_call x3 -> x2, Pallas kernels: 393 us -> 367 us  [the longest x1 248 us: first(): pl.pallas_call(first_kernel, in_specs=[VMEM] * 5 + [HBM] * 7, out_specs=[...]
    unnamed x23 -> x21, local copies, waits for them, and re-layouts: 24 us -> 24 us
where the time goes in v4:
time: 597 us; the launch traced here: 587 us
  Pallas kernels  544 us (91%)
  local copies, waits for them, and re-layouts  28.9 us (5%)
  other arithmetic  13.7 us (2%)
    pallas_call x1, Pallas kernels, first(): pl.pallas_call(first_kernel, in_specs=[VMEM] * 5 + [HBM] * 7, out_specs=[...  248 us
    pallas_call x1, Pallas kernels, last(): pl.pallas_call(last_kernel, in_specs=[VMEM] * 15 + [HBM] * 5, out_specs=[...  177 us
    pallas_call x1, Pallas kernels, middle(): pl.pallas_call(middle_kernel, in_specs=[VMEM] * 2 + [HBM] * 4, out_specs=...  118 us
    unnamed x21, local copies, waits for them, and re-layouts  24 us

profile of v4, /device:TPU:0, one launch (start us, length us, event | category | flops | bytes accessed | tf_op | source)
XLA Modules:
  0.0 587.4 jit_solution(11526800476079910751)
XLA Ops:
  0.7 0.1 pad_add_fusion
  0.7 0.9 convert_reduce_fusion
  1.7 0.1 pad.12.clone
  1.7 0.8 copy.55
  2.5 0.8 copy.56
  3.3 0.8 copy.54
  4.0 0.7 maximum_maximum_fusion.refs_7_
  4.8 0.1 eq.65
  4.8 0.0 copy-start
  4.9 1.5 fusion.3.refs_3_
  6.4 0.3 fusion.8
  6.7 0.8 pad_maximum_fusion
  7.5 3.5 copy.71
  11.0 0.0 copy-done
  11.0 4.1 copy.70
  15.1 248.4 %shard_map.178 = (bf16[1536,2560]{1,0:T(8,128)(2,1)}, bf16[1536,1536]{1,0:T(8,128)(2,1)}, bf16[1536,128]{1,0:T(8,128)(2,1)}, s32[256,128]{1,0:T(8,128)}, bf16[40...) custom-call(bf16[128,1536]{1,0:T(8,128)(2,1)} %refs_0_.3, ...), custom_call_target="tpu_custom_call" | custom-call | tf_op jit(solution)/shard_map/pallas_call | solution.py:1212
  263.5 1.1 fusion.2
  264.6 1.1 compare_reduce_fusion
  265.7 0.1 fusion.5
  265.9 1.1 fusion.1.refs_0_
  267.0 1.0 broadcast_in_dim.62
  268.0 118.2 %shard_map.179 = (f32[128,1536]{1,0:T(8,128)}, bf16[4096,1536]{1,0:T(8,128)(2,1)}, bf16[1536,1024]{1,0:T(8,128)(2,1)}, bf16[1536,896]{1,0:T(8,128)(2,1)}, f32[32...) custom-call(bf16[2048,128]{1,0:T(8,128)(2,1)} %fusion.1.refs_0_, f32[2048,128]{1,0:T(8,128)} %bitcast.37, ...), custom_call_target="tpu_custom_call" | custom-call | tf_op jit(solution)/shard_map/pallas_call | solution.py:1303
  386.3 1.0 fusion.9
  387.3 0.6 pad.4.refs_3_
  388.0 0.0 copy-start.2
  388.0 177.0 %shard_map.180 = (bf16[128,1536]{1,0:T(8,128)(2,1)}, f32[128,1536]{1,0:T(8,128)}, f32[48,2560]{1,0:T(8,128)}, f32[48,1536]{1,0:T(8,128)}, f32[48,128]{1,0:T(8,128)}, /*index=5*/bf16[40,48,1024]{2,1,0:T(8,128)(2,1)}) custom-call(bf16[128,1536]{1,0:T(8,128)(2,1)} %refs_0_.3, bf16[128,1536]{1,0:T(8,128)(2,1)} %refs_1_.1, ...), custom_call_target="tpu_custom_call" | custom-call | tf_op jit(solution)/shard_map/pallas_call | solution.py:1388
  565.0 0.0 copy-done.2
  565.0 2.0 add_convert_fusion
  566.9 1.5 slice_reduce_fusion
  568.5 1.4 copy.62
  569.9 2.1 convert_bitcast_fusion.1
  572.0 0.0 copy-start.1
  572.0 4.2 copy.64
  576.2 0.0 copy-done.1
  576.2 1.0 convert_bitcast_fusion
  577.1 0.0 copy-start.4
  577.2 0.0 copy-start.3
  577.2 0.0 copy-start.5
  577.2 7.8 %copy.63 = f32[48,40,1024]{2,1,0:T(8,128)} copy(f32[48,40,1024]{2,0,1:T(8,128)S(1)} %convert_bitcast_fusion) | data formatting | bytes 15728640
  584.9 0.0 copy-done.4
  585.0 0.7 copy.75
  585.7 0.0 copy-done.3
  585.7 0.8 copy.76
  586.5 0.0 copy-done.5
  586.5 0.7 copy.77
  (7 shorter events, 0.1 us)
Async XLA Ops:
  4.8 6.1 %copy-start = (bf16[48,40,1024]{2,1,0:T(8,128)(2,1)S(1)}, bf16[48,40,1024]{2,1,0:T(8,128)(2,1)}, u32[]{:S(2)}) copy-start(bf16[48,40,1024]{2,1,0:T(8,128)(2,1)} %param.20) | copy-start | bytes 11796484
  388.0 177.0 %copy-start.2 = (f32[128,1536]{1,0:T(8,128)S(1)}, f32[128,1536]{1,0:T(8,128)}, u32[]{:S(2)}) copy-start(f32[128,1536]{1,0:T(8,128)} %get-tuple-element.38.refs_13_) | copy-start | bytes 2359300
  572.0 4.2 copy-start.1
  577.1 7.8 %copy-start.4 = (bf16[128,1536]{1,0:T(8,128)(2,1)S(1)}, bf16[128,1536]{1,0:T(8,128)(2,1)}, u32[]{:S(2)}) copy-start(bf16[128,1536]{1,0:T(8,128)(2,1)} %get-tuple-element.122) | copy-start | bytes 1179652
  577.2 8.5 %copy-start.3 = (f32[48,2560]{1,0:T(8,128)S(1)}, f32[48,2560]{1,0:T(8,128)}, u32[]{:S(2)}) copy-start(f32[48,2560]{1,0:T(8,128)} %get-tuple-element.124) | copy-start | bytes 1474564
  577.2 9.3 %copy-start.5 = (f32[48,1536]{1,0:T(8,128)S(1)}, f32[48,1536]{1,0:T(8,128)}, u32[]{:S(2)}) copy-start(f32[48,1536]{1,0:T(8,128)} %get-tuple-element.125) | copy-start | bytes 884740

commit v5 on v4

--- a/solution.py
+++ b/solution.py
@@ -440,10 +440,10 @@
             pltpu.VMEM((2, M, D), BF16), pltpu.VMEM((2, M, D), BF16),
         ]
 
-    def __init__(self, refs, wf_ref, wo_ref, pick_ref, prob_ref, gates_ref):
+    def __init__(self, refs, wf_ref, wo_ref, pick_ref, ids_ref, share_ref, gates_ref):
         for name, ref in zip(self.NAMES, refs):
             setattr(self, name, ref)
-        self.wf, self.wo, self.pick, self.prob, self.gates = wf_ref, wo_ref, pick_ref, prob_ref, gates_ref
+        self.wf, self.wo, self.pick, self.ids, self.shares, self.gates = wf_ref, wo_ref, pick_ref, ids_ref, share_ref, gates_ref
 
     def picks(self, plane, s):
         return self.pick[pl.ds(pl.multiple_of(plane * (SRC * 64) + s * 64, 64), 64), :]
@@ -454,14 +454,18 @@
             block = pl.ds(pl.multiple_of(s * 128, 128), 128)
             xs = nn(pick, t_ref[block, :]).astype(BF16)
             cs = nn(pick, c_ref[block, :]).astype(BF16)
-            share = pick.astype(F32) * self.prob[pl.ds(pl.multiple_of(plane * (SRC * 64) + s * 64, 64), 64), :]
-            share = jnp.sum(share, axis=1, keepdims=True) * RESIDUAL_SCALE
+            wide = pick.astype(F32)
+            eight = pl.ds(pl.multiple_of(plane * (SRC * TOP) + s * TOP, TOP), TOP)
+            share = []
+            for k, own in enumerate(owned_experts()):
+                prob = jnp.sum(jnp.where(self.ids[eight, :] == own, self.shares[eight, :], 0.0), axis=0, keepdims=True)
+                share.append(jnp.sum(wide[k * CAP:k * CAP + CAP] * prob, axis=1, keepdims=True) * RESIDUAL_SCALE)
             here = pl.ds(pl.multiple_of(s * CAP, CAP), CAP)
             to = pl.ds(pl.multiple_of(step * M + s * CAP, CAP), CAP)
             for k in range(2):
                 self.x[k, to, :] = xs[k * CAP:k * CAP + CAP]
                 self.c[k, to, :] = cs[k * CAP:k * CAP + CAP]
-                self.rw[k, here, :] = jnp.broadcast_to(share[k * CAP:k * CAP + CAP], (CAP, 128))
+                self.rw[k, here, :] = jnp.broadcast_to(share[k], (CAP, 128))
         for s in range(SRC):
             one(s)
 
@@ -1008,7 +1012,12 @@
     def router():
         m = r.middle[...]
         probs = gate_probs(r)
-        gates = gates_ref[...]
+        r.gates[...] = jnp.zeros_like(r.gates)
+        for g in range(8):
+            for j in range(4):
+                r.gates[g * 5 + j : g * 5 + j + 1, :] = gates_ref[g * 4 + j, 0:1, :]
+            r.gates[g * 5 + 4 : g * 5 + 5, :] = sum(gates_ref[g * 4 + j, 1:2, :] for j in range(4))
+        gates = r.gates[...]
         gl = probs * (gates - jnp.sum(probs * gates, axis=0, keepdims=True))
         gl = jnp.concatenate([gl, jnp.zeros((64, TOK), F32)], axis=0).T
         r.gl[...] = gl
@@ -1154,6 +1163,25 @@
     )
 
 
+def owned_experts():
+    me = lax.axis_index("fsdp")
+    return (me // 4) * 5 + lax.rem(me, 4), (me // 4) * 5 + 4
+
+
+def make_picks(ids, named, picks):
+    for s in range(DEVICES):
+        block = ids[s * TOP : s * TOP + TOP, :]
+        for k, e in enumerate(owned_experts()):
+            named[s * 2 + k : s * 2 + k + 1, :] = jnp.max(jnp.where(block == e, 1.0, 0.0), axis=0, keepdims=True)
+    row = lax.broadcasted_iota(jnp.int32, (TOK, TOK), 0)
+    before = jnp.where(row < lax.broadcasted_iota(jnp.int32, (TOK, TOK), 1), 1.0, 0.0).astype(BF16)
+    ranks = nn(named[...].astype(BF16), before)
+    ranks = jnp.where(named[...] > 0.0, ranks, -1.0)
+    slot = lax.broadcasted_iota(jnp.int32, (CAP, TOK), 0).astype(F32)
+    for i in range(DEVICES * 2):
+        picks[i * CAP : i * CAP + CAP, :] = jnp.where(ranks[i : i + 1, :] == slot, 1.0, 0.0).astype(BF16)
+
+
 def route_weights(ids, r, rw):
     probs = gate_probs(r)
     row = lax.broadcasted_iota(jnp.int32, probs.shape, 0)
@@ -1162,10 +1190,11 @@
 
 
 def first_kernel(*refs):
-    (x, cos, sin, bias, ids), dense, (cot,), experts_in, dense_out, outs, results, weights, (rw, load_sem), refs = cut_up(
-        refs, 5, 4, 1, 2, 4, 5, 9, 3, 2
-    )
-    cots, tokens, shares, wf, wo = outs
+    (x, cos, sin, bias, ids), dense, (cot,), experts_in, dense_out, outs, results, weights, work, refs = cut_up(
+        refs, 5, 4, 1, 2, 4, 6, 9, 4, 7
+    )
+    cots, tokens, shares, wf, wo, picks = outs
+    natural, turned, (rw, named, load_sem) = work[:2], work[2:4], work[4:]
     sems1, sems2, sems3, direct_sems, _ = cut_up(refs, 12, 12, 12, 3)
     greet_all()
     p = Place()
@@ -1175,8 +1204,20 @@
     g1 = Gather(p, FIRST_PARTS, dense, dense_out, sems1)
     g2 = Gather(p, ROW_HALVES, [cot], [cots], sems2)
     g3 = Gather(p, TOKEN_PARTS, [r.n2, rw], [tokens, shares], sems3)
-    direct = Direct(weights_out, tuple(experts_in) + (wf, wo), direct_sems)
+    direct = Direct(weights_out, tuple(turned) + (wf, wo), direct_sems)
     g1.step()
+    loads = [pltpu.make_async_copy(a, b, load_sem.at[i]) for i, (a, b) in enumerate(zip(experts_in, natural))]
+    for l in loads:
+        l.start()
+    for l, a, b in zip(loads, natural, turned):
+        l.wait()
+
+        def turn(i, carry):
+            c = lanes(i * 128)
+            b[:, :, c] = jnp.swapaxes(a[:, :, c].astype(F32), 0, 1).astype(BF16)
+            return carry
+
+        lax.fori_loop(0, a.shape[2] // 128, turn, 0)
     direct.own()
     for n in FIRST_BATCHES:
         g1.step()
@@ -1184,18 +1225,19 @@
     g2.step(2)
     direct.start(DEVICES)
     g1.arrived()
-    loads = [pltpu.make_async_copy(a, b, load_sem.at[i]) for i, (a, b) in enumerate(zip(dense_out[:3], weights))]
+    loads = [pltpu.make_async_copy(a, b, load_sem.at[i]) for i, (a, b) in enumerate(zip(dense_out, weights))]
     for l in loads:
         l.start()
     g2.step(2)
     for l in loads:
         l.wait()
-    for i, chunk in enumerate(attention_forward(x, cos, sin, bias, *weights, r)):
+    for i, chunk in enumerate(attention_forward(x, cos, sin, bias, *weights[:3], r)):
         chunk()
         if i % 2 == 1:
             g2.step()
     route_weights(ids, r, rw)
     g3.step(2)
+    make_picks(weights[3], named, picks)
     g2.arrived()
     g3.arrived()
     for g in (g1, g2, g3):
@@ -1212,10 +1254,12 @@
     return pl.pallas_call(
         first_kernel,
         in_specs=[VMEM] * 5 + [HBM] * 7,
-        out_specs=[HBM] * 9 + [VMEM] * 9,
-        out_shape=dense_full + [wide(cot), wide(cot), like(DEVICES * TOP, TOK, dtype=F32), like(D, 2 * F), like(D, OWN_WIDTH)] + [like(*s, dtype=t) for s, t in ATT_SHAPES],
-        scratch_shapes=[pltpu.VMEM(a.shape, a.dtype) for a in dense_full[:3]]
-        + [pltpu.VMEM((TOP, TOK), F32), DMA((3,))]
+        out_specs=[HBM] * 9 + [VMEM] * 10,
+        out_shape=dense_full + [wide(cot), wide(cot), like(DEVICES * TOP, TOK, dtype=F32), like(D, 2 * F), like(D, OWN_WIDTH), like(DEVICES * 64, TOK)] + [like(*s, dtype=t) for s, t in ATT_SHAPES],
+        scratch_shapes=[pltpu.VMEM(a.shape, a.dtype) for a in dense_full]
+        + [pltpu.VMEM(a.shape, a.dtype) for a in (gu, dp)]
+        + [pltpu.VMEM((a.shape[1], a.shape[0], a.shape[2]), a.dtype) for a in (gu, dp)]
+        + [pltpu.VMEM((TOP, TOK), F32), pltpu.VMEM((DEVICES * 2, TOK), F32), DMA((4,))]
         + Gather.scratch(4, FIRST_PARTS)
         + Gather.scratch(1, ROW_HALVES)
         + Gather.scratch(2, TOKEN_PARTS)
@@ -1225,7 +1269,7 @@
 
 
 def middle_kernel(*refs):
-    (picks, probs), (tokens, cots, wf_in, wo_in), (gin,), outs, blocks, work, refs = cut_up(refs, 2, 4, 1, 5, 9, 10)
+    (picks, ids, shares), (tokens, cots, wf_in, wo_in), (gin,), outs, blocks, work, refs = cut_up(refs, 3, 4, 1, 5, 9, 10)
     out_part, dwf, dwo, all_gates, grad_down = outs
     t, c, out_block, gin_block, wf, wo, gates, whole, own = blocks
     (weight_sem, load_sem, out_sem, grad_sem), spaces, sems, direct_sems, _ = cut_up(refs, 4, 5, 9, 3)
@@ -1233,7 +1277,7 @@
     p = Place()
     s = Scatter(p, ROW_HALVES, [gin_block], [gin], spaces, sems, by_plane=True)
     direct = Direct(down_back, (dwo, gates, grad_down, all_gates), direct_sems)
-    e = Experts(work, wf, wo, picks, probs, gates)
+    e = Experts(work, wf, wo, picks, ids, shares, gates)
     R = SRC * TOK
 
     def plane_rows(q):
@@ -1297,12 +1341,12 @@
     direct.finish()
 
 
-def middle(picks, probs, tokens, cots, wf, wo):
+def middle(picks, ids, shares, tokens, cots, wf, wo):
     R = SRC * TOK
     spaces, sems = Scatter.scratch([tokens], ROW_HALVES)
     return pl.pallas_call(
         middle_kernel,
-        in_specs=[VMEM] * 2 + [HBM] * 4,
+        in_specs=[VMEM] * 3 + [HBM] * 4,
         out_specs=[VMEM] + [HBM] * 5,
         out_shape=[like(TOK, D, dtype=F32), like(DEVICES * TOK, D), like(D, 2 * F), like(D, OWN_WIDTH), like(DEVICES, 8, TOK, dtype=F32), like(E, D // DEVICES, F)],
         scratch_shapes=[pltpu.VMEM((R, D), BF16)] * 4
@@ -1314,7 +1358,7 @@
         + [DMA((2,)), DMA((2,)), DMA, DMA((2, 2))]
         + spaces + sems + Direct.scratch(3),
         compiler_params=pltpu.CompilerParams(collective_id=1, has_side_effects=True, vmem_limit_bytes=63 * 2**20),
-    )(picks, probs, tokens, cots, wf, wo)
+    )(picks, ids, shares, tokens, cots, wf, wo)
 
 
 WORK = (
@@ -1326,6 +1370,7 @@
     ("gjf", (TOK, Q_WIDTH + 2 * K_WIDTH), F32),
     ("gj", (TOK, Q_WIDTH + 2 * K_WIDTH), BF16),
     ("gn", (TOK, D), F32),
+    ("gates", (64, TOK), F32),
 )
 
 
@@ -1333,7 +1378,7 @@
     (x, cot, gin, gates, cos, sin), results, (qkv_full, out_full, out_part, dwf, dwo), outs, work, weights, (small_src, load_sem), refs = cut_up(
         refs, 6, 9, 5, 6, len(WORK), 2, 2
     )
-    input_grad, combined, qkv_grad, out_grad, small_grad, grad_gu = outs
+    input_grad, layer_output, qkv_grad, out_grad, small_grad, grad_gu = outs
     spaces1, sems1, spaces2, sems2, direct_sems, _ = cut_up(refs, 5, 9, 12, 9, 3)
     greet_all()
     p = Place()
@@ -1341,8 +1386,9 @@
     for name, ref in zip(ATT_NAMES + tuple(w[0] for w in WORK), tuple(results) + tuple(work)):
         setattr(r, name, ref)
     r.input_grad = input_grad
+    r.combined = r.gn
     qkv_ref, out_ref = weights
-    s1 = Scatter(p, ROW_HALVES, [out_part], [combined], spaces1, sems1)
+    s1 = Scatter(p, ROW_HALVES, [out_part], [r.combined], spaces1, sems1)
     s2 = Scatter(p, DENSE_PARTS, [qkv_ref, out_ref, small_src], [qkv_grad, out_grad, small_grad], spaces2, sems2, in_place=True)
     direct = Direct(gate_up_back, (dwf, dwo, grad_gu), direct_sems)
     s1.begin_all()
@@ -1371,9 +1417,10 @@
             direct.start(2)
     s2.begin_all()
     s1.step(12)
-    while s2.left:
-        s2.step()
-        direct.start(2)
+    s2.step(3)
+    direct.start(DEVICES)
+    layer_output[...] = (r.middle[...] + r.combined[...]).astype(BF16)
+    s2.step(12)
     direct.start(DEVICES)
     s1.finish()
     s2.finish()
@@ -1390,7 +1437,7 @@
         in_specs=[VMEM] * 15 + [HBM] * 5,
         out_specs=[VMEM] * 5 + [HBM],
         out_shape=[
-            like(TOK, D), like(TOK, D, dtype=F32), like(own, qkv_full.shape[1], dtype=F32), like(own, D, dtype=F32),
+            like(TOK, D), like(TOK, D), like(own, qkv_full.shape[1], dtype=F32), like(own, D, dtype=F32),
             like(own, TOK, dtype=F32), like(E, own, 2 * F),
         ],
         scratch_shapes=[pltpu.VMEM(s, t) for _, s, t in WORK]
@@ -1401,11 +1448,26 @@
     )(x, cot, gin, gates, cos, sin, *results, qkv_full, out_full, out_part, dwf, dwo)
 
 
+def turn_kernel(x_ref, o_ref):
+    o_ref[...] = jnp.swapaxes(x_ref[...].astype(F32), 0, 1)
+
+
+def turned_back(x):
+    e, rows, w = x.shape
+    return pl.pallas_call(
+        turn_kernel,
+        grid=(w // 256,),
+        in_specs=[pl.BlockSpec((e, rows, 256), lambda i: (0, 0, i))],
+        out_specs=pl.BlockSpec((rows, e, 256), lambda i: (0, 0, i)),
+        out_shape=like(rows, e, w, dtype=F32),
+        compiler_params=pltpu.CompilerParams(vmem_limit_bytes=48 * 2**20),
+    )(x)
+
+
 def fast(
     layer_input, cotangent, sequence_ids, expert_ids, attention_gain, qkv_weight, output_weight, moe_gain, router, gate_up, down_proj
 ):
-    n, own_rows, T = DEVICES, gate_up.shape[0], layer_input.shape[0]
-    me = lax.axis_index("fsdp")
+    own_rows, T = gate_up.shape[0], layer_input.shape[0]
     small = jnp.concatenate(
         [router, attention_gain[:, None], moe_gain[:, None], jnp.zeros((own_rows, 86), BF16)], axis=1
     )
@@ -1417,29 +1479,16 @@
     bias = jnp.where(allowed, 0.0, -jnp.inf).astype(F32)
 
     ids_t = expert_ids.T
-    qkv_full, out_full, small_full, ids_all, cots, tokens, shares, wf, wo, *results = first(
+    qkv_full, out_full, small_full, ids_all, cots, tokens, shares, wf, wo, picks, *results = first(
         layer_input, cos, sin, bias, ids_t, [qkv_weight, output_weight, small, ids_t], cotangent,
-        jnp.transpose(gate_up, (1, 0, 2)), jnp.transpose(down_proj, (1, 0, 2)),
-    )
-
-    owned = jnp.stack([(me // 4) * 5 + lax.rem(me, 4), (me // 4) * 5 + 4])
-    named = ids_all.reshape(n, TOP, T)[:, :, None, :] == owned[None, None, :, None]
-    probs = jnp.sum(jnp.where(named, shares.reshape(n, TOP, 1, T), 0.0), axis=1)
-    probs = jnp.broadcast_to(probs[:, :, None, :], (n, 2, CAP, T)).reshape(n * 64, T)
-    named = jnp.any(named, axis=1)
-    before = (place_in[:, None] < place_in[None, :]).astype(BF16)
-    ranks = jnp.dot(named.astype(BF16).reshape(2 * n, T), before, preferred_element_type=F32).reshape(n, 2, 1, T)
-    picks = ((ranks == jnp.arange(CAP, dtype=F32)[:, None]) & named[:, :, None, :]).astype(BF16).reshape(n * 64, T)
-    gin, out_part, dwf, dwo, gates, grad_down = middle(picks, probs, tokens, cots, wf, wo)
-    gates = gates.reshape(8, 4, 8, T)
-    gates = jnp.concatenate([gates[:, :, 0], jnp.sum(gates[:, :, 1], axis=1, keepdims=True)], axis=1).reshape(E, T)
-    gates = jnp.pad(gates, ((0, 64 - E), (0, 0)))
-    input_grad, combined, qkv_grad, out_grad, small_grad, grad_gu = last(
+        gate_up, down_proj,
+    )
+
+    gin, out_part, dwf, dwo, gates, grad_down = middle(picks, ids_all, shares, tokens, cots, wf, wo)
+    input_grad, layer_output, qkv_grad, out_grad, small_grad, grad_gu = last(
         layer_input, cotangent, gin, gates, cos, sin, results, qkv_full, out_full, out_part, dwf, dwo
     )
-    layer_output = (results[ATT_NAMES.index("middle")] + combined).astype(BF16)
-    gate_up_grad = jnp.transpose(grad_gu, (1, 0, 2)).astype(F32)
-    down_grad = jnp.transpose(grad_down, (1, 0, 2)).astype(F32)
+    gate_up_grad, down_grad = turned_back(grad_gu), turned_back(grad_down)
     return (
         layer_output,
         input_grad,

time: 597 us -> 578 us (0.968)
  local copies, waits for them, and re-layouts: 28.9 us -> 10.8 us
  other arithmetic: 13.7 us -> 4.18 us
  Pallas kernels: 544 us -> 553 us
    unnamed x21 -> x18, local copies, waits for them, and re-layouts: 24 us -> 7.66 us
    pallas_call x1 -> x3, Pallas kernels: 118 us -> 125 us  [the longest x1 118 us: middle(): pl.pallas_call(middle_kernel, in_specs=[VMEM] * 3 + [HBM] * 4, out_specs=...]
    convert_element_type x4 -> x0, other arithmetic: 6.13 us -> none  [the longest x1 2.08 us: fast(): down_grad = jnp.transpose(grad_down, (1, 0, 2)).astype(F32)]
where the time goes in v5:
time: 578 us; the launch traced here: 568 us
  Pallas kernels  553 us (96%)
  local copies, waits for them, and re-layouts  10.8 us (2%)
    pallas_call x1, Pallas kernels, first(): pl.pallas_call(first_kernel, in_specs=[VMEM] * 5 + [HBM] * 7, out_specs=[...  250 us
    pallas_call x1, Pallas kernels, last(): pl.pallas_call(last_kernel, in_specs=[VMEM] * 15 + [HBM] * 5, out_specs=[...  178 us
    pallas_call x1, Pallas kernels, middle(): pl.pallas_call(middle_kernel, in_specs=[VMEM] * 3 + [HBM] * 4, out_specs=...  118 us

profile of v5, /device:TPU:0, one launch (start us, length us, event | category | flops | bytes accessed | tf_op | source)
XLA Modules:
  0.0 568.5 jit_solution(4732616730453552343)
XLA Ops:
  0.6 0.9 convert_reduce_fusion
  1.6 0.1 pad.3.clone
  1.7 0.8 copy.30
  2.4 0.8 copy.31
  3.2 0.8 copy.29
  4.0 0.7 maximum_maximum_fusion.refs_7_
  4.6 1.4 fusion.refs_3_
  6.1 0.3 fusion.1
  6.4 0.8 pad_maximum_fusion
  7.2 250.4 %shard_map.178 = (bf16[1536,2560]{1,0:T(8,128)(2,1)}, bf16[1536,1536]{1,0:T(8,128)(2,1)}, bf16[1536,128]{1,0:T(8,128)(2,1)}, s32[256,128]{1,0:T(8,128)}, bf16[40...) custom-call(bf16[128,1536]{1,0:T(8,128)(2,1)} %refs_0_.3, ...), custom_call_target="tpu_custom_call" | custom-call | tf_op jit(solution)/shard_map/pallas_call | solution.py:1254
  257.7 117.5 %shard_map.179 = (f32[128,1536]{1,0:T(8,128)}, bf16[4096,1536]{1,0:T(8,128)(2,1)}, bf16[1536,1024]{1,0:T(8,128)(2,1)}, bf16[1536,896]{1,0:T(8,128)(2,1)}, f32[32...) custom-call(bf16[2048,128]{1,0:T(8,128)(2,1)} %get-tuple-element.39.refs_0_, s32[256,128]{1,0:T(8,128)} %get-tuple-element.40.refs_1_, ...), custom_call_target="tpu_custom_call" | custom-call | tf_op jit(solution)/shard_map/pallas_call | solution.py:1347
  375.2 177.5 %shard_map.180 = (bf16[128,1536]{1,0:T(8,128)(2,1)}, bf16[128,1536]{1,0:T(8,128)(2,1)}, f32[48,2560]{1,0:T(8,128)}, f32[48,1536]{1,0:T(8,128)}, f32[48,128]{1,0:T(8,128)}, /*index=5*/bf16[40,48,1024]{2,1,0:T(8,128)(2,1)}) custom-call(bf16[128,1536]{1,0:T(8,128)(2,1)} %refs_0_.3, bf16[128,1536]{1,0:T(8,128)(2,1)} %refs_1_.1, ...), custom_call_target="tpu_custom_call" | custom-call | tf_op jit(solution)/shard_map/pallas_call | solution.py:1435
  552.8 1.5 slice_reduce_fusion
  554.3 1.4 copy.32
  555.7 0.0 copy-start.1
  555.7 1.5 copy-done.1
  557.3 0.0 copy-start
  557.3 2.6 shard_map.182
  559.9 0.9 copy-done
  560.8 0.0 copy-start.4
  560.8 0.0 copy-start.3
  560.8 0.0 copy-start.2
  560.8 0.0 copy-start.5
  560.8 4.5 shard_map.181
  565.3 0.0 copy-done.4
  565.3 0.7 copy.37
  566.1 0.0 copy-done.3
  566.1 0.7 copy.38
  566.8 0.0 copy-done.2
  566.8 0.8 copy.39
  567.6 0.0 copy-done.5
  567.6 0.7 copy.40
  (3 shorter events, 0.0 us)
Async XLA Ops:
  555.7 1.5 copy-start.1
  557.3 3.5 copy-start
  560.8 4.5 copy-start.4
  560.8 5.3 copy-start.3
  560.8 6.0 %copy-start.2 = (f32[48,2560]{1,0:T(8,128)S(1)}, f32[48,2560]{1,0:T(8,128)}, u32[]{:S(2)}) copy-start(f32[48,2560]{1,0:T(8,128)} %get-tuple-element.115) | copy-start | bytes 1474564
  560.8 6.8 %copy-start.5 = (f32[48,1536]{1,0:T(8,128)S(1)}, f32[48,1536]{1,0:T(8,128)}, u32[]{:S(2)}) copy-start(f32[48,1536]{1,0:T(8,128)} %get-tuple-element.116) | copy-start | bytes 884740

commit v6 on v5

--- a/solution.py
+++ b/solution.py
@@ -1306,8 +1306,9 @@
                 l.wait()
         for wait in reads:
             wait()
-        s.step(step)
+        s.step((0, 1, 1, 2)[step])
         e.run(step)
+        s.step((0, 0, 1, 1)[step])
         if store is not None:
             store.wait()
         e.give(p.zq[q], out_block, gin_block)
@@ -1333,7 +1334,7 @@
         if n == 1:
             for wait in reads:
                 wait()
-        if n % 2 == 1:
+        if n in (1, 6, 8, 10, 11):
             s.step()
     s.step(12)
     store.wait()
@@ -1448,20 +1449,44 @@
     )(x, cot, gin, gates, cos, sin, *results, qkv_full, out_full, out_part, dwf, dwo)
 
 
-def turn_kernel(x_ref, o_ref):
-    o_ref[...] = jnp.swapaxes(x_ref[...].astype(F32), 0, 1)
-
-
-def turned_back(x):
-    e, rows, w = x.shape
+def finish_kernel(gu_ref, down_ref, small_ref, *refs):
+    whole, (gu_out, down_out, router_out, gain1_out, gain2_out), copies = refs[:4], refs[4:9], refs[9:]
+    i = pl.program_id(0)
+
+    @pl.when(i == 0)
+    def _():
+        for a, b in zip(whole, copies):
+            b[...] = a[...]
+        small = small_ref[...]
+        rows = small.shape[0]
+        turned = jnp.concatenate([small, jnp.zeros((TOK - rows, TOK), F32)], axis=0).T
+        router_out[...] = turned[:E, :rows]
+        gain1_out[...] = turned[E : E + 1, :rows]
+        gain2_out[...] = turned[E + 1 : E + 2, :rows]
+
+    @pl.when(i < 4)
+    def _():
+        gu_out[...] = jnp.swapaxes(gu_ref[...].astype(F32), 0, 1)
+
+    @pl.when(i >= 4)
+    def _():
+        down_out[...] = jnp.swapaxes(down_ref[...].astype(F32), 0, 1)
+
+
+def finish(gu, down, small, arrays):
+    e, rows, _ = gu.shape
+    early = lambda i: (0, 0, jnp.minimum(i, 3))
+    late = lambda i: (0, 0, jnp.maximum(i - 4, 0))
+    once = lambda a: pl.BlockSpec(a.shape, lambda i: (0, 0), pipeline_mode=pl.Buffered(1))
+    outs = [like(E, rows, dtype=F32), like(1, rows, dtype=F32), like(1, rows, dtype=F32)] + [like(*a.shape, dtype=a.dtype) for a in arrays]
     return pl.pallas_call(
-        turn_kernel,
-        grid=(w // 256,),
-        in_specs=[pl.BlockSpec((e, rows, 256), lambda i: (0, 0, i))],
-        out_specs=pl.BlockSpec((rows, e, 256), lambda i: (0, 0, i)),
-        out_shape=like(rows, e, w, dtype=F32),
-        compiler_params=pltpu.CompilerParams(vmem_limit_bytes=48 * 2**20),
-    )(x)
+        finish_kernel,
+        grid=(6,),
+        in_specs=[pl.BlockSpec((e, rows, 256), early), pl.BlockSpec((e, rows, 256), late), once(small)] + [once(a) for a in arrays],
+        out_specs=[pl.BlockSpec((rows, e, 256), early), pl.BlockSpec((rows, e, 256), late)] + [once(o) for o in outs],
+        out_shape=[like(rows, e, gu.shape[2], dtype=F32), like(rows, e, down.shape[2], dtype=F32)] + outs,
+        compiler_params=pltpu.CompilerParams(vmem_limit_bytes=63 * 2**20),
+    )(gu, down, small, *arrays)
 
 
 def fast(
@@ -1488,15 +1513,17 @@
     input_grad, layer_output, qkv_grad, out_grad, small_grad, grad_gu = last(
         layer_input, cotangent, gin, gates, cos, sin, results, qkv_full, out_full, out_part, dwf, dwo
     )
-    gate_up_grad, down_grad = turned_back(grad_gu), turned_back(grad_down)
+    gate_up_grad, down_grad, router_grad, gain_one, gain_two, layer_output, input_grad, qkv_grad, out_grad = finish(
+        grad_gu, grad_down, small_grad, (layer_output, input_grad, qkv_grad, out_grad)
+    )
     return (
         layer_output,
         input_grad,
-        small_grad[:, E],
+        gain_one.reshape(own_rows),
         qkv_grad,
         out_grad,
-        small_grad[:, E + 1],
-        small_grad[:, :E],
+        gain_two.reshape(own_rows),
+        router_grad.T,
         gate_up_grad,
         down_grad,
     )

time: 578 us -> 570 us (0.986)
  local copies, waits for them, and re-layouts: 10.8 us -> 2.38 us
    unnamed x18 -> x1, local copies, waits for them, and re-layouts: 7.66 us -> 0.79 us
where the time goes in v6:
time: 570 us; the launch traced here: 560 us
  Pallas kernels  552 us (97%)
    pallas_call x1, Pallas kernels, first(): pl.pallas_call(first_kernel, in_specs=[VMEM] * 5 + [HBM] * 7, out_specs=[...  250 us
    pallas_call x1, Pallas kernels, last(): pl.pallas_call(last_kernel, in_specs=[VMEM] * 15 + [HBM] * 5, out_specs=[...  177 us
    pallas_call x1, Pallas kernels, middle(): pl.pallas_call(middle_kernel, in_specs=[VMEM] * 3 + [HBM] * 4, out_specs=...  114 us

profile of v6, /device:TPU:0, one launch (start us, length us, event | category | flops | bytes accessed | tf_op | source)
XLA Modules:
  0.0 559.5 jit_solution(16146101093576820485)
XLA Ops:
  0.6 0.9 convert_reduce_fusion
  1.6 0.1 pad.3.clone
  1.7 0.8 copy.25
  2.4 0.8 copy.26
  3.2 0.8 copy.24
  4.0 0.7 maximum_maximum_fusion.refs_7_
  4.6 1.4 fusion.refs_3_
  6.1 0.3 fusion.1
  6.4 0.8 pad_maximum_fusion
  7.2 250.4 %shard_map.178 = (bf16[1536,2560]{1,0:T(8,128)(2,1)}, bf16[1536,1536]{1,0:T(8,128)(2,1)}, bf16[1536,128]{1,0:T(8,128)(2,1)}, s32[256,128]{1,0:T(8,128)}, bf16[40...) custom-call(bf16[128,1536]{1,0:T(8,128)(2,1)} %refs_0_.3, ...), custom_call_target="tpu_custom_call" | custom-call | tf_op jit(solution)/shard_map/pallas_call | solution.py:1254
  257.7 114.3 %shard_map.179 = (f32[128,1536]{1,0:T(8,128)}, bf16[4096,1536]{1,0:T(8,128)(2,1)}, bf16[1536,1024]{1,0:T(8,128)(2,1)}, bf16[1536,896]{1,0:T(8,128)(2,1)}, f32[32...) custom-call(bf16[2048,128]{1,0:T(8,128)(2,1)} %get-tuple-element.48.refs_0_, s32[256,128]{1,0:T(8,128)} %get-tuple-element.49.refs_1_, ...), custom_call_target="tpu_custom_call" | custom-call | tf_op jit(solution)/shard_map/pallas_call | solution.py:1348
  372.0 176.9 %shard_map.180 = (bf16[128,1536]{1,0:T(8,128)(2,1)}, bf16[128,1536]{1,0:T(8,128)(2,1)}, f32[48,2560]{1,0:T(8,128)}, f32[48,1536]{1,0:T(8,128)}, f32[48,128]{1,0:T(8,128)}, /*index=5*/bf16[40,48,1024]{2,1,0:T(8,128)(2,1)}) custom-call(bf16[128,1536]{1,0:T(8,128)(2,1)} %refs_0_.3, bf16[128,1536]{1,0:T(8,128)(2,1)} %refs_1_.1, ...), custom_call_target="tpu_custom_call" | custom-call | tf_op jit(solution)/shard_map/pallas_call | solution.py:1436
  548.9 10.4 %shard_map.181 = (f32[48,40,1024]{2,1,0:T(8,128)}, f32[48,40,512]{2,1,0:T(8,128)}, f32[40,48]{1,0:T(8,128)}, f32[1,48]{1,0:T(1,128)}, f32[1,48]{1,0:T(1,128)}, /...) custom-call(bf16[40,48,1024]{2,1,0:T(8,128)(2,1)} %get-tuple-element.71.gu_ref, ...), custom_call_target="tpu_custom_call" | custom-call | tf_op jit(solution)/shard_map/pallas_call | solution.py:1482
  (3 shorter events, 0.0 us)

commit v7 on v6

--- a/solution.py
+++ b/solution.py
@@ -1163,6 +1163,21 @@
     )
 
 
+def tables(seq, cos, sin, bias):
+    rows = jnp.broadcast_to(seq[...], (TOK, TOK))
+    same = rows == rows.T
+    t = lax.broadcasted_iota(jnp.int32, (TOK, TOK), 0)
+    s = lax.broadcasted_iota(jnp.int32, (TOK, TOK), 1)
+    places = jnp.sum(jnp.where(same, jnp.where(s < t, 1.0, 0.0), 0.0), axis=1, keepdims=True)
+    bias[...] = jnp.where(same, jnp.where(s <= t, 0.0, -jnp.inf), -jnp.inf)
+    half = HEAD_WIDTH // 2
+    exponents = (s % half).astype(F32) * (2.0 / HEAD_WIDTH)
+    angles = places * jnp.exp(exponents * -math.log(ROPE_BASE))
+    cos[...] = jnp.cos(angles)
+    sine = jnp.sin(angles)
+    sin[...] = jnp.where(s % HEAD_WIDTH < half, -sine, sine)
+
+
 def owned_experts():
     me = lax.axis_index("fsdp")
     return (me // 4) * 5 + lax.rem(me, 4), (me // 4) * 5 + 4
@@ -1190,11 +1205,12 @@
 
 
 def first_kernel(*refs):
-    (x, cos, sin, bias, ids), dense, (cot,), experts_in, dense_out, outs, results, weights, work, refs = cut_up(
-        refs, 5, 4, 1, 2, 4, 6, 9, 4, 7
+    (x, seq, ids), dense, (cot,), experts_in, dense_out, outs, results, weights, work, refs = cut_up(
+        refs, 3, 4, 1, 2, 4, 6, 11, 4, 8
     )
     cots, tokens, shares, wf, wo, picks = outs
-    natural, turned, (rw, named, load_sem) = work[:2], work[2:4], work[4:]
+    natural, turned, (rw, named, bias, load_sem) = work[:2], work[2:4], work[4:]
+    cos, sin = results[9:]
     sems1, sems2, sems3, direct_sems, _ = cut_up(refs, 12, 12, 12, 3)
     greet_all()
     p = Place()
@@ -1219,6 +1235,7 @@
 
         lax.fori_loop(0, a.shape[2] // 128, turn, 0)
     direct.own()
+    tables(seq, cos, sin, bias)
     for n in FIRST_BATCHES:
         g1.step()
         direct.start(n)
@@ -1248,24 +1265,24 @@
 FIRST_BATCHES = (1, 1, 1, 1, 1, 1, 1, 1, 1, 1)
 
 
-def first(x, cos, sin, bias, ids, dense, cot, gu, dp):
+def first(x, seq, ids, dense, cot, gu, dp):
     wide = lambda a: like(DEVICES * a.shape[0], a.shape[1], dtype=a.dtype)
     dense_full = [wide(a) for a in dense]
     return pl.pallas_call(
         first_kernel,
-        in_specs=[VMEM] * 5 + [HBM] * 7,
-        out_specs=[HBM] * 9 + [VMEM] * 10,
-        out_shape=dense_full + [wide(cot), wide(cot), like(DEVICES * TOP, TOK, dtype=F32), like(D, 2 * F), like(D, OWN_WIDTH), like(DEVICES * 64, TOK)] + [like(*s, dtype=t) for s, t in ATT_SHAPES],
+        in_specs=[VMEM] * 3 + [HBM] * 7,
+        out_specs=[HBM] * 9 + [VMEM] * 12,
+        out_shape=dense_full + [wide(cot), wide(cot), like(DEVICES * TOP, TOK, dtype=F32), like(D, 2 * F), like(D, OWN_WIDTH), like(DEVICES * 64, TOK)] + [like(*s, dtype=t) for s, t in ATT_SHAPES] + [like(TOK, TOK, dtype=F32)] * 2,
         scratch_shapes=[pltpu.VMEM(a.shape, a.dtype) for a in dense_full]
         + [pltpu.VMEM(a.shape, a.dtype) for a in (gu, dp)]
         + [pltpu.VMEM((a.shape[1], a.shape[0], a.shape[2]), a.dtype) for a in (gu, dp)]
-        + [pltpu.VMEM((TOP, TOK), F32), pltpu.VMEM((DEVICES * 2, TOK), F32), DMA((4,))]
+        + [pltpu.VMEM((TOP, TOK), F32), pltpu.VMEM((DEVICES * 2, TOK), F32), pltpu.VMEM((TOK, TOK), F32), DMA((4,))]
         + Gather.scratch(4, FIRST_PARTS)
         + Gather.scratch(1, ROW_HALVES)
         + Gather.scratch(2, TOKEN_PARTS)
         + Direct.scratch(5),
         compiler_params=pltpu.CompilerParams(collective_id=0, has_side_effects=True, vmem_limit_bytes=60 * 2**20),
-    )(x, cos, sin, bias, ids, *dense, cot, gu, dp)
+    )(x, seq, ids, *dense, cot, gu, dp)
 
 
 def middle_kernel(*refs):
@@ -1496,16 +1513,9 @@
     small = jnp.concatenate(
         [router, attention_gain[:, None], moe_gain[:, None], jnp.zeros((own_rows, 86), BF16)], axis=1
     )
-    cosine, sine = rope_tables(positions(sequence_ids), HEAD_WIDTH)
-    cos = jnp.concatenate([cosine] * 4, axis=1)
-    sin = jnp.concatenate([-sine, sine] * 2, axis=1)
-    place_in = jnp.arange(T, dtype=jnp.int32)
-    allowed = (sequence_ids[:, None] == sequence_ids[None, :]) & (place_in[None, :] <= place_in[:, None])
-    bias = jnp.where(allowed, 0.0, -jnp.inf).astype(F32)
-
     ids_t = expert_ids.T
-    qkv_full, out_full, small_full, ids_all, cots, tokens, shares, wf, wo, picks, *results = first(
-        layer_input, cos, sin, bias, ids_t, [qkv_weight, output_weight, small, ids_t], cotangent,
+    qkv_full, out_full, small_full, ids_all, cots, tokens, shares, wf, wo, picks, *results, cos, sin = first(
+        layer_input, sequence_ids.astype(F32).reshape(1, T), ids_t, [qkv_weight, output_weight, small, ids_t], cotangent,
         gate_up, down_proj,
     )
 

time: 570 us -> 567 us (level)
  no operation moved by 1% of the time
where the time goes in v7:
time: 567 us; the launch traced here: 558 us
  Pallas kernels  552 us (97%)
    pallas_call x1, Pallas kernels, first(): pl.pallas_call(first_kernel, in_specs=[VMEM] * 3 + [HBM] * 7, out_specs=[...  250 us
    pallas_call x1, Pallas kernels, last(): pl.pallas_call(last_kernel, in_specs=[VMEM] * 15 + [HBM] * 5, out_specs=[...  177 us
    pallas_call x1, Pallas kernels, middle(): pl.pallas_call(middle_kernel, in_specs=[VMEM] * 3 + [HBM] * 4, out_specs=...  114 us

profile of v7, /device:TPU:0, one launch (start us, length us, event | category | flops | bytes accessed | tf_op | source)
XLA Modules:
  0.0 557.6 jit_solution(862414712267010389)
XLA Ops:
  0.6 1.2 convert_bitcast_fusion.refs_1_
  1.8 0.1 pad.3.clone
  1.9 0.8 copy.21
  2.6 0.8 copy.22
  3.4 0.8 copy.20
  4.2 0.7 maximum_maximum_fusion.refs_5_
  4.9 250.4 %shard_map.178 = (bf16[1536,2560]{1,0:T(8,128)(2,1)}, bf16[1536,1536]{1,0:T(8,128)(2,1)}, bf16[1536,128]{1,0:T(8,128)(2,1)}, s32[256,128]{1,0:T(8,128)}, bf16[40...) custom-call(bf16[128,1536]{1,0:T(8,128)(2,1)} %refs_0_.3, ...), custom_call_target="tpu_custom_call" | custom-call | tf_op jit(solution)/shard_map/pallas_call | solution.py:1271
  255.3 114.2 %shard_map.179 = (f32[128,1536]{1,0:T(8,128)}, bf16[4096,1536]{1,0:T(8,128)(2,1)}, bf16[1536,1024]{1,0:T(8,128)(2,1)}, bf16[1536,896]{1,0:T(8,128)(2,1)}, f32[32...) custom-call(bf16[2048,128]{1,0:T(8,128)(2,1)} %get-tuple-element.50.refs_0_, s32[256,128]{1,0:T(8,128)} %get-tuple-element.51.refs_1_, ...), custom_call_target="tpu_custom_call" | custom-call | tf_op jit(solution)/shard_map/pallas_call | solution.py:1365
  369.5 177.2 %shard_map.180 = (bf16[128,1536]{1,0:T(8,128)(2,1)}, bf16[128,1536]{1,0:T(8,128)(2,1)}, f32[48,2560]{1,0:T(8,128)}, f32[48,1536]{1,0:T(8,128)}, f32[48,128]{1,0:T(8,128)}, /*index=5*/bf16[40,48,1024]{2,1,0:T(8,128)(2,1)}) custom-call(bf16[128,1536]{1,0:T(8,128)(2,1)} %refs_0_.3, bf16[128,1536]{1,0:T(8,128)(2,1)} %refs_1_.1, ...), custom_call_target="tpu_custom_call" | custom-call | tf_op jit(solution)/shard_map/pallas_call | solution.py:1453
  546.7 10.4 %shard_map.181 = (f32[48,40,1024]{2,1,0:T(8,128)}, f32[48,40,512]{2,1,0:T(8,128)}, f32[40,48]{1,0:T(8,128)}, f32[1,48]{1,0:T(1,128)}, f32[1,48]{1,0:T(1,128)}, /...) custom-call(bf16[40,48,1024]{2,1,0:T(8,128)(2,1)} %get-tuple-element.75.gu_ref, ...), custom_call_target="tpu_custom_call" | custom-call | tf_op jit(solution)/shard_map/pallas_call | solution.py:1499
  (1 shorter events, 0.0 us)
